TPU v7x, 256 devices: a whole 4x4x8 slice. The times are simulated.
256 devices in a mesh: row: 32 (over y, z), col: 8 (over x, core).
Axes of the slice: x: 4, y: 4, z: 8, core: 2. Of those that a mesh axis runs over, the one named last changes fastest.
Arguments:
- inputs: bfloat16 [768, 8192], P('row', 'col'), may hold values from -6 to 6
- cotangent: bfloat16 [768, 8192], P('row', 'col'), may hold values from -1.5 to 1.5
- up_weight: bfloat16 [8192, 28672], P('col', 'row'), may hold values from -0.125 to 0.125
- down_weight: bfloat16 [28672, 8192], P('row', 'col'), may hold values from -0.0625 to 0.0625
- up_mask: int32 [128, 448], replicated, may hold values from 0 to 1, as said below
- down_mask: int32 [448, 128], replicated, may hold values from 0 to 1, as said below
Outputs:
- output: float32 [768, 8192], P('row', 'col')
- grad_input: float32 [768, 8192], P('row', 'col')
- grad_up: float32 [8192, 28672], P('col', 'row')
- grad_down: float32 [28672, 8192], P('row', 'col')
Inputs may be any that keep to these rules, and one draw needn't show every extreme that they name: `up_mask`: 1 keeps the 64 x 64 tile of the up projection, 0 removes it. In each block of 16 consecutive tile rows (aligned) and each aligned run of 14 tile columns, exactly 7 of those columns hold a kept tile. `down_mask`: 1 keeps the 64 x 64 tile of the down projection, 0 removes it. In each block of 16 consecutive tile columns (aligned) and each aligned run of 14 tile rows, exactly 7 of those rows hold a kept tile.
All inputs are finite; a program needn't handle non-finite values.
Results may differ from a plain program's by a relative error of at most 0.0029.
Values may be sent and summed in bfloat16 or wider, within the bound.
No kernel may reach another device: no remote copies, remote signals or barrier semaphores. Data moves between devices by JAX's collectives and lax.ppermute only.
A program may use at most 128 MiB of HBM per device.

v0:
```python
import jax
import jax.numpy as jnp
from jax import lax
from jax.sharding import PartitionSpec as P

inv_root_two = 0.7071067811865476
inv_root_tau = 0.3989422804014327
last_last = (((1,), (1,)), ((), ()))
first_first = (((0,), (0,)), ((), ()))


def tile_mask(weight, tile_keep):
    blocks = weight.reshape(tile_keep.shape[0], 64, tile_keep.shape[1], 64)
    kept = blocks * tile_keep[:, None, :, None].astype(weight.dtype)
    return kept.reshape(weight.shape)


def gelu_value(hidden):
    return 0.5 * hidden * (1.0 + jax.scipy.special.erf(hidden * inv_root_two))


def gelu_slope(hidden):
    return 0.5 * (
        1.0 + jax.scipy.special.erf(hidden * inv_root_two)
    ) + hidden * inv_root_tau * jnp.exp(-0.5 * hidden * hidden)


def on_device(inputs, cotangent, up_weight, down_weight, up_mask, down_mask):
    tile_rows = up_weight.shape[0] // 64
    hid_tiles = up_weight.shape[1] // 64
    row_at = lax.axis_index("row")
    col_at = lax.axis_index("col")
    up_local = lax.dynamic_slice(
        up_mask, (col_at * tile_rows, row_at * hid_tiles), (tile_rows, hid_tiles)
    )
    down_local = lax.dynamic_slice(
        down_mask, (row_at * hid_tiles, col_at * tile_rows), (hid_tiles, tile_rows)
    )
    w_up = tile_mask(up_weight, up_local)
    w_down = tile_mask(down_weight, down_local)
    all_inputs, all_cotangent = (
        lax.all_gather(inputs, "row", axis=0, tiled=True),
        lax.all_gather(cotangent, "row", axis=0, tiled=True),
    )
    picked = all_inputs
    pre_share = lax.psum_scatter(
        jnp.dot(picked, w_up, preferred_element_type=jnp.float32),
        "col",
        scatter_dimension=0,
        tiled=True,
    )
    activation = lax.all_gather(
        gelu_value(pre_share).astype(jnp.bfloat16), "col", axis=0, tiled=True
    )
    picked = activation
    output = lax.psum_scatter(
        jnp.dot(picked, w_down, preferred_element_type=jnp.float32),
        "row",
        scatter_dimension=0,
        tiled=True,
    )
    grad_down = lax.dot_general(
        activation, all_cotangent, first_first, preferred_element_type=jnp.float32
    )
    grad_down = tile_mask(grad_down, down_local)
    picked = all_cotangent
    grad_share = lax.psum_scatter(
        lax.dot_general(picked, w_down, last_last, preferred_element_type=jnp.float32),
        "col",
        scatter_dimension=0,
        tiled=True,
    )
    grad_pre = lax.all_gather(
        (grad_share * gelu_slope(pre_share)).astype(jnp.bfloat16), "col", axis=0, tiled=True
    )
    grad_up = lax.dot_general(all_inputs, grad_pre, first_first, preferred_element_type=jnp.float32)
    grad_up = tile_mask(grad_up, up_local)
    picked = grad_pre
    grad_input = lax.psum_scatter(
        lax.dot_general(picked, w_up, last_last, preferred_element_type=jnp.float32),
        "row",
        scatter_dimension=0,
        tiled=True,
    )
    return (output, grad_input, grad_up, grad_down)


def solution(mesh):
    in_specs = (P("row", "col"), P("row", "col"), P("col", "row"), P("row", "col"), P(), P())
    out_specs = (P("row", "col"), P("row", "col"), P("col", "row"), P("row", "col"))
    return jax.shard_map(
        on_device, mesh=mesh, in_specs=in_specs, out_specs=out_specs, check_vma=False
    )
```

profile of v0, /device:TPU:8, one launch (start us, length us, event | category | flops | bytes accessed | tf_op | source)
XLA Modules:
  0.0 755.1 jit_solution(6129511550605888493)
XLA Ops:
  9.5 2.4 mul.94
  11.9 6.0 mul.95
  17.9 71.7 %all-gather.9.cloned.1.call-done = bf16[768,1024]{1,0:T(8,128)(2,1)} async-done(((bf16[24,1024]{1,0:T(8,128)(2,1)}), bf16[768,1024]{1,0:T(8,128)(2,1)}) %all-gather.9.cloned.1.call-update) | async-done | bytes 1572880 | tf_op jit(solution)/shard_map/all_gather | solution.py:43
  89.5 4.1 convolution_bitcast_fusion
  95.9 2.9 copy.18
  102.0 6.0 mul.89
  108.0 3.5 mul.90
  111.5 55.3 %all-gather.5.cloned.1.call-done = bf16[768,1024]{1,0:T(8,128)(2,1)} async-done(((bf16[24,1024]{1,0:T(8,128)(2,1)}), bf16[768,1024]{1,0:T(8,128)(2,1)}) %all-gather.5.cloned.1.call-update) | async-done | bytes 1572880 | tf_op jit(solution)/shard_map/all_gather | solution.py:42
  166.8 3.6 convolution_bitcast_fusion.1
  172.6 33.4 %reduce-scatter.15.cloned.1.call-done = f32[96,896]{1,0:T(8,128)} async-done(((f32[768,896]{1,0:T(8,128)}), f32[96,896]{1,0:T(8,128)}) %reduce-scatter.15.cloned.1.call-update) | async-done | bytes 344080 | tf_op jit(solution)/shard_map/reduce_scatter | solution.py:67
  206.0 39.5 %reduce-scatter.13.cloned.1.call-done = f32[96,896]{1,0:T(8,128)} async-done(((f32[768,896]{1,0:T(8,128)}), f32[96,896]{1,0:T(8,128)}) %reduce-scatter.13.cloned.1.call-update) | async-done | bytes 344080 | tf_op jit(solution)/shard_map/reduce_scatter | solution.py:46
  248.1 25.3 %all-gather.7.cloned.1.call-done = bf16[768,896]{1,0:T(8,128)(2,1)} async-done(((bf16[96,896]{1,0:T(8,128)(2,1)}), bf16[768,896]{1,0:T(8,128)(2,1)}) %all-gather.7.cloned.1.call-update) | async-done | bytes 1376272 | tf_op jit(solution)/shard_map/all_gather | solution.py:52
  273.4 5.5 fusion.1
  279.2 23.4 %all-gather.11.cloned.1.call-done = bf16[768,896]{1,0:T(8,128)(2,1)} async-done(((bf16[96,896]{1,0:T(8,128)(2,1)}), bf16[768,896]{1,0:T(8,128)(2,1)}) %all-gather.11.cloned.1.call-update) | async-done | bytes 1376272 | tf_op jit(solution)/shard_map/all_gather | solution.py:73
  302.5 4.7 fusion.8
  307.3 3.5 mul.108
  310.8 7.3 mul.109
  318.1 3.5 mul.105
  321.6 7.4 mul.106
  329.1 5.5 bitcast_multiply_fusion
  334.6 5.2 copy.25
  339.7 5.5 convolution_multiply_fusion
  345.2 180.4 %reduce-scatter.9.cloned.1.call-done = f32[24,1024]{1,0:T(8,128)} async-done(((f32[768,1024]{1,0:T(8,128)}), f32[24,1024]{1,0:T(8,128)}) %reduce-scatter.9.cloned.1.call-update) | async-done | bytes 98320 | tf_op jit(solution)/shard_map/reduce_scatter | solution.py:56
  525.6 222.6 %reduce-scatter.11.cloned.1.call-done = f32[24,1024]{1,0:T(8,128)} async-done(((f32[768,1024]{1,0:T(8,128)}), f32[24,1024]{1,0:T(8,128)}) %reduce-scatter.11.cloned.1.call-update) | async-done | bytes 98320 | tf_op jit(solution)/shard_map/reduce_scatter | solution.py:79
  (34 shorter events, 12.8 us)
Async XLA Ops:
  7.2 82.4 %all-gather.9.cloned.1.call-start = ((), (), s32[]{:S(2)}) async-start(), calls=%async_computation.7 | async-start | bytes 1622016 | tf_op jit(solution)/shard_map/all_gather | solution.py:43
  7.9 158.9 %all-gather.5.cloned.1.call-start = ((), (), s32[]{:S(2)}) async-start(), calls=%async_computation.4 | async-start | bytes 1622016 | tf_op jit(solution)/shard_map/all_gather | solution.py:42
  8.6 197.4 %reduce-scatter.15.cloned.1.call-start = ((), (), s32[]{:S(2)}) async-start(), calls=%async_computation.11 | async-start | bytes 3096576 | tf_op jit(solution)/shard_map/reduce_scatter | solution.py:67
  95.9 149.6 %reduce-scatter.13.cloned.1.call-start = ((), (), s32[]{:S(2)}) async-start(), calls=%async_computation.10 | async-start | bytes 3096576 | tf_op jit(solution)/shard_map/reduce_scatter | solution.py:46
  172.6 100.9 %copy-start = (bf16[896,1024]{1,0:T(8,128)(2,1)S(1)}, bf16[896,1024]{1,0:T(8,128)(2,1)}, u32[]{:S(2)}) copy-start(bf16[896,1024]{1,0:T(8,128)(2,1)} %mul.95) | copy-start | bytes 5505028
  172.6 100.9 %all-gather.7.cloned.1.call-start = ((), (), s32[]{:S(2)}) async-start(), calls=%async_computation.5 | async-start | bytes 1548288 | tf_op jit(solution)/shard_map/all_gather | solution.py:52
  247.5 55.0 %all-gather.11.cloned.1.call-start = ((), (), s32[]{:S(2)}) async-start(), calls=%async_computation.8 | async-start | bytes 1548288 | tf_op jit(solution)/shard_map/all_gather | solution.py:73
  248.1 277.5 %reduce-scatter.9.cloned.1.call-start = ((), (), s32[]{:S(2)}) async-start(), calls=%async_computation.6 | async-start | bytes 3244032 | tf_op jit(solution)/shard_map/reduce_scatter | solution.py:56
  278.9 23.6 %copy-start.1 = (bf16[1024,896]{0,1:T(8,128)(2,1)S(1)}, bf16[1024,896]{0,1:T(8,128)(2,1)}, u32[]{:S(2)}) copy-start(bf16[1024,896]{0,1:T(8,128)(2,1)} %mul.90) | copy-start | bytes 5505028
  278.9 469.3 %reduce-scatter.11.cloned.1.call-start = ((), (), s32[]{:S(2)}) async-start(), calls=%async_computation.9 | async-start | bytes 3244032 | tf_op jit(solution)/shard_map/reduce_scatter | solution.py:79
  321.6 7.4 copy-start.3
  321.6 7.4 copy-start.5
  334.6 5.2 copy-start.2
  334.6 5.2 copy-start.4
Sparse Core Ops, SparseCore 0:
  10.6 78.9 all-gather.8
  92.1 74.6 all-gather.4
  169.9 36.0 reduce-scatter.14
  209.2 36.2 reduce-scatter.12
  247.8 25.6 all-gather.6
  275.7 26.7 all-gather.10
  307.0 218.5 reduce-scatter.8
  530.5 217.6 reduce-scatter.10
where the time goes:
time: 757 us; the launch traced here: 755 us
  waiting for transfers between devices  653 us (86%)
  local copies, waits for them, and re-layouts  50.9 us (7%)
  matrix products  28.9 us (4%)
  between operations  14.2 us (2%)
    reduce_scatter x1, waiting for transfers between devices, on_device(): lax.psum_scatter(lax.dot_general(picked, w_up, last_last, preferred_eleme...  223 us
    reduce_scatter x1, waiting for transfers between devices, on_device(): lax.psum_scatter(jnp.dot(picked, w_down, preferred_element_type=jnp.float...  180 us
    all_gather x1, waiting for transfers between devices, on_device(): lax.all_gather(cotangent, 'row', axis=0, tiled=True)  71.7 us
    all_gather x1, waiting for transfers between devices, on_device(): lax.all_gather(inputs, 'row', axis=0, tiled=True)  55.3 us
    reduce_scatter x1, waiting for transfers between devices, on_device(): lax.psum_scatter(jnp.dot(picked, w_up, preferred_element_type=jnp.float32...  39.5 us
    mul x8, local copies, waits for them, and re-layouts, tile_mask(): kept = blocks * tile_keep[:, None, :, None].astype(weight.dtype)  38.4 us
    reduce_scatter x1, waiting for transfers between devices, on_device(): lax.psum_scatter(lax.dot_general(picked, w_down, last_last, preferred_ele...  33.4 us
    all_gather x1, waiting for transfers between devices, on_device(): lax.all_gather(gelu_value(pre_share).astype(jnp.bfloat16), 'col', axis=0,...  25.3 us
  transfers between devices with their start and end apart: 8, of which 8 were waited for; matrix products, arithmetic and copies ran while one was open for 11% of the time, Pallas kernels for 0%

commit v1 on v0

v1 whole, which is shorter than its diff:
```python
import jax
import jax.numpy as jnp
from jax import lax
from jax.experimental import pallas as pl
from jax.experimental.pallas import tpu as pltpu
from jax.sharding import Mesh, PartitionSpec as P

BF = jnp.bfloat16
F32 = jnp.float32
ROW = ("y", "z")
COL = ("x", "core")
T = 64
USED = 7
inv_root_two = 0.7071067811865476
inv_root_tau = 0.3989422804014327
VMEM = pl.BlockSpec(memory_space=pltpu.VMEM)
SMEM = pl.BlockSpec(memory_space=pltpu.SMEM)


def params(mib):
    return pltpu.CompilerParams(vmem_limit_bytes=mib * 1024 * 1024)


def lane_half(shape):
    return lax.broadcasted_iota(jnp.int32, shape, len(shape) - 1) >= T


def prep_kernel(tu, td, mu, md, wu, wd, wuc, wdc):
    for s in range(USED):
        t = td[s]
        rows = wd[pl.ds(pl.multiple_of(t * T, T), T), :].astype(F32)
        wdc[pl.ds(s * T, T), :] = (rows * md[t]).astype(BF)
    wdc[pl.ds(USED * T, T), :] = jnp.zeros((T, wdc.shape[1]), BF)
    n_feat = wu.shape[0] // T

    def feat(i, _):
        r = pl.ds(pl.multiple_of(i * T, T), T)
        high = lane_half((T, 128))

        def tile(q):
            if q == 0:
                return jnp.zeros((T, 128), F32)
            t = tu[q - 1]
            c = pl.ds(pl.multiple_of((t // 2) * 128, 128), 128)
            blk = wu[r, c].astype(F32) * mu[i, t // 2]
            return pltpu.roll(blk, ((t + q) % 2) * T, 1)

        for p in range(4):
            both = jnp.where(high, tile(2 * p + 1), tile(2 * p))
            wuc[r, pl.ds(p * 128, 128)] = both.astype(BF)
        return 0

    lax.fori_loop(0, n_feat, feat, 0)


def first_kernel(x, c, wuc, wdc, out):
    g = lax.dot_general(c[...], wdc[...], (((1,), (1,)), ((), ())), preferred_element_type=F32)
    p = jnp.dot(x[...], wuc[...], preferred_element_type=F32)
    out[:, 0:384] = g[:, 0:384]
    out[:, 384:512] = g[:, 384:512] + p[:, 0:128]
    out[:, 512:896] = p[:, 128:512]


def middle_kernel(tu, td, recv, out, acc):
    n_dev, rows, _ = recv.shape
    acc[...] = jnp.zeros_like(acc)
    high = lane_half((rows, 128)).astype(jnp.int32)

    def tile_of(k, q):
        return td[k, q] if q < USED else tu[k, q - USED]

    def add(k, _):
        for q in range(2 * USED):
            t = tile_of(k, q)
            blk = recv[k, :, pl.ds((q // 2) * 128, 128)]
            moved = pltpu.roll(blk, ((t + q) % 2) * T, 1)
            at = t // 2 + (0 if q < USED else USED)
            acc[at] += jnp.where(high == t % 2, moved, 0.0)
        return 0

    lax.fori_loop(0, n_dev, add, 0)
    for b in range(USED):
        v = acc[USED + b]
        g = acc[b]
        cdf = 0.5 * (1.0 + lax.erf(v * inv_root_two))
        acc[b] = (v * cdf).astype(BF).astype(F32)
        slope = cdf + v * inv_root_tau * jnp.exp(-0.5 * v * v)
        acc[USED + b] = (g * slope).astype(BF).astype(F32)

    def pick(k, _):
        def tile(q):
            t = tile_of(k, q)
            blk = acc[t // 2 + (0 if q < USED else USED)]
            return pltpu.roll(blk, ((t + q) % 2) * T, 1)

        for p in range(USED):
            both = jnp.where(high == 1, tile(2 * p + 1), tile(2 * p))
            out[k, :, pl.ds(p * 128, 128)] = both.astype(BF)
        return 0

    lax.fori_loop(0, n_dev, pick, 0)


def last_kernel(h, wuc, wdc, out):
    n = wdc.shape[1]
    out[:, 0:n] = jnp.dot(h[:, 0:512], wdc[...], preferred_element_type=F32).astype(BF)
    out[:, n : 2 * n] = lax.dot_general(
        h[:, 384:896], wuc[...], (((1,), (1,)), ((), ())), preferred_element_type=F32
    ).astype(BF)


def grad_down_kernel(td, md, h, c, out, s):
    s[...] = lax.dot_general(h[:, 0:512], c[...], (((0,), (0,)), ((), ())), preferred_element_type=F32)
    out[...] = jnp.zeros_like(out)
    for q in range(USED):
        t = td[q]
        out[pl.ds(pl.multiple_of(t * T, T), T), :] = s[pl.ds(q * T, T), :] * md[t]


def grad_up_kernel(su, mu, h, x, out, s):
    n = out.shape[0]
    full = lax.dot_general(x[...], h[:, 384:896], (((0,), (0,)), ((), ())), preferred_element_type=F32)
    for b in range(4):
        s[b] = full[:, b * 128 : (b + 1) * 128]

    def feat(i, _):
        r = pl.ds(pl.multiple_of(i * T, T), T)
        high = lane_half((T, 128))
        for b in range(USED):
            def tile(half):
                q = su[2 * b + half] + 1
                return pltpu.roll(s[q // 2, r, :], ((q + half) % 2) * T, 1)

            c = pl.ds(b * 128, 128)
            keep = mu[i, b]
            both = jnp.where(high, tile(1), tile(0))
            out[r, c] = jnp.where(keep > 0, both, 0.0)
        return 0

    lax.fori_loop(0, n // T, feat, 0)


def shift(a, axis, by):
    n = lax.axis_size(axis)
    return lax.ppermute(a, axis, [(i, (i + by) % n) for i in range(n)])


def put(whole, part, at, axis):
    starts = [0] * whole.ndim
    starts[axis] = at
    return lax.dynamic_update_slice(whole, jnp.expand_dims(part, axis), starts)


def gather_ring(a, axis):
    n = lax.axis_size(axis)
    got = [(0, a, None)]
    fwd = back = a
    for s in range(1, n // 2):
        fwd, back = shift(fwd, axis, 1), shift(back, axis, -1)
        got += [(-s, fwd, None), (s, back, None)]
    half = a.shape[-1] // 2
    lo = shift(fwd[..., :half], axis, 1)
    hi = shift(back[..., half:], axis, -1)
    got += [(n // 2, jnp.concatenate([lo, hi], axis=-1), None)]
    return got


def gather_into(a, axis, dim):
    n = lax.axis_size(axis)
    me = lax.axis_index(axis)
    shape = list(a.shape)
    shape.insert(dim, n)
    whole = jnp.zeros(shape, a.dtype)
    for off, part, _ in gather_ring(a, axis):
        whole = put(whole, part, (me + off + n) % n, dim)
    return whole


def on_device(inputs, cotangent, up_weight, down_weight, up_mask, down_mask):
    tokens, feat = inputs.shape
    hid = up_weight.shape[1]
    ft, ht = feat // T, hid // T
    ny, nz, nc = lax.axis_size("y"), lax.axis_size("z"), lax.axis_size("x") * lax.axis_size("core")
    rows = ny * nz * tokens
    chunk = rows // nc
    row_at = lax.axis_index(ROW)
    col_at = lax.axis_index(COL)

    all_in = gather_into(gather_into(inputs, "y", 0), "z", 1)
    all_cot = gather_into(gather_into(cotangent, "z", 0), "y", 0)
    all_in = all_in.reshape(rows, feat)
    all_cot = all_cot.reshape(rows, feat)

    up_row = lax.dynamic_slice(up_mask, (0, row_at * ht), (nc * ft, ht))
    down_row = lax.dynamic_slice(down_mask, (row_at * ht, 0), (ht, nc * ft))
    used_up = up_row.reshape(nc, ft, ht).max(axis=1)
    used_down = down_row.reshape(ht, nc, ft).max(axis=2).T
    which = jnp.arange(ht, dtype=jnp.int32)

    def tiles_of(used):
        slot = jnp.cumsum(used, axis=1) - 1
        hit = (slot[:, None, :] == jnp.arange(USED, dtype=jnp.int32)[None, :, None]) & (used[:, None, :] > 0)
        return jnp.where(hit, which, 0).sum(axis=2).astype(jnp.int32), slot

    tu, slot_up = tiles_of(used_up)
    td, _ = tiles_of(used_down)
    tu_own = lax.dynamic_slice(tu, (col_at, 0), (1, USED))[0]
    td_own = lax.dynamic_slice(td, (col_at, 0), (1, USED))[0]
    su_own = jnp.clip(lax.dynamic_slice(slot_up, (col_at, 0), (1, ht))[0], 0, USED - 1)
    mu = jnp.repeat(lax.dynamic_slice(up_row, (col_at * ft, 0), (ft, ht)).astype(F32), T, axis=1).reshape(ft, hid // 128, 1, 128)
    md = jnp.repeat(lax.dynamic_slice(down_row, (0, col_at * ft), (ht, ft)).astype(F32), T, axis=1).reshape(ht, 1, feat)

    wuc, wdc = pl.pallas_call(
        prep_kernel,
        out_shape=[jax.ShapeDtypeStruct((feat, 512), BF), jax.ShapeDtypeStruct((512, feat), BF)],
        in_specs=[SMEM, SMEM, VMEM, VMEM, VMEM, VMEM],
        out_specs=[VMEM, VMEM],
        compiler_params=params(24),
        name="prep",
    )(tu_own, td_own, mu, md, up_weight, down_weight)

    step = rows // 4
    whole = lambda shape: pl.BlockSpec(shape, lambda i: (0, 0))
    shares = pl.pallas_call(
        first_kernel,
        out_shape=jax.ShapeDtypeStruct((rows, hid), F32),
        grid=(4,),
        in_specs=[
            pl.BlockSpec((step, feat), lambda i: (i, 0)),
            pl.BlockSpec((step, feat), lambda i: (i, 0)),
            whole((feat, 512)),
            whole((512, feat)),
        ],
        out_specs=pl.BlockSpec((step, hid), lambda i: (i, 0)),
        compiler_params=params(32),
        name="first",
    )(all_in, all_cot, wuc, wdc)
    recv = lax.all_to_all(shares.reshape(nc, chunk, hid), COL, 0, 0)
    send = pl.pallas_call(
        middle_kernel,
        out_shape=jax.ShapeDtypeStruct((nc, chunk, hid), BF),
        in_specs=[SMEM, SMEM, VMEM],
        out_specs=VMEM,
        scratch_shapes=[pltpu.VMEM((2 * USED, chunk, 128), F32)],
        compiler_params=params(32),
        name="middle",
    )(tu, td, recv)
    hidden = lax.all_to_all(send, COL, 0, 0).reshape(rows, hid)
    part = pl.pallas_call(
        last_kernel,
        out_shape=jax.ShapeDtypeStruct((rows, 2 * feat), BF),
        grid=(4,),
        in_specs=[pl.BlockSpec((step, hid), lambda i: (i, 0)), whole((feat, 512)), whole((512, feat))],
        out_specs=pl.BlockSpec((step, 2 * feat), lambda i: (i, 0)),
        compiler_params=params(32),
        name="last",
    )(hidden, wuc, wdc)
    part = lax.all_to_all(part.reshape(ny, nz * tokens, 2 * feat), "y", 0, 0)
    part = part.astype(F32).sum(axis=0).astype(BF)
    part = lax.all_to_all(part.reshape(nz, tokens, 2 * feat), "z", 0, 0)
    both = part.astype(F32).sum(axis=0)
    grad_down = pl.pallas_call(
        grad_down_kernel,
        out_shape=jax.ShapeDtypeStruct((hid, feat), F32),
        in_specs=[SMEM, VMEM, VMEM, VMEM],
        out_specs=VMEM,
        scratch_shapes=[pltpu.VMEM((512, feat), F32)],
        compiler_params=params(32),
        name="grad_down",
    )(td_own, md, hidden, all_cot)
    grad_up = pl.pallas_call(
        grad_up_kernel,
        out_shape=jax.ShapeDtypeStruct((feat, hid), F32),
        in_specs=[SMEM, VMEM, VMEM, VMEM],
        out_specs=VMEM,
        scratch_shapes=[pltpu.VMEM((4, feat, 128), F32)],
        compiler_params=params(32),
        name="grad_up",
    )(su_own, mu, hidden, all_in)
    return both[:, :feat], both[:, feat:], grad_up, grad_down


def solution(mesh):
    torus = Mesh(mesh.devices.reshape(4, 8, 4, 2), ROW + COL)
    block = P(ROW, COL)
    return jax.shard_map(
        on_device,
        mesh=torus,
        in_specs=(block, block, P(COL, ROW), block, P(), P()),
        out_specs=(block, block, P(COL, ROW), block),
        check_vma=False,
    )
```

time: 757 us -> 218 us (0.29)
  waiting for transfers between devices: 653 us -> 62.8 us
  blocking collectives: 0 us -> 64.5 us
  starting transfers between devices: 0.5 us -> 46 us
  local copies, waits for them, and re-layouts: 50.9 us -> 10.3 us
  matrix products: 28.9 us -> 0 us
  Pallas kernels: 0 us -> 24.3 us
  between operations: 14.2 us -> 1.2 us
    reduce_scatter x4 -> x0, waiting for transfers between devices: 476 us -> none  [the longest x1 223 us: on_device(): lax.psum_scatter(lax.dot_general(picked, w_up, last_last, preferred_eleme...]
    all_gather x4 -> x0, waiting for transfers between devices: 176 us -> none  [the longest x1 71.7 us: on_device(): lax.all_gather(cotangent, 'row', axis=0, tiled=True)]
    all_to_all x0 -> x2, blocking collectives: none -> 64.5 us  [the longest x1 42.3 us: on_device(): part = lax.all_to_all(part.reshape(ny, nz * tokens, 2 * feat), 'y', 0, 0)]
    all_to_all x0 -> x2, waiting for transfers between devices: none -> 44.7 us  [the longest x1 34.1 us: on_device(): recv = lax.all_to_all(shares.reshape(nc, chunk, hid), COL, 0, 0)]
    mul x8 -> x0, local copies, waits for them, and re-layouts: 38.4 us -> none  [tile_mask(): kept = blocks * tile_keep[:, None, :, None].astype(weight.dtype)]
    ppermute x0 -> x24, starting transfers between devices: none -> 37.4 us  [shift(): return lax.ppermute(a, axis, [(i, (i + by) % n) for i in range(n)])]
    dot_general x6 -> x0, matrix products: 28.9 us -> none  [the longest x1 5.51 us: on_device(): lax.dot_general(activation, all_cotangent, first_first, preferred_element...]
    pallas_call x0 -> x6, Pallas kernels: none -> 24.3 us  [the longest x1 6.43 us: on_device(): pl.pallas_call(grad_up_kernel, out_shape=jax.ShapeDtypeStruct((feat, hid)...]
  transfers between devices with their start and end apart: 8 -> 26, of which waited for: 8 -> 11; matrix products, arithmetic and copies ran while one was open for 11% -> 4% of each run, Pallas kernels for 0% -> 6%
where the time goes in v1:
time: 218 us; the launch traced here: 217 us
  blocking collectives  64.5 us (30%)
  waiting for transfers between devices  62.8 us (29%)
  starting transfers between devices  46 us (21%)
  Pallas kernels  24.3 us (11%)
  local copies, waits for them, and re-layouts  10.3 us (5%)
  other arithmetic  7.92 us (4%)
    all_to_all x1, blocking collectives, on_device(): part = lax.all_to_all(part.reshape(ny, nz * tokens, 2 * feat), 'y', 0, 0)  42.3 us
    ppermute x24, starting transfers between devices, shift(): return lax.ppermute(a, axis, [(i, (i + by) % n) for i in range(n)])  37.4 us
    all_to_all x1, waiting for transfers between devices, on_device(): recv = lax.all_to_all(shares.reshape(nc, chunk, hid), COL, 0, 0)  34.1 us
    all_to_all x1, blocking collectives, on_device(): hidden = lax.all_to_all(send, COL, 0, 0).reshape(rows, hid)  22.2 us
    ppermute x24, waiting for transfers between devices, shift(): return lax.ppermute(a, axis, [(i, (i + by) % n) for i in range(n)])  18.1 us
    all_to_all x1, waiting for transfers between devices, on_device(): part = lax.all_to_all(part.reshape(nz, tokens, 2 * feat), 'z', 0, 0)  10.6 us
    pallas_call x1, Pallas kernels, on_device(): pl.pallas_call(grad_up_kernel, out_shape=jax.ShapeDtypeStruct((feat, hid)...  6.43 us
    pallas_call x1, Pallas kernels, on_device(): pl.pallas_call(middle_kernel, out_shape=jax.ShapeDtypeStruct((nc, chunk,...  5.56 us
  transfers between devices with their start and end apart: 26, of which 11 were waited for; matrix products, arithmetic and copies ran while one was open for 4% of the time, Pallas kernels for 6%

profile of v1, /device:TPU:8, one launch (start us, length us, event | category | flops | bytes accessed | tf_op | source)
XLA Modules:
  0.0 217.1 jit_solution(6448891130485248102)
XLA Ops:
  2.9 5.7 %collective-permute-start.13 = (bf16[24,1024]{1,0:T(8,128)(2,1)}, bf16[24,1024]{1,0:T(8,128)(2,1)S(1)}, u32[]{:S(2)}, u32[]{:S(2)}) collective-permute-start(bf16[24,1024]{1,0:T(8,128)(2,1)} %param.7), channel_id=1, source_target_pairs={{0,56},{8,0},{16,8},{24,16},{32,24},{40,32},{48,40},{56,48},{1,57}... | collective-permute-start | bytes 147464 | tf_op jit(solution)/shard_map/ppermute | solution.py:145
  17.5 2.8 %prep.1 = (bf16[1024,512]{1,0:T(8,128)(2,1)S(1)}, bf16[512,1024]{1,0:T(8,128)(2,1)S(1)}) custom-call(s32[7]{0:T(128)S(1)} %fusion.6.tu, s32[7]{0:T(128)S(1)} %fusion.7.td, f32[16,7,1,128]{3,2,1,0:T(1,128)S(1)} %reshape_reshape.8.mu, f32[14,1,1024]{2,1,0:T(1,128)S(1)} %reshape_reshape.7.md, bf16[1024,896]{1,0:T(8,128)(2,1)S(1)} %copy-done.7, ...), custom_call_target="tpu_custom_call" | custom-call | tf_op jit(solution)/shard_map/prep/pallas_call | solution.py:213
  22.5 3.2 %collective-permute-start.15 = (bf16[24,1024]{1,0:T(8,128)(2,1)S(1)}, bf16[24,1024]{1,0:T(8,128)(2,1)S(1)}, u32[]{:S(2)}, u32[]{:S(2)}) collective-permute-start(bf16[24,1024]{1,0:T(8,128)(2,1)S(1)} %collective-permute-done.13), channel_id=1, source_target_pairs={{0,56},{8,0},{16,8},{24,16},{32,24},{40,32},{48,40},{56,48},{1,57}... | collective-permute-start | bytes 147464 | tf_op jit(solution)/shard_map/ppermute | solution.py:145
  26.9 3.2 %collective-permute-start.5 = (bf16[4,24,1024]{2,1,0:T(8,128)(2,1)S(1)}, bf16[4,24,1024]{2,1,0:T(8,128)(2,1)S(1)}, u32[]{:S(2)}, u32[]{:S(2)}) collective-permute-start(bf16[4,24,1024]{2,1,0:T(8,128)(2,1)S(1)} %fusion.2), channel_id=1, source_target_pairs={{0,56},{8,0},{16,8},{24,16},{32,24},{40,32},{48,40},{56,48},{1,57}... | collective-permute-start | bytes 589832 | tf_op jit(solution)/shard_map/ppermute | solution.py:145
  30.4 3.3 %collective-permute-start.17 = (bf16[24,1024]{1,0:T(8,128)(2,1)S(1)}, bf16[24,1024]{1,0:T(8,128)(2,1)S(1)}, u32[]{:S(2)}, u32[]{:S(2)}) collective-permute-start(bf16[24,1024]{1,0:T(8,128)(2,1)S(1)} %collective-permute-done.15), channel_id=1, source_target_pairs={{0,56},{8,0},{16,8},{24,16},{32,24},{40,32},{48,40},{56,48},{1,57}... | collective-permute-start | bytes 147464 | tf_op jit(solution)/shard_map/ppermute | solution.py:145
  35.4 3.5 %collective-permute-start.19 = (bf16[24,512]{1,0:T(8,128)(2,1)S(1)}, bf16[24,512]{1,0:T(8,128)(2,1)S(1)}, u32[]{:S(2)}, u32[]{:S(2)}) collective-permute-start(bf16[24,512]{1,0:T(8,128)(2,1)S(1)} %slice.45), channel_id=1, source_target_pairs={{0,56},{8,0},{16,8},{24,16},{32,24},{40,32},{48,40},{56,48},{1,57}... | collective-permute-start | bytes 73736 | tf_op jit(solution)/shard_map/ppermute | solution.py:145
  40.5 3.7 %collective-permute-done.18 = bf16[24,512]{1,0:T(8,128)(2,1)S(1)} collective-permute-done((bf16[24,512]{1,0:T(8,128)(2,1)S(1)}, bf16[24,512]{1,0:T(8,128)(2,1)S(1)}, u32[]{:S(2)}, u32[]{:S(2)}) %collective-permute-start.18) | collective-permute-done | bytes 24608 | tf_op jit(solution)/shard_map/ppermute | solution.py:145
  44.2 3.2 %collective-permute-start.21 = (bf16[8,24,1024]{2,1,0:T(8,128)(2,1)S(1)}, bf16[8,24,1024]{2,1,0:T(8,128)(2,1)S(1)}, u32[]{:S(2)}, u32[]{:S(2)}) collective-permute-start(bf16[8,24,1024]{2,1,0:T(8,128)(2,1)S(1)} %fusion.3), channel_id=1, source_target_pairs={{0,192},{64,0},{128,64},{192,128},{1,193},{65,1},{129,65},{193,129... | collective-permute-start | bytes 1179656 | tf_op jit(solution)/shard_map/ppermute | solution.py:145
  49.8 3.6 %collective-permute-done.7 = bf16[4,24,1024]{2,1,0:T(8,128)(2,1)S(1)} collective-permute-done((bf16[4,24,1024]{2,1,0:T(8,128)(2,1)S(1)}, bf16[4,24,1024]{2,1,0:T(8,128)(2,1)S(1)}, u32[]{:S(2)}, u32[]{:S(2)}) %collective-permute-start.7) | collective-permute-done | bytes 196640 | tf_op jit(solution)/shard_map/ppermute | solution.py:145
  53.4 2.6 %collective-permute-start.9 = (bf16[4,24,1024]{2,1,0:T(8,128)(2,1)S(1)}, bf16[4,24,1024]{2,1,0:T(8,128)(2,1)S(1)}, u32[]{:S(2)}, u32[]{:S(2)}) collective-permute-start(bf16[4,24,1024]{2,1,0:T(8,128)(2,1)S(1)} %collective-permute-done.7), channel_id=1, source_target_pairs={{0,56},{8,0},{16,8},{24,16},{32,24},{40,32},{48,40},{56,48},{1,57}... | collective-permute-start | bytes 589832 | tf_op jit(solution)/shard_map/ppermute | solution.py:145
  59.2 3.8 %collective-permute-start.11 = (bf16[4,24,512]{2,1,0:T(8,128)(2,1)S(1)}, bf16[4,24,512]{2,1,0:T(8,128)(2,1)S(1)}, u32[]{:S(2)}, u32[]{:S(2)}) collective-permute-start(bf16[4,24,512]{2,1,0:T(8,128)(2,1)S(1)} %slice.43), channel_id=1, source_target_pairs={{0,56},{8,0},{16,8},{24,16},{32,24},{40,32},{48,40},{56,48},{1,57}... | collective-permute-start | bytes 294920 | tf_op jit(solution)/shard_map/ppermute | solution.py:145
  65.2 3.7 %collective-permute-done.10 = bf16[4,24,512]{2,1,0:T(8,128)(2,1)S(1)} collective-permute-done((bf16[4,24,512]{2,1,0:T(8,128)(2,1)S(1)}, bf16[4,24,512]{2,1,0:T(8,128)(2,1)S(1)}, u32[]{:S(2)}, u32[]{:S(2)}) %collective-permute-start.10) | collective-permute-done | bytes 98336 | tf_op jit(solution)/shard_map/ppermute | solution.py:145
  69.0 2.9 %first.1 = f32[768,896]{1,0:T(8,128)S(1)} custom-call(bf16[768,1024]{1,0:T(8,128)(2,1)S(1)} %bitcast.85, bf16[768,1024]{1,0:T(8,128)(2,1)S(1)} %bitcast.87, bf16[1024,512]{1,0:T(8,128)(2,1)S(1)} %get-tuple-element.6.wuc, bf16[512,1024]{1,0:T(8,128)(2,1)S(1)} %get-tuple-element.7.wdc), custom_call_target="tpu_custom_call" | custom-call | tf_op jit(solution)/shard_map/first/pallas_call | solution.py:224
  73.5 4.4 %all-to-all-start = ((f32[8,96,896]{2,1,0:T(8,128)}), f32[8,96,896]{2,1,0:T(8,128)}, u32[]{:S(2)}, u32[]{:S(2)}) async-start(f32[8,96,896]{2,1,0:T(8,128)} %bitcast.90), calls=%async_computation | async-start | bytes 5505024 | tf_op jit(solution)/shard_map/all_to_all | solution.py:238
  78.0 34.1 %all-to-all-done.recv = f32[8,96,896]{2,1,0:T(8,128)} async-done(((f32[8,96,896]{2,1,0:T(8,128)}), f32[8,96,896]{2,1,0:T(8,128)}, u32[]{:S(2)}, u32[]{:S(2)}) %all-to-all-start) | async-done | bytes 2752544 | tf_op jit(solution)/shard_map/all_to_all | solution.py:238
  112.1 5.6 %middle.1 = bf16[8,96,896]{2,1,0:T(8,128)(2,1)S(1)} custom-call(s32[8,7]{1,0:T(8,128)S(1)} %copy.100.tu, s32[8,7]{1,0:T(8,128)S(1)} %copy.101.td, f32[8,96,896]{2,1,0:T(8,128)} %all-to-all-done.recv), custom_call_target="tpu_custom_call" | custom-call | tf_op jit(solution)/shard_map/middle/pallas_call | solution.py:239
  117.7 22.2 %all_to_all.20 = bf16[8,96,896]{2,1,0:T(8,128)(2,1)S(1)} all-to-all(bf16[8,96,896]{2,1,0:T(8,128)(2,1)S(1)} %middle.1), channel_id=1, replica_groups=mesh['y'=4,'z'=8,'x'=4,'core'=2] {'x','core'}, dimensions={0} | all-to-all | bytes 2752512 | tf_op jit(solution)/shard_map/all_to_all | solution.py:248
  139.9 3.0 %last.1 = bf16[768,2048]{1,0:T(8,128)(2,1)S(1)} custom-call(bf16[768,896]{1,0:T(8,128)(2,1)S(1)} %bitcast.82, bf16[1024,512]{1,0:T(8,128)(2,1)S(1)} %copy-done.4, bf16[512,1024]{1,0:T(8,128)(2,1)S(1)} %copy-done.6), custom_call_target="tpu_custom_call" | custom-call | tf_op jit(solution)/shard_map/last/pallas_call | solution.py:249
  142.9 42.3 %all_to_all.21 = bf16[4,192,2048]{2,1,0:T(8,128)(2,1)} all-to-all(bf16[4,192,2048]{2,1,0:T(8,128)(2,1)S(1)} %bitcast.89), channel_id=1, replica_groups=mesh['y'=4,'z'=8,'x'=4,'core'=2] {'y'}, dimensions={0} | all-to-all | bytes 6291456 | tf_op jit(solution)/shard_map/all_to_all | solution.py:258
  185.2 3.6 %reduce_sum.41 = bf16[192,2048]{1,0:T(8,128)(2,1)} reduce(bf16[4,192,2048]{2,1,0:T(8,128)(2,1)} %all_to_all.21, bf16[]{:T(256)} %constant.159.clone.1), dimensions={0}, to_apply=%region_6.7 | reduce | flops 1179648 | bytes 3932162 | tf_op jit(solution)/shard_map/reduce_sum | solution.py:259
  188.8 4.2 %all-to-all-start.3 = ((bf16[8,24,2048]{2,1,0:T(8,128)(2,1)}), bf16[8,24,2048]{2,1,0:T(8,128)(2,1)}, u32[]{:S(2)}, u32[]{:S(2)}) async-start(bf16[8,24,2048]{2,1,0:T(8,128)(2,1)} %bitcast.91), calls=%async_computation.3 | async-start | bytes 1572864 | tf_op jit(solution)/shard_map/all_to_all | solution.py:260
  194.5 3.6 %grad_down.1 = f32[896,1024]{1,0:T(8,128)} custom-call(s32[7]{0:T(128)S(1)} %fusion.7.td, f32[14,1,1024]{2,1,0:T(1,128)S(1)} %reshape_reshape.7.md, bf16[768,896]{1,0:T(8,128)(2,1)S(1)} %bitcast.83, bf16[768,1024]{1,0:T(8,128)(2,1)S(1)} %bitcast.88), custom_call_target="tpu_custom_call" | custom-call | tf_op jit(solution)/shard_map/grad_down/pallas_call | solution.py:262
  198.1 6.4 %grad_up.1 = f32[1024,896]{1,0:T(8,128)} custom-call(s32[14]{0:T(128)S(1)} %fusion.9.su, f32[16,7,1,128]{3,2,1,0:T(1,128)S(1)} %reshape_reshape.8.mu, bf16[768,896]{1,0:T(8,128)(2,1)S(1)} %bitcast.84, bf16[768,1024]{1,0:T(8,128)(2,1)S(1)} %bitcast.86), custom_call_target="tpu_custom_call" | custom-call | tf_op jit(solution)/shard_map/grad_up/pallas_call | solution.py:271
  204.5 10.6 %all-to-all-done.3 = bf16[8,24,2048]{2,1,0:T(8,128)(2,1)} async-done(((bf16[8,24,2048]{2,1,0:T(8,128)(2,1)}), bf16[8,24,2048]{2,1,0:T(8,128)(2,1)}, u32[]{:S(2)}, u32[]{:S(2)}) %all-to-all-start.3) | async-done | bytes 786464 | tf_op jit(solution)/shard_map/all_to_all | solution.py:260
  (120 shorter events, 30.6 us)
Async XLA Ops:
  0.6 19.7 %collective-permute-start.1 = (bf16[24,1024]{1,0:T(8,128)(2,1)}, bf16[24,1024]{1,0:T(8,128)(2,1)S(1)}, u32[]{:S(2)}, u32[]{:S(2)}) collective-permute-start(bf16[24,1024]{1,0:T(8,128)(2,1)} %param.6), channel_id=1, source_target_pairs={{0,192},{64,0},{128,64},{192,128},{1,193},{65,1},{129,65},{193,129... | collective-permute-start | bytes 147464 | tf_op jit(solution)/shard_map/ppermute | solution.py:145
  2.9 19.0 %collective-permute-start = (bf16[24,1024]{1,0:T(8,128)(2,1)}, bf16[24,1024]{1,0:T(8,128)(2,1)S(1)}, u32[]{:S(2)}, u32[]{:S(2)}) collective-permute-start(bf16[24,1024]{1,0:T(8,128)(2,1)} %param.6), channel_id=1, source_target_pairs={{0,64},{64,128},{128,192},{192,0},{1,65},{65,129},{129,193},{193,1... | collective-permute-start | bytes 147464 | tf_op jit(solution)/shard_map/ppermute | solution.py:145
  2.9 19.6 %collective-permute-start.13 = (bf16[24,1024]{1,0:T(8,128)(2,1)}, bf16[24,1024]{1,0:T(8,128)(2,1)S(1)}, u32[]{:S(2)}, u32[]{:S(2)}) collective-permute-start(bf16[24,1024]{1,0:T(8,128)(2,1)} %param.7), channel_id=1, source_target_pairs={{0,56},{8,0},{16,8},{24,16},{32,24},{40,32},{48,40},{56,48},{1,57}... | collective-permute-start | bytes 147464 | tf_op jit(solution)/shard_map/ppermute | solution.py:145
  8.6 17.1 %collective-permute-start.12 = (bf16[24,1024]{1,0:T(8,128)(2,1)}, bf16[24,1024]{1,0:T(8,128)(2,1)S(1)}, u32[]{:S(2)}, u32[]{:S(2)}) collective-permute-start(bf16[24,1024]{1,0:T(8,128)(2,1)} %param.7), channel_id=1, source_target_pairs={{0,8},{8,16},{16,24},{24,32},{32,40},{40,48},{48,56},{56,0},{1,9},... | collective-permute-start | bytes 147464 | tf_op jit(solution)/shard_map/ppermute | solution.py:145
  20.4 5.4 %collective-permute-start.3 = (bf16[24,512]{1,0:T(8,128)(2,1)S(1)}, bf16[24,512]{1,0:T(8,128)(2,1)S(1)}, u32[]{:S(2)}, u32[]{:S(2)}) collective-permute-start(bf16[24,512]{1,0:T(8,128)(2,1)S(1)} %slice.41), channel_id=1, source_target_pairs={{0,192},{64,0},{128,64},{192,128},{1,193},{65,1},{129,65},{193,129... | collective-permute-start | bytes 73736 | tf_op jit(solution)/shard_map/ppermute | solution.py:145
  22.5 7.8 %collective-permute-start.15 = (bf16[24,1024]{1,0:T(8,128)(2,1)S(1)}, bf16[24,1024]{1,0:T(8,128)(2,1)S(1)}, u32[]{:S(2)}, u32[]{:S(2)}) collective-permute-start(bf16[24,1024]{1,0:T(8,128)(2,1)S(1)} %collective-permute-done.13), channel_id=1, source_target_pairs={{0,56},{8,0},{16,8},{24,16},{32,24},{40,32},{48,40},{56,48},{1,57}... | collective-permute-start | bytes 147464 | tf_op jit(solution)/shard_map/ppermute | solution.py:145
  25.7 8.0 %collective-permute-start.14 = (bf16[24,1024]{1,0:T(8,128)(2,1)S(1)}, bf16[24,1024]{1,0:T(8,128)(2,1)S(1)}, u32[]{:S(2)}, u32[]{:S(2)}) collective-permute-start(bf16[24,1024]{1,0:T(8,128)(2,1)S(1)} %collective-permute-done.12), channel_id=1, source_target_pairs={{0,8},{8,16},{16,24},{24,32},{32,40},{40,48},{48,56},{56,0},{1,9},... | collective-permute-start | bytes 147464 | tf_op jit(solution)/shard_map/ppermute | solution.py:145
  26.9 20.7 %collective-permute-start.5 = (bf16[4,24,1024]{2,1,0:T(8,128)(2,1)S(1)}, bf16[4,24,1024]{2,1,0:T(8,128)(2,1)S(1)}, u32[]{:S(2)}, u32[]{:S(2)}) collective-permute-start(bf16[4,24,1024]{2,1,0:T(8,128)(2,1)S(1)} %fusion.2), channel_id=1, source_target_pairs={{0,56},{8,0},{16,8},{24,16},{32,24},{40,32},{48,40},{56,48},{1,57}... | collective-permute-start | bytes 589832 | tf_op jit(solution)/shard_map/ppermute | solution.py:145
  30.1 17.7 %collective-permute-start.4 = (bf16[4,24,1024]{2,1,0:T(8,128)(2,1)S(1)}, bf16[4,24,1024]{2,1,0:T(8,128)(2,1)S(1)}, u32[]{:S(2)}, u32[]{:S(2)}) collective-permute-start(bf16[4,24,1024]{2,1,0:T(8,128)(2,1)S(1)} %fusion.2), channel_id=1, source_target_pairs={{0,8},{8,16},{16,24},{24,32},{32,40},{40,48},{48,56},{56,0},{1,9},... | collective-permute-start | bytes 589832 | tf_op jit(solution)/shard_map/ppermute | solution.py:145
  30.4 5.1 %collective-permute-start.17 = (bf16[24,1024]{1,0:T(8,128)(2,1)S(1)}, bf16[24,1024]{1,0:T(8,128)(2,1)S(1)}, u32[]{:S(2)}, u32[]{:S(2)}) collective-permute-start(bf16[24,1024]{1,0:T(8,128)(2,1)S(1)} %collective-permute-done.15), channel_id=1, source_target_pairs={{0,56},{8,0},{16,8},{24,16},{32,24},{40,32},{48,40},{56,48},{1,57}... | collective-permute-start | bytes 147464 | tf_op jit(solution)/shard_map/ppermute | solution.py:145
  33.7 5.5 %collective-permute-start.16 = (bf16[24,1024]{1,0:T(8,128)(2,1)S(1)}, bf16[24,1024]{1,0:T(8,128)(2,1)S(1)}, u32[]{:S(2)}, u32[]{:S(2)}) collective-permute-start(bf16[24,1024]{1,0:T(8,128)(2,1)S(1)} %collective-permute-done.14), channel_id=1, source_target_pairs={{0,8},{8,16},{16,24},{24,32},{32,40},{40,48},{48,56},{56,0},{1,9},... | collective-permute-start | bytes 147464 | tf_op jit(solution)/shard_map/ppermute | solution.py:145
  35.4 5.1 %collective-permute-start.19 = (bf16[24,512]{1,0:T(8,128)(2,1)S(1)}, bf16[24,512]{1,0:T(8,128)(2,1)S(1)}, u32[]{:S(2)}, u32[]{:S(2)}) collective-permute-start(bf16[24,512]{1,0:T(8,128)(2,1)S(1)} %slice.45), channel_id=1, source_target_pairs={{0,56},{8,0},{16,8},{24,16},{32,24},{40,32},{48,40},{56,48},{1,57}... | collective-permute-start | bytes 73736 | tf_op jit(solution)/shard_map/ppermute | solution.py:145
  44.2 11.8 %collective-permute-start.21 = (bf16[8,24,1024]{2,1,0:T(8,128)(2,1)S(1)}, bf16[8,24,1024]{2,1,0:T(8,128)(2,1)S(1)}, u32[]{:S(2)}, u32[]{:S(2)}) collective-permute-start(bf16[8,24,1024]{2,1,0:T(8,128)(2,1)S(1)} %fusion.3), channel_id=1, source_target_pairs={{0,192},{64,0},{128,64},{192,128},{1,193},{65,1},{129,65},{193,129... | collective-permute-start | bytes 1179656 | tf_op jit(solution)/shard_map/ppermute | solution.py:145
  47.4 10.9 %collective-permute-start.20 = (bf16[8,24,1024]{2,1,0:T(8,128)(2,1)S(1)}, bf16[8,24,1024]{2,1,0:T(8,128)(2,1)S(1)}, u32[]{:S(2)}, u32[]{:S(2)}) collective-permute-start(bf16[8,24,1024]{2,1,0:T(8,128)(2,1)S(1)} %fusion.3), channel_id=1, source_target_pairs={{0,64},{64,128},{128,192},{192,0},{1,65},{65,129},{129,193},{193,1... | collective-permute-start | bytes 1179656 | tf_op jit(solution)/shard_map/ppermute | solution.py:145
  47.7 5.7 %collective-permute-start.7 = (bf16[4,24,1024]{2,1,0:T(8,128)(2,1)S(1)}, bf16[4,24,1024]{2,1,0:T(8,128)(2,1)S(1)}, u32[]{:S(2)}, u32[]{:S(2)}) collective-permute-start(bf16[4,24,1024]{2,1,0:T(8,128)(2,1)S(1)} %collective-permute-done.5), channel_id=1, source_target_pairs={{0,56},{8,0},{16,8},{24,16},{32,24},{40,32},{48,40},{56,48},{1,57}... | collective-permute-start | bytes 589832 | tf_op jit(solution)/shard_map/ppermute | solution.py:145
  47.8 8.2 %collective-permute-start.6 = (bf16[4,24,1024]{2,1,0:T(8,128)(2,1)S(1)}, bf16[4,24,1024]{2,1,0:T(8,128)(2,1)S(1)}, u32[]{:S(2)}, u32[]{:S(2)}) collective-permute-start(bf16[4,24,1024]{2,1,0:T(8,128)(2,1)S(1)} %collective-permute-done.4), channel_id=1, source_target_pairs={{0,8},{8,16},{16,24},{24,32},{32,40},{40,48},{48,56},{56,0},{1,9},... | collective-permute-start | bytes 589832 | tf_op jit(solution)/shard_map/ppermute | solution.py:145
  53.4 5.8 %collective-permute-start.9 = (bf16[4,24,1024]{2,1,0:T(8,128)(2,1)S(1)}, bf16[4,24,1024]{2,1,0:T(8,128)(2,1)S(1)}, u32[]{:S(2)}, u32[]{:S(2)}) collective-permute-start(bf16[4,24,1024]{2,1,0:T(8,128)(2,1)S(1)} %collective-permute-done.7), channel_id=1, source_target_pairs={{0,56},{8,0},{16,8},{24,16},{32,24},{40,32},{48,40},{56,48},{1,57}... | collective-permute-start | bytes 589832 | tf_op jit(solution)/shard_map/ppermute | solution.py:145
  56.0 7.0 %collective-permute-start.8 = (bf16[4,24,1024]{2,1,0:T(8,128)(2,1)S(1)}, bf16[4,24,1024]{2,1,0:T(8,128)(2,1)S(1)}, u32[]{:S(2)}, u32[]{:S(2)}) collective-permute-start(bf16[4,24,1024]{2,1,0:T(8,128)(2,1)S(1)} %collective-permute-done.6), channel_id=1, source_target_pairs={{0,8},{8,16},{16,24},{24,32},{32,40},{40,48},{48,56},{56,0},{1,9},... | collective-permute-start | bytes 589832 | tf_op jit(solution)/shard_map/ppermute | solution.py:145
  56.1 12.8 %collective-permute-start.23 = (bf16[8,24,512]{2,1,0:T(8,128)(2,1)S(1)}, bf16[8,24,512]{2,1,0:T(8,128)(2,1)S(1)}, u32[]{:S(2)}, u32[]{:S(2)}) collective-permute-start(bf16[8,24,512]{2,1,0:T(8,128)(2,1)S(1)} %slice.47), channel_id=1, source_target_pairs={{0,192},{64,0},{128,64},{192,128},{1,193},{65,1},{129,65},{193,129... | collective-permute-start | bytes 589832 | tf_op jit(solution)/shard_map/ppermute | solution.py:145
  58.3 10.6 %collective-permute-start.22 = (bf16[8,24,512]{2,1,0:T(8,128)(2,1)S(1)}, bf16[8,24,512]{2,1,0:T(8,128)(2,1)S(1)}, u32[]{:S(2)}, u32[]{:S(2)}) collective-permute-start(bf16[8,24,512]{2,1,0:T(8,128)(2,1)S(1)} %slice.46), channel_id=1, source_target_pairs={{0,64},{64,128},{128,192},{192,0},{1,65},{65,129},{129,193},{193,1... | collective-permute-start | bytes 589832 | tf_op jit(solution)/shard_map/ppermute | solution.py:145
  59.2 6.0 %collective-permute-start.11 = (bf16[4,24,512]{2,1,0:T(8,128)(2,1)S(1)}, bf16[4,24,512]{2,1,0:T(8,128)(2,1)S(1)}, u32[]{:S(2)}, u32[]{:S(2)}) collective-permute-start(bf16[4,24,512]{2,1,0:T(8,128)(2,1)S(1)} %slice.43), channel_id=1, source_target_pairs={{0,56},{8,0},{16,8},{24,16},{32,24},{40,32},{48,40},{56,48},{1,57}... | collective-permute-start | bytes 294920 | tf_op jit(solution)/shard_map/ppermute | solution.py:145
  63.0 5.9 %collective-permute-start.10 = (bf16[4,24,512]{2,1,0:T(8,128)(2,1)S(1)}, bf16[4,24,512]{2,1,0:T(8,128)(2,1)S(1)}, u32[]{:S(2)}, u32[]{:S(2)}) collective-permute-start(bf16[4,24,512]{2,1,0:T(8,128)(2,1)S(1)} %slice.42), channel_id=1, source_target_pairs={{0,8},{8,16},{16,24},{24,32},{32,40},{40,48},{48,56},{56,0},{1,9},... | collective-permute-start | bytes 294920 | tf_op jit(solution)/shard_map/ppermute | solution.py:145
  73.5 38.6 %all-to-all-start = ((f32[8,96,896]{2,1,0:T(8,128)}), f32[8,96,896]{2,1,0:T(8,128)}, u32[]{:S(2)}, u32[]{:S(2)}) async-start(f32[8,96,896]{2,1,0:T(8,128)} %bitcast.90), calls=%async_computation | async-start | bytes 5505024 | tf_op jit(solution)/shard_map/all_to_all | solution.py:238
  188.8 26.3 %all-to-all-start.3 = ((bf16[8,24,2048]{2,1,0:T(8,128)(2,1)}), bf16[8,24,2048]{2,1,0:T(8,128)(2,1)}, u32[]{:S(2)}, u32[]{:S(2)}) async-start(bf16[8,24,2048]{2,1,0:T(8,128)(2,1)} %bitcast.91), calls=%async_computation.3 | async-start | bytes 1572864 | tf_op jit(solution)/shard_map/all_to_all | solution.py:260
  (11 other events, 174.6 us)

commit v2 on v1

v2 whole, which is shorter than its diff:
```python
import functools

import jax
import jax.numpy as jnp
from jax import lax
from jax.experimental import pallas as pl
from jax.experimental.pallas import tpu as pltpu
from jax.sharding import Mesh, PartitionSpec as P

BF = jnp.bfloat16
F32 = jnp.float32
ROW = ("y", "z")
COL = ("x", "core")
T = 64
USED = 7
inv_root_two = 0.7071067811865476
inv_root_tau = 0.3989422804014327
VMEM = pl.BlockSpec(memory_space=pltpu.VMEM)
SMEM = pl.BlockSpec(memory_space=pltpu.SMEM)


def params(mib):
    return pltpu.CompilerParams(vmem_limit_bytes=mib * 1024 * 1024)


def lane_half(shape):
    return lax.broadcasted_iota(jnp.int32, shape, len(shape) - 1) >= T


def prep_down_kernel(td, md, wd, wdc):
    for s in range(USED):
        t = td[s]
        for j in range(wd.shape[1] // 128):
            c = pl.ds(j * 128, 128)
            rows = wd[pl.ds(pl.multiple_of(t * T, T), T), c].astype(F32)
            keep = jnp.where(lane_half((T, 128)), md[t, 2 * j + 1], md[t, 2 * j])
            wdc[pl.ds(s * T, T), c] = jnp.where(keep > 0, rows, 0.0).astype(BF)
    wdc[pl.ds(USED * T, T), :] = jnp.zeros((T, wdc.shape[1]), BF)


def prep_up_kernel(tu, mu, wu, wuc):
    def feat(i, _):
        r = pl.ds(pl.multiple_of(i * T, T), T)
        high = lane_half((T, 128))

        def tile(q):
            if q == USED:
                return jnp.zeros((T, 128), F32)
            t = tu[q]
            c = pl.ds(pl.multiple_of((t // 2) * 128, 128), 128)
            blk = wu[r, c].astype(F32) * mu[i, t].astype(F32)
            return pltpu.roll(blk, ((t + q) % 2) * T, 1)

        for p in range(4):
            both = jnp.where(high, tile(2 * p + 1), tile(2 * p))
            wuc[r, pl.ds(p * 128, 128)] = both.astype(BF)
        return 0

    lax.fori_loop(0, wu.shape[0] // T, feat, 0)


def pack(put_rows, blocks, rows, dtype):
    for b in range(3):
        put_rows(pl.ds(b * rows, rows), blocks[b].astype(dtype))
    half = rows // 2
    last = blocks[3]
    both = jnp.where(lane_half((half, 128)), pltpu.roll(last[half:], T, 1), last[:half])
    put_rows(pl.ds(3 * rows, half), both.astype(dtype))


def unpack_last(both):
    return jnp.concatenate([both, pltpu.roll(both, T, 1)], axis=0)


def share_kernel(transposed, chunk, x, w, out):
    dims = (((1,), (1 if transposed else 0,)), ((), ()))
    full = lax.dot_general(x[...], w[...], dims, preferred_element_type=F32)
    for k in range(out.shape[0]):
        part = full[k * chunk : (k + 1) * chunk]

        def put_rows(r, v, k=k):
            out[k, r, :] = v

        pack(put_rows, [part[:, b * 128 : (b + 1) * 128] for b in range(4)], chunk, F32)


def scatter_add(tiles, recv, acc, tmp):
    n_dev, rows = recv.shape[0], acc.shape[1]
    acc[...] = jnp.zeros_like(acc)
    high = lane_half((rows, 128)).astype(jnp.int32)

    def add(k, _):
        tmp[...] = unpack_last(recv[k, pl.ds(3 * rows, rows // 2), :])
        for q in range(USED):
            t = tiles[k, q]
            blk = tmp[...] if q == 6 else recv[k, pl.ds((q // 2) * rows, rows), :]
            moved = pltpu.roll(blk, ((t + q) % 2) * T, 1)
            acc[t // 2] += jnp.where(high == t % 2, moved, 0.0)
        return 0

    lax.fori_loop(0, n_dev, add, 0)


def pick_tiles(tiles, acc, out):
    n_dev, rows = out.shape[0], acc.shape[1]
    high = lane_half((rows, 128))

    def pick(k, _):
        def tile(q):
            t = tiles[k, min(q, USED - 1)]
            return pltpu.roll(acc[t // 2], ((t + q) % 2) * T, 1)

        def put_rows(r, v):
            out[k, r, :] = v

        pack(put_rows, [jnp.where(high, tile(2 * p + 1), tile(2 * p)) for p in range(4)], rows, BF)
        return 0

    lax.fori_loop(0, n_dev, pick, 0)


def act_kernel(tu, td, recv, pre, out, acc, tmp):
    scatter_add(tu, recv, pre, tmp)
    for b in range(USED):
        v = pre[b]
        acc[b] = (0.5 * v * (1.0 + lax.erf(v * inv_root_two))).astype(BF).astype(F32)
    pick_tiles(td, acc, out)


def grad_pre_kernel(tu, td, recv, slope, out, acc, tmp):
    scatter_add(td, recv, acc, tmp)
    for b in range(USED):
        acc[b] = (acc[b] * slope[b]).astype(BF).astype(F32)
    pick_tiles(tu, acc, out)


def gelu_slope(hidden):
    return 0.5 * (1.0 + lax.erf(hidden * inv_root_two)) + hidden * inv_root_tau * jnp.exp(-0.5 * hidden * hidden)


def unpack_hidden(chunk, h, hidden):
    for k in range(h.shape[0]):
        rows = pl.ds(k * chunk, chunk)
        for b in range(3):
            hidden[rows, pl.ds(b * 128, 128)] = h[k, pl.ds(b * chunk, chunk), :]
        last = unpack_last(h[k, pl.ds(3 * chunk, chunk // 2), :].astype(F32))
        hidden[rows, pl.ds(384, 128)] = last.astype(BF)


def out_kernel(chunk, at, h, w, hidden, own, fwd, back):
    unpack_hidden(chunk, h, hidden)
    rows, n = own.shape
    ny = hidden.shape[0] // rows

    def share(j):
        start = pl.multiple_of(lax.rem(at[0] + j, ny) * rows, rows)
        return jnp.dot(hidden[pl.ds(start, rows), :], w[...], preferred_element_type=F32).astype(BF)

    fwd[:, 0:n] = share(1)
    far = share(2)
    fwd[:, n:] = far[:, 0 : n // 2]
    back[:, n:] = far[:, n // 2 :]
    back[:, 0:n] = share(3)
    own[...] = share(0)


def add_kernel(at, own, fwd, back, low, high, *outs):
    n = own.shape[2]
    for j, out in enumerate(outs):
        z = lax.rem(at[1] + j, len(outs))
        far = jnp.concatenate([low[z], high[z]], axis=-1).astype(F32)
        total = own[z].astype(F32) + fwd[z, :, 0:n].astype(F32) + back[z, :, 0:n].astype(F32) + far
        out[...] = total.astype(out.dtype)


def grad_in_kernel(chunk, h, w, hidden, out):
    unpack_hidden(chunk, h, hidden)
    out[...] = lax.dot_general(
        hidden[...], w[...], (((1,), (1,)), ((), ())), preferred_element_type=F32
    ).astype(BF)


def grad_down_kernel(td, md, h, c, out, s):
    s[...] = lax.dot_general(h[...], c[...], (((0,), (0,)), ((), ())), preferred_element_type=F32)
    out[...] = jnp.zeros_like(out)
    for q in range(USED):
        t = td[q]
        for j in range(out.shape[1] // 128):
            c = pl.ds(j * 128, 128)
            keep = jnp.where(lane_half((T, 128)), md[t, 2 * j + 1], md[t, 2 * j])
            out[pl.ds(pl.multiple_of(t * T, T), T), c] = jnp.where(keep > 0, s[pl.ds(q * T, T), c], 0.0)


def grad_up_kernel(su, mu, h, x, out, s):
    n = out.shape[0]
    full = lax.dot_general(x[...], h[...], (((0,), (0,)), ((), ())), preferred_element_type=F32)
    for b in range(4):
        s[b] = full[:, b * 128 : (b + 1) * 128]

    def feat(i, _):
        r = pl.ds(pl.multiple_of(i * T, T), T)
        high = lane_half((T, 128))
        for b in range(USED):
            def tile(half):
                q = su[2 * b + half]
                return pltpu.roll(s[q // 2, r, :], ((q + half) % 2) * T, 1)

            c = pl.ds(b * 128, 128)
            keep = jnp.where(high, mu[i, 2 * b + 1], mu[i, 2 * b])
            both = jnp.where(high, tile(1), tile(0))
            out[r, c] = jnp.where(keep > 0, both, 0.0)
        return 0

    lax.fori_loop(0, n // T, feat, 0)


def copies_of(a, axis):
    return jnp.broadcast_to(a[None], (lax.axis_size(axis),) + a.shape)


def gather(a, axis):
    return lax.all_to_all(copies_of(a, axis), axis, 0, 0)


def once_there(x, *dep):
    return lax.optimization_barrier((x, dep))[0]


def shift(a, axis, by):
    n = lax.axis_size(axis)
    return lax.ppermute(a, axis, [(i, (i + by) % n) for i in range(n)])


def ring(a, axis):
    n = lax.axis_size(axis)
    steps = [(a, a)]
    for _ in range(1, n // 2):
        steps.append((shift(steps[-1][0], axis, 1), shift(steps[-1][1], axis, -1)))
    half = a.shape[-1] // 2
    far = shift(steps[-1][0][..., :half], axis, 1), shift(steps[-1][1][..., half:], axis, -1)
    return steps[1:], far


def place_kernel(at, own, *refs):
    out = refs[-1]
    ny, nz = lax.axis_size("y"), lax.axis_size("z")
    parts = [(0, 0, own)]
    for s in range(1, nz // 2):
        parts += [(-s, 0, refs[2 * s - 2]), (s, 0, refs[2 * s - 1])]
    parts += [(nz // 2, 0, refs[nz - 2]), (nz // 2, own.shape[2] // 2, refs[nz - 1])]
    for dz, left, part in parts:
        for j in range(ny):
            slot = lax.rem(at[0] + j, ny) * nz + lax.rem(at[1] + dz + nz, nz)
            out[slot, :, left : left + part.shape[2]] = part[j]


def on_device(inputs, cotangent, up_weight, down_weight, up_mask, down_mask):
    tokens, feat = inputs.shape
    hid = up_weight.shape[1]
    ft, ht = feat // T, hid // T
    ny, nz, nc = lax.axis_size("y"), lax.axis_size("z"), lax.axis_size("x") * lax.axis_size("core")
    rows = ny * nz * tokens
    chunk = rows // nc
    row_at = lax.axis_index(ROW)
    col_at = lax.axis_index(COL)

    near, far = ring(cotangent, "y")
    own = jnp.stack([cotangent, near[0][1], jnp.concatenate(far, axis=-1), near[0][0]])
    in_copies = copies_of(gather(inputs, "z"), "y")
    all_in = lax.all_to_all(once_there(in_copies, own), "y", 0, 0).reshape(rows, feat)
    steps, far = ring(own, "z")
    at = jnp.stack([lax.axis_index("y"), lax.axis_index("z")]).astype(jnp.int32)
    pieces = [p for step in steps for p in step] + list(far)
    all_cot = pl.pallas_call(
        place_kernel,
        out_shape=jax.ShapeDtypeStruct((ny * nz, tokens, feat), BF),
        in_specs=[SMEM] + [VMEM] * (1 + len(pieces)),
        out_specs=VMEM,
        compiler_params=params(8),
        name="place",
    )(at, own, *pieces).reshape(rows, feat)

    up_row = lax.dynamic_slice(up_mask, (0, row_at * ht), (nc * ft, ht))
    down_row = lax.dynamic_slice(down_mask, (row_at * ht, 0), (ht, nc * ft))
    used_up = up_row.reshape(nc, ft, ht).max(axis=1)
    used_down = down_row.reshape(ht, nc, ft).max(axis=2).T
    which = jnp.arange(ht, dtype=jnp.int32)

    def tiles_of(used):
        slot = jnp.cumsum(used, axis=1) - 1
        hit = (slot[:, None, :] == jnp.arange(USED, dtype=jnp.int32)[None, :, None]) & (used[:, None, :] > 0)
        return jnp.where(hit, which, 0).sum(axis=2).astype(jnp.int32), slot

    tu, slot_up = tiles_of(used_up)
    td, _ = tiles_of(used_down)
    tu_own = lax.dynamic_slice(tu, (col_at, 0), (1, USED))[0]
    td_own = lax.dynamic_slice(td, (col_at, 0), (1, USED))[0]
    su_own = jnp.clip(lax.dynamic_slice(slot_up, (col_at, 0), (1, ht))[0], 0, USED - 1)
    mu = lax.dynamic_slice(up_row, (col_at * ft, 0), (ft, ht))
    md = lax.dynamic_slice(down_row, (0, col_at * ft), (ht, ft))

    wuc = pl.pallas_call(
        prep_up_kernel,
        out_shape=jax.ShapeDtypeStruct((feat, 512), BF),
        in_specs=[SMEM, SMEM, VMEM],
        out_specs=VMEM,
        compiler_params=params(16),
        name="prep_up",
    )(tu_own, mu, up_weight)
    wdc = pl.pallas_call(
        prep_down_kernel,
        out_shape=jax.ShapeDtypeStruct((512, feat), BF),
        in_specs=[SMEM, SMEM, VMEM],
        out_specs=VMEM,
        compiler_params=params(16),
        name="prep_down",
    )(td_own, md, once_there(down_weight, all_in))

    packed = chunk * 7 // 2
    blocks = (USED, chunk, 128)
    whole = lambda *shape: pl.BlockSpec(shape, lambda i: (0,) * len(shape))

    def share(x, w, transposed, name):
        return pl.pallas_call(
            functools.partial(share_kernel, transposed, chunk),
            out_shape=jax.ShapeDtypeStruct((nc, packed, 128), F32),
            grid=(4,),
            in_specs=[pl.BlockSpec((rows // 4, feat), lambda i: (i, 0)), whole(*w.shape)],
            out_specs=pl.BlockSpec((nc // 4, packed, 128), lambda i: (i, 0, 0)),
            compiler_params=params(20),
            name=name,
        )(x, w)

    scratch = [pltpu.VMEM(blocks, F32), pltpu.VMEM((chunk, 128), F32)]
    pre_share = once_there(share(all_in, wuc, False, "pre"), *steps[:2])
    pre_parts = once_there(lax.all_to_all(pre_share, COL, 0, 0), steps[2], far)
    pre, act = pl.pallas_call(
        act_kernel,
        out_shape=[jax.ShapeDtypeStruct(blocks, F32), jax.ShapeDtypeStruct((nc, packed, 128), BF)],
        in_specs=[SMEM, SMEM, VMEM],
        out_specs=[VMEM, VMEM],
        scratch_shapes=scratch,
        compiler_params=params(12),
        name="act",
    )(tu, td, pre_parts)
    grad_share = share(all_cot, wdc, True, "grad_act")
    act_parts = once_there(lax.all_to_all(act, COL, 0, 0), grad_share)
    grad_parts = lax.all_to_all(once_there(grad_share, act_parts), COL, 0, 0)
    wide = feat * 3 // 2
    hidden, own, fwd, back = pl.pallas_call(
        functools.partial(out_kernel, chunk),
        out_shape=[jax.ShapeDtypeStruct((rows, 512), BF)]
        + [jax.ShapeDtypeStruct((rows // ny, n), BF) for n in (feat, wide, wide)],
        in_specs=[SMEM, VMEM, VMEM],
        out_specs=[VMEM] * 4,
        compiler_params=params(12),
        name="out",
    )(at, act_parts, wdc)
    fwd, back = shift(fwd, "y", 1), shift(back, "y", -1)
    low, high = shift(fwd[:, feat:], "y", 1), shift(back[:, feat:], "y", -1)
    shares = [own, fwd, back, low, high]
    grad_pre = pl.pallas_call(
        grad_pre_kernel,
        out_shape=jax.ShapeDtypeStruct((nc, packed, 128), BF),
        in_specs=[SMEM, SMEM, VMEM, VMEM],
        out_specs=VMEM,
        scratch_shapes=scratch,
        compiler_params=params(12),
        name="grad_pre",
    )(tu, td, grad_parts, gelu_slope(pre))
    grad_pre_parts = lax.all_to_all(once_there(grad_pre, act_parts, fwd, back), COL, 0, 0)

    shares_z = pl.pallas_call(
        add_kernel,
        out_shape=[jax.ShapeDtypeStruct((tokens, feat), BF if j else F32) for j in range(nz)],
        in_specs=[SMEM] + [VMEM] * 5,
        out_specs=[VMEM] * nz,
        compiler_params=params(12),
        name="add",
    )(at, *[share.reshape(nz, tokens, -1) for share in shares])
    moved_z = [shift(shares_z[j], "z", j) for j in range(1, nz)]
    output = shares_z[0]
    for share in moved_z:
        output = output + share.astype(F32)

    step = rows // 4
    grad_hidden, part = pl.pallas_call(
        functools.partial(grad_in_kernel, chunk),
        out_shape=[jax.ShapeDtypeStruct((rows, n), BF) for n in (512, feat)],
        grid=(4,),
        in_specs=[pl.BlockSpec((nc // 4, packed, 128), lambda i: (i, 0, 0)), whole(feat, 512)],
        out_specs=[pl.BlockSpec((step, n), lambda i: (i, 0)) for n in (512, feat)],
        compiler_params=params(20),
        name="grad_in",
    )(once_there(grad_pre_parts, shares_z[0]), wuc)
    part = lax.all_to_all(part.reshape(ny, nz * tokens, feat), "y", 0, 0)
    part = once_there(part, *moved_z)
    part = part.astype(F32).sum(axis=0).astype(BF)
    part = lax.all_to_all(part.reshape(nz, tokens, feat), "z", 0, 0)
    grad_input = part.astype(F32).sum(axis=0)
    grad_down = pl.pallas_call(
        grad_down_kernel,
        out_shape=jax.ShapeDtypeStruct((hid, feat), F32),
        in_specs=[SMEM, SMEM, VMEM, VMEM],
        out_specs=VMEM,
        scratch_shapes=[pltpu.VMEM((512, feat), F32)],
        compiler_params=params(16),
        name="grad_down",
    )(td_own, md, hidden, all_cot)
    grad_up = pl.pallas_call(
        grad_up_kernel,
        out_shape=jax.ShapeDtypeStruct((feat, hid), F32),
        in_specs=[SMEM, SMEM, VMEM, VMEM],
        out_specs=VMEM,
        scratch_shapes=[pltpu.VMEM((4, feat, 128), F32)],
        compiler_params=params(16),
        name="grad_up",
    )(su_own, mu, grad_hidden, all_in)
    return output, grad_input, grad_up, grad_down


def solution(mesh):
    torus = Mesh(mesh.devices.reshape(4, 8, 4, 2), ROW + COL)
    block = P(ROW, COL)
    return jax.shard_map(
        on_device,
        mesh=torus,
        in_specs=(block, block, P(COL, ROW), block, P(), P()),
        out_specs=(block, block, P(COL, ROW), block),
        check_vma=False,
    )
```

time: 218 us -> 205 us (0.940)
  blocking collectives: 64.5 us -> 0 us
  local copies, waits for them, and re-layouts: 10.3 us -> 35.7 us
  starting transfers between devices: 46 us -> 70.3 us
  waiting for transfers between devices: 62.8 us -> 51.8 us
  Pallas kernels: 24.3 us -> 35 us
    all_to_all x2 -> x0, blocking collectives: 64.5 us -> none  [the longest x1 42.3 us: on_device(): part = lax.all_to_all(part.reshape(ny, nz * tokens, 2 * feat), 'y', 0, 0)]
    all_to_all x2 -> x8, starting transfers between devices: 8.62 us -> 41.5 us  [the longest x1 8.47 us: gather(): return lax.all_to_all(copies_of(a, axis), axis, 0, 0)]
    all_to_all x2 -> x8, waiting for transfers between devices: 44.7 us -> 23.4 us  [the longest x1 10.5 us: on_device(): grad_parts = lax.all_to_all(once_there(grad_share, act_parts), COL, 0, 0)]
    unnamed x18 -> x125, local copies, waits for them, and re-layouts: 4.45 us -> 24.3 us
    pallas_call x4 -> x10, Pallas kernels: 14.3 us -> 24.6 us  [the longest x2 4.09 us: share(): pl.pallas_call(functools.partial(share_kernel, transposed, chunk), out_sh...]
    ppermute x24 -> x23, waiting for transfers between devices: 18.1 us -> 28.4 us  [shift(): return lax.ppermute(a, axis, [(i, (i + by) % n) for i in range(n)])]
    ppermute x24 -> x23, starting transfers between devices: 37.4 us -> 28.8 us  [shift(): return lax.ppermute(a, axis, [(i, (i + by) % n) for i in range(n)])]
    broadcast_in_dim x4 -> x2, local copies, waits for them, and re-layouts: 0.23 us -> 2.93 us  [copies_of(): return jnp.broadcast_to(a[None], (lax.axis_size(axis),) + a.shape)]
  transfers between devices with their start and end apart: 26 -> 31, of which waited for: 11 -> 19; matrix products, arithmetic and copies ran while one was open for 4% -> 7% of each run, Pallas kernels for 6% -> 14%
where the time goes in v2:
time: 205 us; the launch traced here: 204 us
  starting transfers between devices  70.3 us (34%)
  waiting for transfers between devices  51.8 us (25%)
  local copies, waits for them, and re-layouts  35.7 us (17%)
  Pallas kernels  35 us (17%)
  other arithmetic  9.67 us (5%)
    ppermute x23, starting transfers between devices, shift(): return lax.ppermute(a, axis, [(i, (i + by) % n) for i in range(n)])  28.8 us
    ppermute x23, waiting for transfers between devices, shift(): return lax.ppermute(a, axis, [(i, (i + by) % n) for i in range(n)])  28.4 us
    unnamed x125, local copies, waits for them, and re-layouts  24.3 us
    all_to_all x1, waiting for transfers between devices, on_device(): grad_parts = lax.all_to_all(once_there(grad_share, act_parts), COL, 0, 0)  10.5 us
    all_to_all x1, starting transfers between devices, gather(): return lax.all_to_all(copies_of(a, axis), axis, 0, 0)  8.47 us
    pallas_call x1, Pallas kernels, on_device(): pl.pallas_call(grad_up_kernel, out_shape=jax.ShapeDtypeStruct((feat, hid)...  6.6 us
    all_to_all x1, starting transfers between devices, on_device(): part = lax.all_to_all(part.reshape(ny, nz * tokens, feat), 'y', 0, 0)  6.35 us
    all_to_all x1, starting transfers between devices, on_device(): lax.all_to_all(once_there(in_copies, own), 'y', 0, 0).reshape(rows, feat)  4.91 us
  transfers between devices with their start and end apart: 31, of which 19 were waited for; matrix products, arithmetic and copies ran while one was open for 7% of the time, Pallas kernels for 14%

profile of v2, /device:TPU:8, one launch (start us, length us, event | category | flops | bytes accessed | tf_op | source)
XLA Modules:
  0.0 203.6 jit_solution(13766119213367532541)
XLA Ops:
  2.2 8.5 %all-to-all-start = ((bf16[8,24,1024]{2,1,0:T(8,128)(2,1)}), bf16[8,24,1024]{2,1,0:T(8,128)(2,1)S(1)}, u32[]{:S(2)}, u32[]{:S(2)}) async-start(bf16[8,24,1024]{2,1,0:T(8,128)(2,1)} %broadcast_in_dim.33), calls=%async_computation | async-start | bytes 786432 | tf_op jit(solution)/shard_map/all_to_all | solution.py:222
  21.2 4.1 %all-to-all-done = bf16[8,24,1024]{2,1,0:T(8,128)(2,1)S(1)} async-done(((bf16[8,24,1024]{2,1,0:T(8,128)(2,1)}), bf16[8,24,1024]{2,1,0:T(8,128)(2,1)S(1)}, u32[]{:S(2)}, u32[]{:S(2)}) %all-to-all-start) | async-done | bytes 393248 | tf_op jit(solution)/shard_map/all_to_all | solution.py:222
  26.7 4.9 %all-to-all-start.1 = ((bf16[4,8,24,1024]{3,2,1,0:T(8,128)(2,1)}), bf16[4,8,24,1024]{3,2,1,0:T(8,128)(2,1)S(1)}, u32[]{:S(2)}, u32[]{:S(2)}) async-start(bf16[4,8,24,1024]{3,2,1,0:T(8,128)(2,1)} %broadcast_in_dim.34), calls=%async_computation.1 | async-start | bytes 3145728 | tf_op jit(solution)/shard_map/all_to_all | solution.py:270
  35.0 3.6 %collective-permute-done.5.refs_1_ = bf16[4,24,1024]{2,1,0:T(8,128)(2,1)S(1)} collective-permute-done((bf16[4,24,1024]{2,1,0:T(8,128)(2,1)S(1)}, bf16[4,24,1024]{2,1,0:T(8,128)(2,1)S(1)}, u32[]{:S(2)}, u32[]{:S(2)}) %collective-permute-start.5) | collective-permute-done | bytes 196640 | tf_op jit(solution)/shard_map/ppermute | solution.py:231
  43.5 3.0 %prep_up.1.w = bf16[1024,512]{1,0:T(8,128)(2,1)S(1)} custom-call(s32[7]{0:T(128)S(1)} %dynamic-slice_reduce_fusion.1.tu, s32[16,14]{1,0:T(8,128)S(1)} %copy.47.mu, bf16[1024,896]{1,0:T(8,128)(2,1)S(1)} %copy-done.7), custom_call_target="tpu_custom_call" | custom-call | tf_op jit(solution)/shard_map/prep_up/pallas_call | solution.py:302
  46.5 3.6 %all-to-all-done.1 = bf16[4,8,24,1024]{3,2,1,0:T(8,128)(2,1)S(1)} async-done(((bf16[4,8,24,1024]{3,2,1,0:T(8,128)(2,1)}), bf16[4,8,24,1024]{3,2,1,0:T(8,128)(2,1)S(1)}, u32[]{:S(2)}, u32[]{:S(2)}) %all-to-all-start.1) | async-done | bytes 1572896 | tf_op jit(solution)/shard_map/all_to_all | solution.py:270
  53.0 4.3 %all-to-all-start.2 = ((f32[8,336,128]{2,1,0:T(8,128)}), f32[8,336,128]{2,1,0:T(8,128)S(1)}, u32[]{:S(2)}, u32[]{:S(2)}) async-start(f32[8,336,128]{2,1,0:T(8,128)} %copy-done.4), calls=%async_computation.2 | async-start | bytes 2752512 | tf_op jit(solution)/shard_map/all_to_all | solution.py:336
  60.9 5.5 %collective-permute-done.9.refs_5_ = bf16[4,24,1024]{2,1,0:T(8,128)(2,1)S(1)} collective-permute-done((bf16[4,24,1024]{2,1,0:T(8,128)(2,1)}, bf16[4,24,1024]{2,1,0:T(8,128)(2,1)S(1)}, u32[]{:S(2)}, u32[]{:S(2)}) %collective-permute-start.9) | collective-permute-done | bytes 196640 | tf_op jit(solution)/shard_map/ppermute | solution.py:231
  71.9 3.4 %collective-permute-done.10.refs_6_ = bf16[4,24,512]{2,1,0:T(8,128)(2,1)} collective-permute-done((bf16[4,24,512]{2,1,0:T(8,128)(2,1)}, bf16[4,24,512]{2,1,0:T(8,128)(2,1)}, u32[]{:S(2)}, u32[]{:S(2)}) %collective-permute-start.10) | collective-permute-done | bytes 98336 | tf_op jit(solution)/shard_map/ppermute | solution.py:231
  76.8 3.4 %act.1 = (f32[7,96,128]{2,1,0:T(8,128)S(1)}, bf16[8,336,128]{2,1,0:T(8,128)(2,1)S(1)}) custom-call(s32[8,7]{1,0:T(8,128)S(1)} %copy.43.tu, s32[8,7]{1,0:T(8,128)S(1)} %copy.44.td, f32[8,336,128]{2,1,0:T(8,128)S(1)} %all-to-all-done.2.recv), custom_call_target="tpu_custom_call" | custom-call | tf_op jit(solution)/shard_map/act/pallas_call | solution.py:337
  81.9 4.4 %all-to-all-start.3 = ((bf16[8,336,128]{2,1,0:T(8,128)(2,1)}), bf16[8,336,128]{2,1,0:T(8,128)(2,1)}, u32[]{:S(2)}, u32[]{:S(2)}) async-start(bf16[8,336,128]{2,1,0:T(8,128)(2,1)} %copy-done.14), calls=%async_computation.3 | async-start | bytes 1376256 | tf_op jit(solution)/shard_map/all_to_all | solution.py:347
  98.8 4.6 %all-to-all-start.4 = ((f32[8,336,128]{2,1,0:T(8,128)}), f32[8,336,128]{2,1,0:T(8,128)}, u32[]{:S(2)}, u32[]{:S(2)}) async-start(f32[8,336,128]{2,1,0:T(8,128)} %copy-done.5), calls=%async_computation.4 | async-start | bytes 2752512 | tf_op jit(solution)/shard_map/all_to_all | solution.py:348
  104.7 3.0 %out.1 = (bf16[768,512]{1,0:T(8,128)(2,1)S(1)}, bf16[192,1024]{1,0:T(8,128)(2,1)S(1)}, bf16[192,1536]{1,0:T(8,128)(2,1)}, bf16[192,1536]{1,0:T(8,128)(2,1)}) custom-call(s32[2]{0:T(128)S(1)} %copy-done.35, bf16[8,336,128]{2,1,0:T(8,128)(2,1)} %all-to-all-done.3.h, bf16[512,1024]{1,0:T(8,128)(2,1)S(1)} %copy-done.1), custom_call_target="tpu_custom_call" | custom-call | tf_op jit(solution)/shard_map/out/pallas_call | solution.py:350
  112.5 10.5 %all-to-all-done.4.recv = f32[8,336,128]{2,1,0:T(8,128)} async-done(((f32[8,336,128]{2,1,0:T(8,128)}), f32[8,336,128]{2,1,0:T(8,128)}, u32[]{:S(2)}, u32[]{:S(2)}) %all-to-all-start.4) | async-done | bytes 1376288 | tf_op jit(solution)/shard_map/all_to_all | solution.py:348
  123.0 4.1 %grad_pre.1 = bf16[8,336,128]{2,1,0:T(8,128)(2,1)S(1)} custom-call(s32[8,7]{1,0:T(8,128)S(1)} %copy-done.29, s32[8,7]{1,0:T(8,128)S(1)} %copy-done.31, f32[8,336,128]{2,1,0:T(8,128)} %all-to-all-done.4.recv, f32[7,96,128]{2,1,0:T(8,128)S(1)} %fusion.2.slope), custom_call_target="tpu_custom_call" | custom-call | tf_op jit(solution)/shard_map/grad_pre/pallas_call | solution.py:362
  128.0 4.4 %all-to-all-start.5 = ((bf16[8,336,128]{2,1,0:T(8,128)(2,1)}), bf16[8,336,128]{2,1,0:T(8,128)(2,1)}, u32[]{:S(2)}, u32[]{:S(2)}) async-start(bf16[8,336,128]{2,1,0:T(8,128)(2,1)} %copy-done.6), calls=%async_computation.5 | async-start | bytes 1376256 | tf_op jit(solution)/shard_map/all_to_all | solution.py:371
  136.4 4.1 %collective-permute-done.14 = bf16[192,512]{1,0:T(8,128)(2,1)S(1)} collective-permute-done((bf16[192,512]{1,0:T(8,128)(2,1)S(1)}, bf16[192,512]{1,0:T(8,128)(2,1)S(1)}, u32[]{:S(2)}, u32[]{:S(2)}) %collective-permute-start.14) | collective-permute-done | bytes 196640 | tf_op jit(solution)/shard_map/ppermute | solution.py:231
  150.5 3.4 %grad_in.1 = (bf16[768,512]{1,0:T(8,128)(2,1)S(1)}, bf16[768,1024]{1,0:T(8,128)(2,1)S(1)}) custom-call(bf16[8,336,128]{2,1,0:T(8,128)(2,1)} %all-to-all-done.5.h, bf16[1024,512]{1,0:T(8,128)(2,1)S(1)} %copy-done.3), custom_call_target="tpu_custom_call" | custom-call | tf_op jit(solution)/shard_map/grad_in/pallas_call | solution.py:387
  156.0 6.3 %all-to-all-start.6 = ((bf16[4,192,1024]{2,1,0:T(8,128)(2,1)}), bf16[4,192,1024]{2,1,0:T(8,128)(2,1)}, u32[]{:S(2)}, u32[]{:S(2)}) async-start(bf16[4,192,1024]{2,1,0:T(8,128)(2,1)} %bitcast.26), calls=%async_computation.6 | async-start | bytes 3145728 | tf_op jit(solution)/shard_map/all_to_all | solution.py:396
  162.6 3.1 %collective-permute-start.18 = (bf16[24,1024]{1,0:T(8,128)(2,1)S(1)}, bf16[24,1024]{1,0:T(8,128)(2,1)S(1)}, u32[]{:S(2)}, u32[]{:S(2)}) collective-permute-start(bf16[24,1024]{1,0:T(8,128)(2,1)S(1)} %copy-done.46), channel_id=1, source_target_pairs={{0,24},{8,32},{16,40},{24,48},{32,56},{40,0},{48,8},{56,16},{1,25}... | collective-permute-start | bytes 147464 | tf_op jit(solution)/shard_map/ppermute | solution.py:231
  165.8 3.2 %collective-permute-start.19 = (bf16[24,1024]{1,0:T(8,128)(2,1)S(1)}, bf16[24,1024]{1,0:T(8,128)(2,1)S(1)}, u32[]{:S(2)}, u32[]{:S(2)}) collective-permute-start(bf16[24,1024]{1,0:T(8,128)(2,1)S(1)} %copy-done.44), channel_id=1, source_target_pairs={{0,32},{8,40},{16,48},{24,56},{32,0},{40,8},{48,16},{56,24},{1,33}... | collective-permute-start | bytes 147464 | tf_op jit(solution)/shard_map/ppermute | solution.py:231
  184.2 4.1 %all-to-all-start.7 = ((bf16[8,24,1024]{2,1,0:T(8,128)(2,1)}), bf16[8,24,1024]{2,1,0:T(8,128)(2,1)}, u32[]{:S(2)}, u32[]{:S(2)}) async-start(bf16[8,24,1024]{2,1,0:T(8,128)(2,1)} %bitcast.30), calls=%async_computation.7 | async-start | bytes 786432 | tf_op jit(solution)/shard_map/all_to_all | solution.py:399
  190.2 3.8 %grad_down.1 = f32[896,1024]{1,0:T(8,128)} custom-call(s32[7]{0:T(128)S(1)} %copy-done.33, s32[14,16]{1,0:T(8,128)S(1)} %dynamic_slice.26.md, bf16[768,512]{1,0:T(8,128)(2,1)S(1)} %copy-done.11, bf16[768,1024]{1,0:T(8,128)(2,1)S(1)} %bitcast.25), custom_call_target="tpu_custom_call" | custom-call | tf_op jit(solution)/shard_map/grad_down/pallas_call | solution.py:401
  194.7 6.6 %grad_up.1 = f32[1024,896]{1,0:T(8,128)} custom-call(s32[14]{0:T(128)S(1)} %fusion.6.su, s32[16,14]{1,0:T(8,128)S(1)} %copy.47.mu, bf16[768,512]{1,0:T(8,128)(2,1)S(1)} %copy-done.13, bf16[768,1024]{1,0:T(8,128)(2,1)S(1)} %bitcast.23), custom_call_target="tpu_custom_call" | custom-call | tf_op jit(solution)/shard_map/grad_up/pallas_call | solution.py:410
  (213 shorter events, 92.5 us)
Async XLA Ops:
  2.2 23.2 %all-to-all-start = ((bf16[8,24,1024]{2,1,0:T(8,128)(2,1)}), bf16[8,24,1024]{2,1,0:T(8,128)(2,1)S(1)}, u32[]{:S(2)}, u32[]{:S(2)}) async-start(bf16[8,24,1024]{2,1,0:T(8,128)(2,1)} %broadcast_in_dim.33), calls=%async_computation | async-start | bytes 786432 | tf_op jit(solution)/shard_map/all_to_all | solution.py:222
  26.7 23.4 %all-to-all-start.1 = ((bf16[4,8,24,1024]{3,2,1,0:T(8,128)(2,1)}), bf16[4,8,24,1024]{3,2,1,0:T(8,128)(2,1)S(1)}, u32[]{:S(2)}, u32[]{:S(2)}) async-start(bf16[4,8,24,1024]{3,2,1,0:T(8,128)(2,1)} %broadcast_in_dim.34), calls=%async_computation.1 | async-start | bytes 3145728 | tf_op jit(solution)/shard_map/all_to_all | solution.py:270
  33.0 7.0 %collective-permute-start.4 = (bf16[4,24,1024]{2,1,0:T(8,128)(2,1)S(1)}, bf16[4,24,1024]{2,1,0:T(8,128)(2,1)S(1)}, u32[]{:S(2)}, u32[]{:S(2)}) collective-permute-start(bf16[4,24,1024]{2,1,0:T(8,128)(2,1)S(1)} %pad_maximum_fusion.own), channel_id=1, source_target_pairs={{0,8},{8,16},{16,24},{24,32},{32,40},{40,48},{48,56},{56,0},{1,9},... | collective-permute-start | bytes 589832 | tf_op jit(solution)/shard_map/ppermute | solution.py:231
  38.7 14.4 %collective-permute-start.7 = (bf16[4,24,1024]{2,1,0:T(8,128)(2,1)S(1)}, bf16[4,24,1024]{2,1,0:T(8,128)(2,1)S(1)}, u32[]{:S(2)}, u32[]{:S(2)}) collective-permute-start(bf16[4,24,1024]{2,1,0:T(8,128)(2,1)S(1)} %collective-permute-done.5.refs_1_), channel_id=1, source_target_pairs={{0,56},{8,0},{16,8},{24,16},{32,24},{40,32},{48,40},{56,48},{1,57}... | collective-permute-start | bytes 589832 | tf_op jit(solution)/shard_map/ppermute | solution.py:231
  40.0 13.1 %collective-permute-start.6 = (bf16[4,24,1024]{2,1,0:T(8,128)(2,1)S(1)}, bf16[4,24,1024]{2,1,0:T(8,128)(2,1)}, u32[]{:S(2)}, u32[]{:S(2)}) collective-permute-start(bf16[4,24,1024]{2,1,0:T(8,128)(2,1)S(1)} %collective-permute-done.4.refs_0_), channel_id=1, source_target_pairs={{0,8},{8,16},{16,24},{24,32},{32,40},{40,48},{48,56},{56,0},{1,9},... | collective-permute-start | bytes 589832 | tf_op jit(solution)/shard_map/ppermute | solution.py:231
  53.0 23.8 %all-to-all-start.2 = ((f32[8,336,128]{2,1,0:T(8,128)}), f32[8,336,128]{2,1,0:T(8,128)S(1)}, u32[]{:S(2)}, u32[]{:S(2)}) async-start(f32[8,336,128]{2,1,0:T(8,128)} %copy-done.4), calls=%async_computation.2 | async-start | bytes 2752512 | tf_op jit(solution)/shard_map/all_to_all | solution.py:336
  58.8 7.5 %collective-permute-start.9 = (bf16[4,24,1024]{2,1,0:T(8,128)(2,1)}, bf16[4,24,1024]{2,1,0:T(8,128)(2,1)S(1)}, u32[]{:S(2)}, u32[]{:S(2)}) collective-permute-start(bf16[4,24,1024]{2,1,0:T(8,128)(2,1)} %copy-done.24), channel_id=1, source_target_pairs={{0,56},{8,0},{16,8},{24,16},{32,24},{40,32},{48,40},{56,48},{1,57}... | collective-permute-start | bytes 589832 | tf_op jit(solution)/shard_map/ppermute | solution.py:231
  58.9 9.7 %collective-permute-start.8 = (bf16[4,24,1024]{2,1,0:T(8,128)(2,1)}, bf16[4,24,1024]{2,1,0:T(8,128)(2,1)S(1)}, u32[]{:S(2)}, u32[]{:S(2)}) collective-permute-start(bf16[4,24,1024]{2,1,0:T(8,128)(2,1)} %collective-permute-done.6.refs_2_), channel_id=1, source_target_pairs={{0,8},{8,16},{16,24},{24,32},{32,40},{40,48},{48,56},{56,0},{1,9},... | collective-permute-start | bytes 589832 | tf_op jit(solution)/shard_map/ppermute | solution.py:231
  69.2 6.1 %collective-permute-start.10 = (bf16[4,24,512]{2,1,0:T(8,128)(2,1)}, bf16[4,24,512]{2,1,0:T(8,128)(2,1)}, u32[]{:S(2)}, u32[]{:S(2)}) collective-permute-start(bf16[4,24,512]{2,1,0:T(8,128)(2,1)} %slice.26), channel_id=1, source_target_pairs={{0,8},{8,16},{16,24},{24,32},{32,40},{40,48},{48,56},{56,0},{1,9},... | collective-permute-start | bytes 294920 | tf_op jit(solution)/shard_map/ppermute | solution.py:231
  81.9 16.9 %all-to-all-start.3 = ((bf16[8,336,128]{2,1,0:T(8,128)(2,1)}), bf16[8,336,128]{2,1,0:T(8,128)(2,1)}, u32[]{:S(2)}, u32[]{:S(2)}) async-start(bf16[8,336,128]{2,1,0:T(8,128)(2,1)} %copy-done.14), calls=%async_computation.3 | async-start | bytes 1376256 | tf_op jit(solution)/shard_map/all_to_all | solution.py:347
  98.8 24.2 %all-to-all-start.4 = ((f32[8,336,128]{2,1,0:T(8,128)}), f32[8,336,128]{2,1,0:T(8,128)}, u32[]{:S(2)}, u32[]{:S(2)}) async-start(f32[8,336,128]{2,1,0:T(8,128)} %copy-done.5), calls=%async_computation.4 | async-start | bytes 2752512 | tf_op jit(solution)/shard_map/all_to_all | solution.py:348
  109.4 18.6 %collective-permute-start.12 = (bf16[192,1536]{1,0:T(8,128)(2,1)}, bf16[192,1536]{1,0:T(8,128)(2,1)}, u32[]{:S(2)}, u32[]{:S(2)}) collective-permute-start(bf16[192,1536]{1,0:T(8,128)(2,1)} %get-tuple-element.36), channel_id=1, source_target_pairs={{0,64},{64,128},{128,192},{192,0},{1,65},{65,129},{129,193},{193,1... | collective-permute-start | bytes 1769480 | tf_op jit(solution)/shard_map/ppermute | solution.py:231
  109.4 18.6 %collective-permute-start.13 = (bf16[192,1536]{1,0:T(8,128)(2,1)}, bf16[192,1536]{1,0:T(8,128)(2,1)}, u32[]{:S(2)}, u32[]{:S(2)}) collective-permute-start(bf16[192,1536]{1,0:T(8,128)(2,1)} %get-tuple-element.37), channel_id=1, source_target_pairs={{0,192},{64,0},{128,64},{192,128},{1,193},{65,1},{129,65},{193,129... | collective-permute-start | bytes 1769480 | tf_op jit(solution)/shard_map/ppermute | solution.py:231
  128.0 21.3 %all-to-all-start.5 = ((bf16[8,336,128]{2,1,0:T(8,128)(2,1)}), bf16[8,336,128]{2,1,0:T(8,128)(2,1)}, u32[]{:S(2)}, u32[]{:S(2)}) async-start(bf16[8,336,128]{2,1,0:T(8,128)(2,1)} %copy-done.6), calls=%async_computation.5 | async-start | bytes 1376256 | tf_op jit(solution)/shard_map/all_to_all | solution.py:371
  133.3 7.3 %collective-permute-start.14 = (bf16[192,512]{1,0:T(8,128)(2,1)S(1)}, bf16[192,512]{1,0:T(8,128)(2,1)S(1)}, u32[]{:S(2)}, u32[]{:S(2)}) collective-permute-start(bf16[192,512]{1,0:T(8,128)(2,1)S(1)} %slice.28), channel_id=1, source_target_pairs={{0,64},{64,128},{128,192},{192,0},{1,65},{65,129},{129,193},{193,1... | collective-permute-start | bytes 589832 | tf_op jit(solution)/shard_map/ppermute | solution.py:231
  134.3 7.9 %collective-permute-start.15 = (bf16[192,512]{1,0:T(8,128)(2,1)S(1)}, bf16[192,512]{1,0:T(8,128)(2,1)S(1)}, u32[]{:S(2)}, u32[]{:S(2)}) collective-permute-start(bf16[192,512]{1,0:T(8,128)(2,1)S(1)} %slice.29), channel_id=1, source_target_pairs={{0,192},{64,0},{128,64},{192,128},{1,193},{65,1},{129,65},{193,129... | collective-permute-start | bytes 589832 | tf_op jit(solution)/shard_map/ppermute | solution.py:231
  156.0 25.6 %all-to-all-start.6 = ((bf16[4,192,1024]{2,1,0:T(8,128)(2,1)}), bf16[4,192,1024]{2,1,0:T(8,128)(2,1)}, u32[]{:S(2)}, u32[]{:S(2)}) async-start(bf16[4,192,1024]{2,1,0:T(8,128)(2,1)} %bitcast.26), calls=%async_computation.6 | async-start | bytes 3145728 | tf_op jit(solution)/shard_map/all_to_all | solution.py:396
  162.4 8.0 %collective-permute-start.16 = (bf16[24,1024]{1,0:T(8,128)(2,1)S(1)}, bf16[24,1024]{1,0:T(8,128)(2,1)S(1)}, u32[]{:S(2)}, u32[]{:S(2)}) collective-permute-start(bf16[24,1024]{1,0:T(8,128)(2,1)S(1)} %copy-done.50), channel_id=1, source_target_pairs={{0,8},{8,16},{16,24},{24,32},{32,40},{40,48},{48,56},{56,0},{1,9},... | collective-permute-start | bytes 147464 | tf_op jit(solution)/shard_map/ppermute | solution.py:231
  162.4 10.8 %collective-permute-start.17 = (bf16[24,1024]{1,0:T(8,128)(2,1)S(1)}, bf16[24,1024]{1,0:T(8,128)(2,1)S(1)}, u32[]{:S(2)}, u32[]{:S(2)}) collective-permute-start(bf16[24,1024]{1,0:T(8,128)(2,1)S(1)} %copy-done.48), channel_id=1, source_target_pairs={{0,16},{8,24},{16,32},{24,40},{32,48},{40,56},{48,0},{56,8},{1,17}... | collective-permute-start | bytes 147464 | tf_op jit(solution)/shard_map/ppermute | solution.py:231
  162.6 12.3 %collective-permute-start.18 = (bf16[24,1024]{1,0:T(8,128)(2,1)S(1)}, bf16[24,1024]{1,0:T(8,128)(2,1)S(1)}, u32[]{:S(2)}, u32[]{:S(2)}) collective-permute-start(bf16[24,1024]{1,0:T(8,128)(2,1)S(1)} %copy-done.46), channel_id=1, source_target_pairs={{0,24},{8,32},{16,40},{24,48},{32,56},{40,0},{48,8},{56,16},{1,25}... | collective-permute-start | bytes 147464 | tf_op jit(solution)/shard_map/ppermute | solution.py:231
  165.8 9.1 %collective-permute-start.19 = (bf16[24,1024]{1,0:T(8,128)(2,1)S(1)}, bf16[24,1024]{1,0:T(8,128)(2,1)S(1)}, u32[]{:S(2)}, u32[]{:S(2)}) collective-permute-start(bf16[24,1024]{1,0:T(8,128)(2,1)S(1)} %copy-done.44), channel_id=1, source_target_pairs={{0,32},{8,40},{16,48},{24,56},{32,0},{40,8},{48,16},{56,24},{1,33}... | collective-permute-start | bytes 147464 | tf_op jit(solution)/shard_map/ppermute | solution.py:231
  169.0 6.5 %collective-permute-start.20 = (bf16[24,1024]{1,0:T(8,128)(2,1)S(1)}, bf16[24,1024]{1,0:T(8,128)(2,1)S(1)}, u32[]{:S(2)}, u32[]{:S(2)}) collective-permute-start(bf16[24,1024]{1,0:T(8,128)(2,1)S(1)} %copy-done.42), channel_id=1, source_target_pairs={{0,40},{8,48},{16,56},{24,0},{32,8},{40,16},{48,24},{56,32},{1,41}... | collective-permute-start | bytes 147464 | tf_op jit(solution)/shard_map/ppermute | solution.py:231
  170.3 7.5 %collective-permute-start.21 = (bf16[24,1024]{1,0:T(8,128)(2,1)S(1)}, bf16[24,1024]{1,0:T(8,128)(2,1)S(1)}, u32[]{:S(2)}, u32[]{:S(2)}) collective-permute-start(bf16[24,1024]{1,0:T(8,128)(2,1)S(1)} %copy-done.40), channel_id=1, source_target_pairs={{0,48},{8,56},{16,0},{24,8},{32,16},{40,24},{48,32},{56,40},{1,49}... | collective-permute-start | bytes 147464 | tf_op jit(solution)/shard_map/ppermute | solution.py:231
  184.2 17.8 %all-to-all-start.7 = ((bf16[8,24,1024]{2,1,0:T(8,128)(2,1)}), bf16[8,24,1024]{2,1,0:T(8,128)(2,1)}, u32[]{:S(2)}, u32[]{:S(2)}) async-start(bf16[8,24,1024]{2,1,0:T(8,128)(2,1)} %bitcast.30), calls=%async_computation.7 | async-start | bytes 786432 | tf_op jit(solution)/shard_map/all_to_all | solution.py:399
  (69 other events, 375.3 us)

commit v3 on v2

--- a/solution.py
+++ b/solution.py
@@ -21,6 +21,10 @@
 
 def params(mib):
     return pltpu.CompilerParams(vmem_limit_bytes=mib * 1024 * 1024)
+
+
+def hbm(shape, dtype):
+    return pltpu.HBM(shape, dtype)
 
 
 def lane_half(shape):
@@ -299,6 +303,7 @@
     mu = lax.dynamic_slice(up_row, (col_at * ft, 0), (ft, ht))
     md = lax.dynamic_slice(down_row, (0, col_at * ft), (ht, ft))
 
+    all_in = once_there(all_in, td, td_own, md)
     wuc = pl.pallas_call(
         prep_up_kernel,
         out_shape=jax.ShapeDtypeStruct((feat, 512), BF),
@@ -323,7 +328,7 @@
     def share(x, w, transposed, name):
         return pl.pallas_call(
             functools.partial(share_kernel, transposed, chunk),
-            out_shape=jax.ShapeDtypeStruct((nc, packed, 128), F32),
+            out_shape=hbm((nc, packed, 128), F32),
             grid=(4,),
             in_specs=[pl.BlockSpec((rows // 4, feat), lambda i: (i, 0)), whole(*w.shape)],
             out_specs=pl.BlockSpec((nc // 4, packed, 128), lambda i: (i, 0, 0)),
@@ -336,7 +341,7 @@
     pre_parts = once_there(lax.all_to_all(pre_share, COL, 0, 0), steps[2], far)
     pre, act = pl.pallas_call(
         act_kernel,
-        out_shape=[jax.ShapeDtypeStruct(blocks, F32), jax.ShapeDtypeStruct((nc, packed, 128), BF)],
+        out_shape=[hbm(blocks, F32), hbm((nc, packed, 128), BF)],
         in_specs=[SMEM, SMEM, VMEM],
         out_specs=[VMEM, VMEM],
         scratch_shapes=scratch,
@@ -349,8 +354,7 @@
     wide = feat * 3 // 2
     hidden, own, fwd, back = pl.pallas_call(
         functools.partial(out_kernel, chunk),
-        out_shape=[jax.ShapeDtypeStruct((rows, 512), BF)]
-        + [jax.ShapeDtypeStruct((rows // ny, n), BF) for n in (feat, wide, wide)],
+        out_shape=[hbm((rows, 512), BF)] + [hbm((rows // ny, n), BF) for n in (feat, wide, wide)],
         in_specs=[SMEM, VMEM, VMEM],
         out_specs=[VMEM] * 4,
         compiler_params=params(12),
@@ -361,7 +365,7 @@
     shares = [own, fwd, back, low, high]
     grad_pre = pl.pallas_call(
         grad_pre_kernel,
-        out_shape=jax.ShapeDtypeStruct((nc, packed, 128), BF),
+        out_shape=hbm((nc, packed, 128), BF),
         in_specs=[SMEM, SMEM, VMEM, VMEM],
         out_specs=VMEM,
         scratch_shapes=scratch,
@@ -372,7 +376,7 @@
 
     shares_z = pl.pallas_call(
         add_kernel,
-        out_shape=[jax.ShapeDtypeStruct((tokens, feat), BF if j else F32) for j in range(nz)],
+        out_shape=[hbm((tokens, feat), BF if j else F32) for j in range(nz)],
         in_specs=[SMEM] + [VMEM] * 5,
         out_specs=[VMEM] * nz,
         compiler_params=params(12),
@@ -386,13 +390,13 @@
     step = rows // 4
     grad_hidden, part = pl.pallas_call(
         functools.partial(grad_in_kernel, chunk),
-        out_shape=[jax.ShapeDtypeStruct((rows, n), BF) for n in (512, feat)],
+        out_shape=[hbm((rows, n), BF) for n in (512, feat)],
         grid=(4,),
         in_specs=[pl.BlockSpec((nc // 4, packed, 128), lambda i: (i, 0, 0)), whole(feat, 512)],
         out_specs=[pl.BlockSpec((step, n), lambda i: (i, 0)) for n in (512, feat)],
         compiler_params=params(20),
         name="grad_in",
-    )(once_there(grad_pre_parts, shares_z[0]), wuc)
+    )(once_there(grad_pre_parts, low, high), wuc)
     part = lax.all_to_all(part.reshape(ny, nz * tokens, feat), "y", 0, 0)
     part = once_there(part, *moved_z)
     part = part.astype(F32).sum(axis=0).astype(BF)

time: 205 us -> 202 us (0.985)
  local copies, waits for them, and re-layouts: 35.7 us -> 29.2 us
  Pallas kernels: 35 us -> 40.6 us
  waiting for transfers between devices: 51.8 us -> 49.5 us
    unnamed x125 -> x77, local copies, waits for them, and re-layouts: 24.3 us -> 16.2 us
    pallas_call x5, Pallas kernels: 15.4 us -> 19.1 us  [the longest x1 4.91 us: on_device(): pl.pallas_call(grad_pre_kernel, out_shape=hbm((nc, packed, 128), BF), in_...]
    all_to_all x1, waiting for transfers between devices: 2.97 us -> 0.01 us  [on_device(): part = lax.all_to_all(part.reshape(ny, nz * tokens, feat), 'y', 0, 0)]
    ppermute x23, waiting for transfers between devices: 28.4 us -> 26 us  [shift(): return lax.ppermute(a, axis, [(i, (i + by) % n) for i in range(n)])]
    all_to_all x1, waiting for transfers between devices: 3.65 us -> 1.2 us  [on_device(): lax.all_to_all(once_there(in_copies, own), 'y', 0, 0).reshape(rows, feat)]
    all_to_all x1, waiting for transfers between devices: 0.01 us -> 2.17 us  [on_device(): lax.all_to_all(once_there(grad_pre, act_parts, fwd, back), COL, 0, 0)]
  transfers between devices with their start and end apart: 31 -> 31, of which waited for: 19 -> 18; matrix products, arithmetic and copies ran while one was open for 7% -> 7% of each run, Pallas kernels for 14% -> 16%
where the time goes in v3:
time: 202 us; the launch traced here: 200 us
  starting transfers between devices  70.9 us (35%)
  waiting for transfers between devices  49.5 us (25%)
  Pallas kernels  40.6 us (20%)
  local copies, waits for them, and re-layouts  29.2 us (14%)
  other arithmetic  9.04 us (4%)
    ppermute x23, starting transfers between devices, shift(): return lax.ppermute(a, axis, [(i, (i + by) % n) for i in range(n)])  30.3 us
    ppermute x23, waiting for transfers between devices, shift(): return lax.ppermute(a, axis, [(i, (i + by) % n) for i in range(n)])  26 us
    unnamed x77, local copies, waits for them, and re-layouts  16.2 us
    all_to_all x1, waiting for transfers between devices, on_device(): grad_parts = lax.all_to_all(once_there(grad_share, act_parts), COL, 0, 0)  11.7 us
    all_to_all x1, starting transfers between devices, gather(): return lax.all_to_all(copies_of(a, axis), axis, 0, 0)  8.47 us
    pallas_call x1, Pallas kernels, on_device(): pl.pallas_call(grad_up_kernel, out_shape=jax.ShapeDtypeStruct((feat, hid)...  6.6 us
    pallas_call x2, Pallas kernels, share(): pl.pallas_call(functools.partial(share_kernel, transposed, chunk), out_sh...  6 us
    all_to_all x1, starting transfers between devices, on_device(): part = lax.all_to_all(part.reshape(ny, nz * tokens, feat), 'y', 0, 0)  5.9 us
  transfers between devices with their start and end apart: 31, of which 18 were waited for; matrix products, arithmetic and copies ran while one was open for 7% of the time, Pallas kernels for 16%

profile of v3, /device:TPU:8, one launch (start us, length us, event | category | flops | bytes accessed | tf_op | source)
XLA Modules:
  0.0 200.2 jit_solution(8535334299511073360)
XLA Ops:
  2.2 8.5 %all-to-all-start = ((bf16[8,24,1024]{2,1,0:T(8,128)(2,1)}), bf16[8,24,1024]{2,1,0:T(8,128)(2,1)S(1)}, u32[]{:S(2)}, u32[]{:S(2)}) async-start(bf16[8,24,1024]{2,1,0:T(8,128)(2,1)} %broadcast_in_dim.33), calls=%async_computation | async-start | bytes 786432 | tf_op jit(solution)/shard_map/all_to_all | solution.py:226
  21.2 4.1 %all-to-all-done = bf16[8,24,1024]{2,1,0:T(8,128)(2,1)S(1)} async-done(((bf16[8,24,1024]{2,1,0:T(8,128)(2,1)}), bf16[8,24,1024]{2,1,0:T(8,128)(2,1)S(1)}, u32[]{:S(2)}, u32[]{:S(2)}) %all-to-all-start) | async-done | bytes 393248 | tf_op jit(solution)/shard_map/all_to_all | solution.py:226
  26.7 4.9 %all-to-all-start.1 = ((bf16[4,8,24,1024]{3,2,1,0:T(8,128)(2,1)}), bf16[4,8,24,1024]{3,2,1,0:T(8,128)(2,1)S(1)}, u32[]{:S(2)}, u32[]{:S(2)}) async-start(bf16[4,8,24,1024]{3,2,1,0:T(8,128)(2,1)} %broadcast_in_dim.34), calls=%async_computation.1 | async-start | bytes 3145728 | tf_op jit(solution)/shard_map/all_to_all | solution.py:274
  37.4 3.6 %collective-permute-done.5.refs_1_ = bf16[4,24,1024]{2,1,0:T(8,128)(2,1)S(1)} collective-permute-done((bf16[4,24,1024]{2,1,0:T(8,128)(2,1)S(1)}, bf16[4,24,1024]{2,1,0:T(8,128)(2,1)S(1)}, u32[]{:S(2)}, u32[]{:S(2)}) %collective-permute-start.5) | collective-permute-done | bytes 196640 | tf_op jit(solution)/shard_map/ppermute | solution.py:235
  45.9 3.0 %prep_up.1.w = bf16[1024,512]{1,0:T(8,128)(2,1)S(1)} custom-call(s32[7]{0:T(128)S(1)} %dynamic-slice_reduce_fusion.tu, s32[16,14]{1,0:T(8,128)S(1)} %copy.47.mu, bf16[1024,896]{1,0:T(8,128)(2,1)S(1)} %copy-done.4), custom_call_target="tpu_custom_call" | custom-call | tf_op jit(solution)/shard_map/prep_up/pallas_call | solution.py:307
  53.6 4.3 %all-to-all-start.2 = ((f32[8,336,128]{2,1,0:T(8,128)}), f32[8,336,128]{2,1,0:T(8,128)S(1)}, u32[]{:S(2)}, u32[]{:S(2)}) async-start(f32[8,336,128]{2,1,0:T(8,128)} %pre.1), calls=%async_computation.2 | async-start | bytes 2752512 | tf_op jit(solution)/shard_map/all_to_all | solution.py:341
  60.0 5.5 %collective-permute-done.9.refs_5_ = bf16[4,24,1024]{2,1,0:T(8,128)(2,1)S(1)} collective-permute-done((bf16[4,24,1024]{2,1,0:T(8,128)(2,1)}, bf16[4,24,1024]{2,1,0:T(8,128)(2,1)S(1)}, u32[]{:S(2)}, u32[]{:S(2)}) %collective-permute-start.9) | collective-permute-done | bytes 196640 | tf_op jit(solution)/shard_map/ppermute | solution.py:235
  72.0 3.5 %collective-permute-done.10.refs_6_ = bf16[4,24,512]{2,1,0:T(8,128)(2,1)} collective-permute-done((bf16[4,24,512]{2,1,0:T(8,128)(2,1)}, bf16[4,24,512]{2,1,0:T(8,128)(2,1)}, u32[]{:S(2)}, u32[]{:S(2)}) %collective-permute-start.10) | collective-permute-done | bytes 98336 | tf_op jit(solution)/shard_map/ppermute | solution.py:235
  78.8 4.3 %act.1 = (f32[7,96,128]{2,1,0:T(8,128)}, bf16[8,336,128]{2,1,0:T(8,128)(2,1)}) custom-call(s32[8,7]{1,0:T(8,128)S(1)} %copy-done.23, s32[8,7]{1,0:T(8,128)S(1)} %copy-done.21, f32[8,336,128]{2,1,0:T(8,128)S(1)} %all-to-all-done.2.recv), custom_call_target="tpu_custom_call" | custom-call | tf_op jit(solution)/shard_map/act/pallas_call | solution.py:342
  83.0 4.4 %all-to-all-start.3 = ((bf16[8,336,128]{2,1,0:T(8,128)(2,1)}), bf16[8,336,128]{2,1,0:T(8,128)(2,1)}, u32[]{:S(2)}, u32[]{:S(2)}) async-start(bf16[8,336,128]{2,1,0:T(8,128)(2,1)} %get-tuple-element.34), calls=%async_computation.3 | async-start | bytes 1376256 | tf_op jit(solution)/shard_map/all_to_all | solution.py:352
  93.8 3.2 %grad_act.1 = f32[8,336,128]{2,1,0:T(8,128)} custom-call(bf16[768,1024]{1,0:T(8,128)(2,1)S(1)} %bitcast.24, bf16[512,1024]{1,0:T(8,128)(2,1)S(1)} %prep_down.1.w), custom_call_target="tpu_custom_call" | custom-call | tf_op jit(solution)/shard_map/grad_act/pallas_call | solution.py:329
  99.4 4.3 %all-to-all-start.4 = ((f32[8,336,128]{2,1,0:T(8,128)}), f32[8,336,128]{2,1,0:T(8,128)}, u32[]{:S(2)}, u32[]{:S(2)}) async-start(f32[8,336,128]{2,1,0:T(8,128)} %grad_act.1), calls=%async_computation.4 | async-start | bytes 2752512 | tf_op jit(solution)/shard_map/all_to_all | solution.py:353
  104.9 3.4 %out.1 = (bf16[768,512]{1,0:T(8,128)(2,1)}, bf16[192,1024]{1,0:T(8,128)(2,1)}, bf16[192,1536]{1,0:T(8,128)(2,1)}, bf16[192,1536]{1,0:T(8,128)(2,1)}) custom-call(s32[2]{0:T(128)S(1)} %copy-done.28, bf16[8,336,128]{2,1,0:T(8,128)(2,1)} %all-to-all-done.3.h, bf16[512,1024]{1,0:T(8,128)(2,1)S(1)} %copy-done.1), custom_call_target="tpu_custom_call" | custom-call | tf_op jit(solution)/shard_map/out/pallas_call | solution.py:355
  111.4 11.7 %all-to-all-done.4.recv = f32[8,336,128]{2,1,0:T(8,128)} async-done(((f32[8,336,128]{2,1,0:T(8,128)}), f32[8,336,128]{2,1,0:T(8,128)}, u32[]{:S(2)}, u32[]{:S(2)}) %all-to-all-start.4) | async-done | bytes 1376288 | tf_op jit(solution)/shard_map/all_to_all | solution.py:353
  123.1 4.9 %grad_pre.1 = bf16[8,336,128]{2,1,0:T(8,128)(2,1)} custom-call(s32[8,7]{1,0:T(8,128)S(1)} %copy-done.24, s32[8,7]{1,0:T(8,128)S(1)} %copy-done.22, f32[8,336,128]{2,1,0:T(8,128)} %all-to-all-done.4.recv, f32[7,96,128]{2,1,0:T(8,128)S(1)} %fusion.2.slope), custom_call_target="tpu_custom_call" | custom-call | tf_op jit(solution)/shard_map/grad_pre/pallas_call | solution.py:366
  128.0 4.2 %all-to-all-start.5 = ((bf16[8,336,128]{2,1,0:T(8,128)(2,1)}), bf16[8,336,128]{2,1,0:T(8,128)(2,1)}, u32[]{:S(2)}, u32[]{:S(2)}) async-start(bf16[8,336,128]{2,1,0:T(8,128)(2,1)} %grad_pre.1), calls=%async_computation.5 | async-start | bytes 1376256 | tf_op jit(solution)/shard_map/all_to_all | solution.py:375
  136.3 4.1 %collective-permute-done.14 = bf16[192,512]{1,0:T(8,128)(2,1)S(1)} collective-permute-done((bf16[192,512]{1,0:T(8,128)(2,1)S(1)}, bf16[192,512]{1,0:T(8,128)(2,1)S(1)}, u32[]{:S(2)}, u32[]{:S(2)}) %collective-permute-start.14) | collective-permute-done | bytes 196640 | tf_op jit(solution)/shard_map/ppermute | solution.py:235
  145.6 4.4 %grad_in.1 = (bf16[768,512]{1,0:T(8,128)(2,1)}, bf16[768,1024]{1,0:T(8,128)(2,1)}) custom-call(bf16[8,336,128]{2,1,0:T(8,128)(2,1)} %all-to-all-done.5.h, bf16[1024,512]{1,0:T(8,128)(2,1)S(1)} %copy-done.3), custom_call_target="tpu_custom_call" | custom-call | tf_op jit(solution)/shard_map/grad_in/pallas_call | solution.py:391
  149.9 5.9 %all-to-all-start.6 = ((bf16[4,192,1024]{2,1,0:T(8,128)(2,1)}), bf16[4,192,1024]{2,1,0:T(8,128)(2,1)}, u32[]{:S(2)}, u32[]{:S(2)}) async-start(bf16[4,192,1024]{2,1,0:T(8,128)(2,1)} %bitcast.29), calls=%async_computation.6 | async-start | bytes 3145728 | tf_op jit(solution)/shard_map/all_to_all | solution.py:400
  163.9 3.1 %collective-permute-start.19 = (bf16[24,1024]{1,0:T(8,128)(2,1)}, bf16[24,1024]{1,0:T(8,128)(2,1)S(1)}, u32[]{:S(2)}, u32[]{:S(2)}) collective-permute-start(bf16[24,1024]{1,0:T(8,128)(2,1)} %get-tuple-element.44), channel_id=1, source_target_pairs={{0,32},{8,40},{16,48},{24,56},{32,0},{40,8},{48,16},{56,24},{1,33}... | collective-permute-start | bytes 147464 | tf_op jit(solution)/shard_map/ppermute | solution.py:235
  174.0 3.2 %collective-permute-done.21 = bf16[24,1024]{1,0:T(8,128)(2,1)S(1)} collective-permute-done((bf16[24,1024]{1,0:T(8,128)(2,1)}, bf16[24,1024]{1,0:T(8,128)(2,1)S(1)}, u32[]{:S(2)}, u32[]{:S(2)}) %collective-permute-start.21) | collective-permute-done | bytes 49184 | tf_op jit(solution)/shard_map/ppermute | solution.py:235
  180.4 4.1 %all-to-all-start.7 = ((bf16[8,24,1024]{2,1,0:T(8,128)(2,1)}), bf16[8,24,1024]{2,1,0:T(8,128)(2,1)}, u32[]{:S(2)}, u32[]{:S(2)}) async-start(bf16[8,24,1024]{2,1,0:T(8,128)(2,1)} %bitcast.30), calls=%async_computation.7 | async-start | bytes 786432 | tf_op jit(solution)/shard_map/all_to_all | solution.py:403
  186.3 3.8 %grad_down.1 = f32[896,1024]{1,0:T(8,128)} custom-call(s32[7]{0:T(128)S(1)} %copy-done.26, s32[14,16]{1,0:T(8,128)S(1)} %dynamic_slice.24.md, bf16[768,512]{1,0:T(8,128)(2,1)S(1)} %copy-done.6, bf16[768,1024]{1,0:T(8,128)(2,1)S(1)} %bitcast.25), custom_call_target="tpu_custom_call" | custom-call | tf_op jit(solution)/shard_map/grad_down/pallas_call | solution.py:405
  190.8 6.6 %grad_up.1 = f32[1024,896]{1,0:T(8,128)} custom-call(s32[14]{0:T(128)S(1)} %fusion.6.su, s32[16,14]{1,0:T(8,128)S(1)} %copy.47.mu, bf16[768,512]{1,0:T(8,128)(2,1)S(1)} %copy-done.7, bf16[768,1024]{1,0:T(8,128)(2,1)S(1)} %bitcast.23), custom_call_target="tpu_custom_call" | custom-call | tf_op jit(solution)/shard_map/grad_up/pallas_call | solution.py:414
  (165 shorter events, 86.3 us)
Async XLA Ops:
  2.2 23.2 %all-to-all-start = ((bf16[8,24,1024]{2,1,0:T(8,128)(2,1)}), bf16[8,24,1024]{2,1,0:T(8,128)(2,1)S(1)}, u32[]{:S(2)}, u32[]{:S(2)}) async-start(bf16[8,24,1024]{2,1,0:T(8,128)(2,1)} %broadcast_in_dim.33), calls=%async_computation | async-start | bytes 786432 | tf_op jit(solution)/shard_map/all_to_all | solution.py:226
  26.7 23.4 %all-to-all-start.1 = ((bf16[4,8,24,1024]{3,2,1,0:T(8,128)(2,1)}), bf16[4,8,24,1024]{3,2,1,0:T(8,128)(2,1)S(1)}, u32[]{:S(2)}, u32[]{:S(2)}) async-start(bf16[4,8,24,1024]{3,2,1,0:T(8,128)(2,1)} %broadcast_in_dim.34), calls=%async_computation.1 | async-start | bytes 3145728 | tf_op jit(solution)/shard_map/all_to_all | solution.py:274
  35.4 7.0 %collective-permute-start.4 = (bf16[4,24,1024]{2,1,0:T(8,128)(2,1)S(1)}, bf16[4,24,1024]{2,1,0:T(8,128)(2,1)S(1)}, u32[]{:S(2)}, u32[]{:S(2)}) collective-permute-start(bf16[4,24,1024]{2,1,0:T(8,128)(2,1)S(1)} %pad_maximum_fusion.own), channel_id=1, source_target_pairs={{0,8},{8,16},{16,24},{24,32},{32,40},{40,48},{48,56},{56,0},{1,9},... | collective-permute-start | bytes 589832 | tf_op jit(solution)/shard_map/ppermute | solution.py:235
  41.1 11.9 %collective-permute-start.7 = (bf16[4,24,1024]{2,1,0:T(8,128)(2,1)S(1)}, bf16[4,24,1024]{2,1,0:T(8,128)(2,1)S(1)}, u32[]{:S(2)}, u32[]{:S(2)}) collective-permute-start(bf16[4,24,1024]{2,1,0:T(8,128)(2,1)S(1)} %collective-permute-done.5.refs_1_), channel_id=1, source_target_pairs={{0,56},{8,0},{16,8},{24,16},{32,24},{40,32},{48,40},{56,48},{1,57}... | collective-permute-start | bytes 589832 | tf_op jit(solution)/shard_map/ppermute | solution.py:235
  42.4 10.6 %collective-permute-start.6 = (bf16[4,24,1024]{2,1,0:T(8,128)(2,1)S(1)}, bf16[4,24,1024]{2,1,0:T(8,128)(2,1)}, u32[]{:S(2)}, u32[]{:S(2)}) collective-permute-start(bf16[4,24,1024]{2,1,0:T(8,128)(2,1)S(1)} %collective-permute-done.4.refs_0_), channel_id=1, source_target_pairs={{0,8},{8,16},{16,24},{24,32},{32,40},{40,48},{48,56},{56,0},{1,9},... | collective-permute-start | bytes 589832 | tf_op jit(solution)/shard_map/ppermute | solution.py:235
  53.6 23.8 %all-to-all-start.2 = ((f32[8,336,128]{2,1,0:T(8,128)}), f32[8,336,128]{2,1,0:T(8,128)S(1)}, u32[]{:S(2)}, u32[]{:S(2)}) async-start(f32[8,336,128]{2,1,0:T(8,128)} %pre.1), calls=%async_computation.2 | async-start | bytes 2752512 | tf_op jit(solution)/shard_map/all_to_all | solution.py:341
  57.9 7.5 %collective-permute-start.9 = (bf16[4,24,1024]{2,1,0:T(8,128)(2,1)}, bf16[4,24,1024]{2,1,0:T(8,128)(2,1)S(1)}, u32[]{:S(2)}, u32[]{:S(2)}) collective-permute-start(bf16[4,24,1024]{2,1,0:T(8,128)(2,1)} %copy-done.19), channel_id=1, source_target_pairs={{0,56},{8,0},{16,8},{24,16},{32,24},{40,32},{48,40},{56,48},{1,57}... | collective-permute-start | bytes 589832 | tf_op jit(solution)/shard_map/ppermute | solution.py:235
  59.3 9.4 %collective-permute-start.8 = (bf16[4,24,1024]{2,1,0:T(8,128)(2,1)}, bf16[4,24,1024]{2,1,0:T(8,128)(2,1)S(1)}, u32[]{:S(2)}, u32[]{:S(2)}) collective-permute-start(bf16[4,24,1024]{2,1,0:T(8,128)(2,1)} %collective-permute-done.6.refs_2_), channel_id=1, source_target_pairs={{0,8},{8,16},{16,24},{24,32},{32,40},{40,48},{48,56},{56,0},{1,9},... | collective-permute-start | bytes 589832 | tf_op jit(solution)/shard_map/ppermute | solution.py:235
  69.4 6.1 %collective-permute-start.10 = (bf16[4,24,512]{2,1,0:T(8,128)(2,1)}, bf16[4,24,512]{2,1,0:T(8,128)(2,1)}, u32[]{:S(2)}, u32[]{:S(2)}) collective-permute-start(bf16[4,24,512]{2,1,0:T(8,128)(2,1)} %slice.26), channel_id=1, source_target_pairs={{0,8},{8,16},{16,24},{24,32},{32,40},{40,48},{48,56},{56,0},{1,9},... | collective-permute-start | bytes 294920 | tf_op jit(solution)/shard_map/ppermute | solution.py:235
  83.0 16.3 %all-to-all-start.3 = ((bf16[8,336,128]{2,1,0:T(8,128)(2,1)}), bf16[8,336,128]{2,1,0:T(8,128)(2,1)}, u32[]{:S(2)}, u32[]{:S(2)}) async-start(bf16[8,336,128]{2,1,0:T(8,128)(2,1)} %get-tuple-element.34), calls=%async_computation.3 | async-start | bytes 1376256 | tf_op jit(solution)/shard_map/all_to_all | solution.py:352
  99.4 23.8 %all-to-all-start.4 = ((f32[8,336,128]{2,1,0:T(8,128)}), f32[8,336,128]{2,1,0:T(8,128)}, u32[]{:S(2)}, u32[]{:S(2)}) async-start(f32[8,336,128]{2,1,0:T(8,128)} %grad_act.1), calls=%async_computation.4 | async-start | bytes 2752512 | tf_op jit(solution)/shard_map/all_to_all | solution.py:353
  108.3 19.8 %collective-permute-start.12 = (bf16[192,1536]{1,0:T(8,128)(2,1)}, bf16[192,1536]{1,0:T(8,128)(2,1)}, u32[]{:S(2)}, u32[]{:S(2)}) collective-permute-start(bf16[192,1536]{1,0:T(8,128)(2,1)} %get-tuple-element.38), channel_id=1, source_target_pairs={{0,64},{64,128},{128,192},{192,0},{1,65},{65,129},{129,193},{193,1... | collective-permute-start | bytes 1769480 | tf_op jit(solution)/shard_map/ppermute | solution.py:235
  108.5 19.5 %collective-permute-start.13 = (bf16[192,1536]{1,0:T(8,128)(2,1)}, bf16[192,1536]{1,0:T(8,128)(2,1)}, u32[]{:S(2)}, u32[]{:S(2)}) collective-permute-start(bf16[192,1536]{1,0:T(8,128)(2,1)} %get-tuple-element.39), channel_id=1, source_target_pairs={{0,192},{64,0},{128,64},{192,128},{1,193},{65,1},{129,65},{193,129... | collective-permute-start | bytes 1769480 | tf_op jit(solution)/shard_map/ppermute | solution.py:235
  128.0 16.3 %all-to-all-start.5 = ((bf16[8,336,128]{2,1,0:T(8,128)(2,1)}), bf16[8,336,128]{2,1,0:T(8,128)(2,1)}, u32[]{:S(2)}, u32[]{:S(2)}) async-start(bf16[8,336,128]{2,1,0:T(8,128)(2,1)} %grad_pre.1), calls=%async_computation.5 | async-start | bytes 1376256 | tf_op jit(solution)/shard_map/all_to_all | solution.py:375
  133.2 7.3 %collective-permute-start.14 = (bf16[192,512]{1,0:T(8,128)(2,1)S(1)}, bf16[192,512]{1,0:T(8,128)(2,1)S(1)}, u32[]{:S(2)}, u32[]{:S(2)}) collective-permute-start(bf16[192,512]{1,0:T(8,128)(2,1)S(1)} %slice.28), channel_id=1, source_target_pairs={{0,64},{64,128},{128,192},{192,0},{1,65},{65,129},{129,193},{193,1... | collective-permute-start | bytes 589832 | tf_op jit(solution)/shard_map/ppermute | solution.py:235
  134.5 7.0 %collective-permute-start.15 = (bf16[192,512]{1,0:T(8,128)(2,1)S(1)}, bf16[192,512]{1,0:T(8,128)(2,1)S(1)}, u32[]{:S(2)}, u32[]{:S(2)}) collective-permute-start(bf16[192,512]{1,0:T(8,128)(2,1)S(1)} %slice.29), channel_id=1, source_target_pairs={{0,192},{64,0},{128,64},{192,128},{1,193},{65,1},{129,65},{193,129... | collective-permute-start | bytes 589832 | tf_op jit(solution)/shard_map/ppermute | solution.py:235
  149.9 27.8 %all-to-all-start.6 = ((bf16[4,192,1024]{2,1,0:T(8,128)(2,1)}), bf16[4,192,1024]{2,1,0:T(8,128)(2,1)}, u32[]{:S(2)}, u32[]{:S(2)}) async-start(bf16[4,192,1024]{2,1,0:T(8,128)(2,1)} %bitcast.29), calls=%async_computation.6 | async-start | bytes 3145728 | tf_op jit(solution)/shard_map/all_to_all | solution.py:400
  160.5 9.2 %collective-permute-start.16 = (bf16[24,1024]{1,0:T(8,128)(2,1)}, bf16[24,1024]{1,0:T(8,128)(2,1)S(1)}, u32[]{:S(2)}, u32[]{:S(2)}) collective-permute-start(bf16[24,1024]{1,0:T(8,128)(2,1)} %get-tuple-element.41), channel_id=1, source_target_pairs={{0,8},{8,16},{16,24},{24,32},{32,40},{40,48},{48,56},{56,0},{1,9},... | collective-permute-start | bytes 147464 | tf_op jit(solution)/shard_map/ppermute | solution.py:235
  160.6 11.9 %collective-permute-start.17 = (bf16[24,1024]{1,0:T(8,128)(2,1)}, bf16[24,1024]{1,0:T(8,128)(2,1)S(1)}, u32[]{:S(2)}, u32[]{:S(2)}) collective-permute-start(bf16[24,1024]{1,0:T(8,128)(2,1)} %get-tuple-element.42), channel_id=1, source_target_pairs={{0,16},{8,24},{16,32},{24,40},{32,48},{40,56},{48,0},{56,8},{1,17}... | collective-permute-start | bytes 147464 | tf_op jit(solution)/shard_map/ppermute | solution.py:235
  161.9 12.0 %collective-permute-start.18 = (bf16[24,1024]{1,0:T(8,128)(2,1)}, bf16[24,1024]{1,0:T(8,128)(2,1)S(1)}, u32[]{:S(2)}, u32[]{:S(2)}) collective-permute-start(bf16[24,1024]{1,0:T(8,128)(2,1)} %get-tuple-element.43), channel_id=1, source_target_pairs={{0,24},{8,32},{16,40},{24,48},{32,56},{40,0},{48,8},{56,16},{1,25}... | collective-permute-start | bytes 147464 | tf_op jit(solution)/shard_map/ppermute | solution.py:235
  163.9 10.0 %collective-permute-start.19 = (bf16[24,1024]{1,0:T(8,128)(2,1)}, bf16[24,1024]{1,0:T(8,128)(2,1)S(1)}, u32[]{:S(2)}, u32[]{:S(2)}) collective-permute-start(bf16[24,1024]{1,0:T(8,128)(2,1)} %get-tuple-element.44), channel_id=1, source_target_pairs={{0,32},{8,40},{16,48},{24,56},{32,0},{40,8},{48,16},{56,24},{1,33}... | collective-permute-start | bytes 147464 | tf_op jit(solution)/shard_map/ppermute | solution.py:235
  167.1 6.9 %collective-permute-start.20 = (bf16[24,1024]{1,0:T(8,128)(2,1)}, bf16[24,1024]{1,0:T(8,128)(2,1)S(1)}, u32[]{:S(2)}, u32[]{:S(2)}) collective-permute-start(bf16[24,1024]{1,0:T(8,128)(2,1)} %get-tuple-element.45), channel_id=1, source_target_pairs={{0,40},{8,48},{16,56},{24,0},{32,8},{40,16},{48,24},{56,32},{1,41}... | collective-permute-start | bytes 147464 | tf_op jit(solution)/shard_map/ppermute | solution.py:235
  169.8 7.4 %collective-permute-start.21 = (bf16[24,1024]{1,0:T(8,128)(2,1)}, bf16[24,1024]{1,0:T(8,128)(2,1)S(1)}, u32[]{:S(2)}, u32[]{:S(2)}) collective-permute-start(bf16[24,1024]{1,0:T(8,128)(2,1)} %get-tuple-element.46), channel_id=1, source_target_pairs={{0,48},{8,56},{16,0},{24,8},{32,16},{40,24},{48,32},{56,40},{1,49}... | collective-permute-start | bytes 147464 | tf_op jit(solution)/shard_map/ppermute | solution.py:235
  180.4 18.2 %all-to-all-start.7 = ((bf16[8,24,1024]{2,1,0:T(8,128)(2,1)}), bf16[8,24,1024]{2,1,0:T(8,128)(2,1)}, u32[]{:S(2)}, u32[]{:S(2)}) async-start(bf16[8,24,1024]{2,1,0:T(8,128)(2,1)} %bitcast.30), calls=%async_computation.7 | async-start | bytes 786432 | tf_op jit(solution)/shard_map/all_to_all | solution.py:403
  (45 other events, 238.7 us)

commit v4 on v3

--- a/solution.py
+++ b/solution.py
@@ -175,6 +175,13 @@
         far = jnp.concatenate([low[z], high[z]], axis=-1).astype(F32)
         total = own[z].astype(F32) + fwd[z, :, 0:n].astype(F32) + back[z, :, 0:n].astype(F32) + far
         out[...] = total.astype(out.dtype)
+
+
+def sum_kernel(parts, out):
+    total = parts[0].astype(F32)
+    for k in range(1, parts.shape[0]):
+        total += parts[k].astype(F32)
+    out[...] = total.astype(out.dtype)
 
 
 def grad_in_kernel(chunk, h, w, hidden, out):
@@ -399,9 +406,24 @@
     )(once_there(grad_pre_parts, low, high), wuc)
     part = lax.all_to_all(part.reshape(ny, nz * tokens, feat), "y", 0, 0)
     part = once_there(part, *moved_z)
-    part = part.astype(F32).sum(axis=0).astype(BF)
+    part = pl.pallas_call(
+        sum_kernel,
+        out_shape=hbm((rows // ny, feat), BF),
+        grid=(4,),
+        in_specs=[pl.BlockSpec((ny, rows // ny // 4, feat), lambda i: (0, i, 0))],
+        out_specs=pl.BlockSpec((rows // ny // 4, feat), lambda i: (i, 0)),
+        compiler_params=params(12),
+        name="sum_y",
+    )(part)
     part = lax.all_to_all(part.reshape(nz, tokens, feat), "z", 0, 0)
-    grad_input = part.astype(F32).sum(axis=0)
+    grad_input = pl.pallas_call(
+        sum_kernel,
+        out_shape=jax.ShapeDtypeStruct((tokens, feat), F32),
+        in_specs=[VMEM],
+        out_specs=VMEM,
+        compiler_params=params(8),
+        name="sum_z",
+    )(part)
     grad_down = pl.pallas_call(
         grad_down_kernel,
         out_shape=jax.ShapeDtypeStruct((hid, feat), F32),

time: 202 us -> 202 us (level)
  other arithmetic: 9.04 us -> 4.79 us
  Pallas kernels: 40.6 us -> 44.8 us
    reduce_sum x2 -> x0, other arithmetic: 4.26 us -> none  [the longest x1 2.56 us: on_device(): part = part.astype(F32).sum(axis=0).astype(BF)]
    pallas_call x0 -> x2, Pallas kernels: none -> 4.12 us  [the longest x1 3.43 us: on_device(): pl.pallas_call(sum_kernel, out_shape=hbm((rows // ny, feat), BF), grid=(4...]
    unnamed x77 -> x97, local copies, waits for them, and re-layouts: 16.2 us -> 16.9 us
  transfers between devices with their start and end apart: 31 -> 31, of which waited for: 18 -> 18; matrix products, arithmetic and copies ran while one was open for 7% -> 8% of each run, Pallas kernels for 16% -> 16%
where the time goes in v4:
time: 202 us; the launch traced here: 200 us
  starting transfers between devices  71.1 us (35%)
  waiting for transfers between devices  48.6 us (24%)
  Pallas kernels  44.8 us (22%)
  local copies, waits for them, and re-layouts  30 us (15%)
  other arithmetic  4.79 us (2%)
    ppermute x23, starting transfers between devices, shift(): return lax.ppermute(a, axis, [(i, (i + by) % n) for i in range(n)])  30.5 us
    ppermute x23, waiting for transfers between devices, shift(): return lax.ppermute(a, axis, [(i, (i + by) % n) for i in range(n)])  25.9 us
    unnamed x97, local copies, waits for them, and re-layouts  16.9 us
    all_to_all x1, waiting for transfers between devices, on_device(): grad_parts = lax.all_to_all(once_there(grad_share, act_parts), COL, 0, 0)  11.7 us
    all_to_all x1, starting transfers between devices, gather(): return lax.all_to_all(copies_of(a, axis), axis, 0, 0)  8.47 us
    pallas_call x1, Pallas kernels, on_device(): pl.pallas_call(grad_up_kernel, out_shape=jax.ShapeDtypeStruct((feat, hid)...  6.6 us
    pallas_call x2, Pallas kernels, share(): pl.pallas_call(functools.partial(share_kernel, transposed, chunk), out_sh...  6 us
    all_to_all x1, starting transfers between devices, on_device(): part = lax.all_to_all(part.reshape(ny, nz * tokens, feat), 'y', 0, 0)  5.91 us
  transfers between devices with their start and end apart: 31, of which 18 were waited for; matrix products, arithmetic and copies ran while one was open for 8% of the time, Pallas kernels for 16%

profile of v4, /device:TPU:8, one launch (start us, length us, event | category | flops | bytes accessed | tf_op | source)
XLA Modules:
  0.0 200.3 jit_solution(10527367579779790497)
XLA Ops:
  2.2 8.5 %all-to-all-start = ((bf16[8,24,1024]{2,1,0:T(8,128)(2,1)}), bf16[8,24,1024]{2,1,0:T(8,128)(2,1)S(1)}, u32[]{:S(2)}, u32[]{:S(2)}) async-start(bf16[8,24,1024]{2,1,0:T(8,128)(2,1)} %broadcast_in_dim.33), calls=%async_computation | async-start | bytes 786432 | tf_op jit(solution)/shard_map/all_to_all | solution.py:233
  21.2 4.1 %all-to-all-done = bf16[8,24,1024]{2,1,0:T(8,128)(2,1)S(1)} async-done(((bf16[8,24,1024]{2,1,0:T(8,128)(2,1)}), bf16[8,24,1024]{2,1,0:T(8,128)(2,1)S(1)}, u32[]{:S(2)}, u32[]{:S(2)}) %all-to-all-start) | async-done | bytes 393248 | tf_op jit(solution)/shard_map/all_to_all | solution.py:233
  26.7 4.9 %all-to-all-start.1 = ((bf16[4,8,24,1024]{3,2,1,0:T(8,128)(2,1)}), bf16[4,8,24,1024]{3,2,1,0:T(8,128)(2,1)S(1)}, u32[]{:S(2)}, u32[]{:S(2)}) async-start(bf16[4,8,24,1024]{3,2,1,0:T(8,128)(2,1)} %broadcast_in_dim.34), calls=%async_computation.1 | async-start | bytes 3145728 | tf_op jit(solution)/shard_map/all_to_all | solution.py:281
  37.4 3.6 %collective-permute-done.5.refs_1_ = bf16[4,24,1024]{2,1,0:T(8,128)(2,1)S(1)} collective-permute-done((bf16[4,24,1024]{2,1,0:T(8,128)(2,1)S(1)}, bf16[4,24,1024]{2,1,0:T(8,128)(2,1)S(1)}, u32[]{:S(2)}, u32[]{:S(2)}) %collective-permute-start.5) | collective-permute-done | bytes 196640 | tf_op jit(solution)/shard_map/ppermute | solution.py:242
  46.0 3.0 %prep_up.1.w = bf16[1024,512]{1,0:T(8,128)(2,1)S(1)} custom-call(s32[7]{0:T(128)S(1)} %dynamic-slice_reduce_fusion.tu, s32[16,14]{1,0:T(8,128)S(1)} %copy.47.mu, bf16[1024,896]{1,0:T(8,128)(2,1)S(1)} %copy-done.4), custom_call_target="tpu_custom_call" | custom-call | tf_op jit(solution)/shard_map/prep_up/pallas_call | solution.py:314
  53.7 4.3 %all-to-all-start.2 = ((f32[8,336,128]{2,1,0:T(8,128)}), f32[8,336,128]{2,1,0:T(8,128)S(1)}, u32[]{:S(2)}, u32[]{:S(2)}) async-start(f32[8,336,128]{2,1,0:T(8,128)} %pre.1), calls=%async_computation.2 | async-start | bytes 2752512 | tf_op jit(solution)/shard_map/all_to_all | solution.py:348
  60.0 5.5 %collective-permute-done.9.refs_5_ = bf16[4,24,1024]{2,1,0:T(8,128)(2,1)S(1)} collective-permute-done((bf16[4,24,1024]{2,1,0:T(8,128)(2,1)}, bf16[4,24,1024]{2,1,0:T(8,128)(2,1)S(1)}, u32[]{:S(2)}, u32[]{:S(2)}) %collective-permute-start.9) | collective-permute-done | bytes 196640 | tf_op jit(solution)/shard_map/ppermute | solution.py:242
  72.2 3.5 %collective-permute-done.10.refs_6_ = bf16[4,24,512]{2,1,0:T(8,128)(2,1)} collective-permute-done((bf16[4,24,512]{2,1,0:T(8,128)(2,1)}, bf16[4,24,512]{2,1,0:T(8,128)(2,1)}, u32[]{:S(2)}, u32[]{:S(2)}) %collective-permute-start.10) | collective-permute-done | bytes 98336 | tf_op jit(solution)/shard_map/ppermute | solution.py:242
  78.8 4.3 %act.1 = (f32[7,96,128]{2,1,0:T(8,128)}, bf16[8,336,128]{2,1,0:T(8,128)(2,1)}) custom-call(s32[8,7]{1,0:T(8,128)S(1)} %copy-done.23, s32[8,7]{1,0:T(8,128)S(1)} %copy-done.21, f32[8,336,128]{2,1,0:T(8,128)S(1)} %all-to-all-done.2.recv), custom_call_target="tpu_custom_call" | custom-call | tf_op jit(solution)/shard_map/act/pallas_call | solution.py:349
  83.1 4.4 %all-to-all-start.3 = ((bf16[8,336,128]{2,1,0:T(8,128)(2,1)}), bf16[8,336,128]{2,1,0:T(8,128)(2,1)}, u32[]{:S(2)}, u32[]{:S(2)}) async-start(bf16[8,336,128]{2,1,0:T(8,128)(2,1)} %get-tuple-element.34), calls=%async_computation.3 | async-start | bytes 1376256 | tf_op jit(solution)/shard_map/all_to_all | solution.py:359
  93.9 3.2 %grad_act.1 = f32[8,336,128]{2,1,0:T(8,128)} custom-call(bf16[768,1024]{1,0:T(8,128)(2,1)S(1)} %bitcast.24, bf16[512,1024]{1,0:T(8,128)(2,1)S(1)} %prep_down.1.w), custom_call_target="tpu_custom_call" | custom-call | tf_op jit(solution)/shard_map/grad_act/pallas_call | solution.py:336
  99.4 4.3 %all-to-all-start.4 = ((f32[8,336,128]{2,1,0:T(8,128)}), f32[8,336,128]{2,1,0:T(8,128)}, u32[]{:S(2)}, u32[]{:S(2)}) async-start(f32[8,336,128]{2,1,0:T(8,128)} %grad_act.1), calls=%async_computation.4 | async-start | bytes 2752512 | tf_op jit(solution)/shard_map/all_to_all | solution.py:360
  104.9 3.4 %out.1 = (bf16[768,512]{1,0:T(8,128)(2,1)}, bf16[192,1024]{1,0:T(8,128)(2,1)}, bf16[192,1536]{1,0:T(8,128)(2,1)}, bf16[192,1536]{1,0:T(8,128)(2,1)}) custom-call(s32[2]{0:T(128)S(1)} %copy-done.28, bf16[8,336,128]{2,1,0:T(8,128)(2,1)} %all-to-all-done.3.h, bf16[512,1024]{1,0:T(8,128)(2,1)S(1)} %copy-done.1), custom_call_target="tpu_custom_call" | custom-call | tf_op jit(solution)/shard_map/out/pallas_call | solution.py:362
  111.5 11.7 %all-to-all-done.4.recv = f32[8,336,128]{2,1,0:T(8,128)} async-done(((f32[8,336,128]{2,1,0:T(8,128)}), f32[8,336,128]{2,1,0:T(8,128)}, u32[]{:S(2)}, u32[]{:S(2)}) %all-to-all-start.4) | async-done | bytes 1376288 | tf_op jit(solution)/shard_map/all_to_all | solution.py:360
  123.2 4.9 %grad_pre.1 = bf16[8,336,128]{2,1,0:T(8,128)(2,1)} custom-call(s32[8,7]{1,0:T(8,128)S(1)} %copy-done.24, s32[8,7]{1,0:T(8,128)S(1)} %copy-done.22, f32[8,336,128]{2,1,0:T(8,128)} %all-to-all-done.4.recv, f32[7,96,128]{2,1,0:T(8,128)S(1)} %fusion.2.slope), custom_call_target="tpu_custom_call" | custom-call | tf_op jit(solution)/shard_map/grad_pre/pallas_call | solution.py:373
  128.1 4.2 %all-to-all-start.5 = ((bf16[8,336,128]{2,1,0:T(8,128)(2,1)}), bf16[8,336,128]{2,1,0:T(8,128)(2,1)}, u32[]{:S(2)}, u32[]{:S(2)}) async-start(bf16[8,336,128]{2,1,0:T(8,128)(2,1)} %grad_pre.1), calls=%async_computation.5 | async-start | bytes 1376256 | tf_op jit(solution)/shard_map/all_to_all | solution.py:382
  136.4 4.1 %collective-permute-done.14 = bf16[192,512]{1,0:T(8,128)(2,1)S(1)} collective-permute-done((bf16[192,512]{1,0:T(8,128)(2,1)S(1)}, bf16[192,512]{1,0:T(8,128)(2,1)S(1)}, u32[]{:S(2)}, u32[]{:S(2)}) %collective-permute-start.14) | collective-permute-done | bytes 196640 | tf_op jit(solution)/shard_map/ppermute | solution.py:242
  145.6 4.4 %grad_in.1 = (bf16[768,512]{1,0:T(8,128)(2,1)}, bf16[768,1024]{1,0:T(8,128)(2,1)}) custom-call(bf16[8,336,128]{2,1,0:T(8,128)(2,1)} %all-to-all-done.5.h, bf16[1024,512]{1,0:T(8,128)(2,1)S(1)} %copy-done.3), custom_call_target="tpu_custom_call" | custom-call | tf_op jit(solution)/shard_map/grad_in/pallas_call | solution.py:398
  150.0 5.9 %all-to-all-start.6 = ((bf16[4,192,1024]{2,1,0:T(8,128)(2,1)}), bf16[4,192,1024]{2,1,0:T(8,128)(2,1)}, u32[]{:S(2)}, u32[]{:S(2)}) async-start(bf16[4,192,1024]{2,1,0:T(8,128)(2,1)} %bitcast.29), calls=%async_computation.6 | async-start | bytes 3145728 | tf_op jit(solution)/shard_map/all_to_all | solution.py:407
  164.0 3.1 %collective-permute-start.19 = (bf16[24,1024]{1,0:T(8,128)(2,1)}, bf16[24,1024]{1,0:T(8,128)(2,1)S(1)}, u32[]{:S(2)}, u32[]{:S(2)}) collective-permute-start(bf16[24,1024]{1,0:T(8,128)(2,1)} %get-tuple-element.44), channel_id=1, source_target_pairs={{0,32},{8,40},{16,48},{24,56},{32,0},{40,8},{48,16},{56,24},{1,33}... | collective-permute-start | bytes 147464 | tf_op jit(solution)/shard_map/ppermute | solution.py:242
  177.9 3.4 %sum_y.1 = bf16[192,1024]{1,0:T(8,128)(2,1)} custom-call(bf16[4,192,1024]{2,1,0:T(8,128)(2,1)} %all-to-all-done.6.parts), custom_call_target="tpu_custom_call" | custom-call | tf_op jit(solution)/shard_map/sum_y/pallas_call | solution.py:409
  181.3 4.1 %all-to-all-start.7 = ((bf16[8,24,1024]{2,1,0:T(8,128)(2,1)}), bf16[8,24,1024]{2,1,0:T(8,128)(2,1)S(1)}, u32[]{:S(2)}, u32[]{:S(2)}) async-start(bf16[8,24,1024]{2,1,0:T(8,128)(2,1)} %bitcast.30), calls=%async_computation.7 | async-start | bytes 786432 | tf_op jit(solution)/shard_map/all_to_all | solution.py:418
  188.0 3.8 %grad_down.1 = f32[896,1024]{1,0:T(8,128)} custom-call(s32[7]{0:T(128)S(1)} %copy-done.26, s32[14,16]{1,0:T(8,128)S(1)} %dynamic_slice.24.md, bf16[768,512]{1,0:T(8,128)(2,1)S(1)} %copy-done.6, bf16[768,1024]{1,0:T(8,128)(2,1)S(1)} %bitcast.25), custom_call_target="tpu_custom_call" | custom-call | tf_op jit(solution)/shard_map/grad_down/pallas_call | solution.py:427
  192.6 6.6 %grad_up.1 = f32[1024,896]{1,0:T(8,128)} custom-call(s32[14]{0:T(128)S(1)} %fusion.6.su, s32[16,14]{1,0:T(8,128)S(1)} %copy.47.mu, bf16[768,512]{1,0:T(8,128)(2,1)S(1)} %copy-done.7, bf16[768,1024]{1,0:T(8,128)(2,1)S(1)} %bitcast.23), custom_call_target="tpu_custom_call" | custom-call | tf_op jit(solution)/shard_map/grad_up/pallas_call | solution.py:436
  (185 shorter events, 86.0 us)
Async XLA Ops:
  2.2 23.2 %all-to-all-start = ((bf16[8,24,1024]{2,1,0:T(8,128)(2,1)}), bf16[8,24,1024]{2,1,0:T(8,128)(2,1)S(1)}, u32[]{:S(2)}, u32[]{:S(2)}) async-start(bf16[8,24,1024]{2,1,0:T(8,128)(2,1)} %broadcast_in_dim.33), calls=%async_computation | async-start | bytes 786432 | tf_op jit(solution)/shard_map/all_to_all | solution.py:233
  26.7 23.4 %all-to-all-start.1 = ((bf16[4,8,24,1024]{3,2,1,0:T(8,128)(2,1)}), bf16[4,8,24,1024]{3,2,1,0:T(8,128)(2,1)S(1)}, u32[]{:S(2)}, u32[]{:S(2)}) async-start(bf16[4,8,24,1024]{3,2,1,0:T(8,128)(2,1)} %broadcast_in_dim.34), calls=%async_computation.1 | async-start | bytes 3145728 | tf_op jit(solution)/shard_map/all_to_all | solution.py:281
  35.4 7.0 %collective-permute-start.4 = (bf16[4,24,1024]{2,1,0:T(8,128)(2,1)S(1)}, bf16[4,24,1024]{2,1,0:T(8,128)(2,1)S(1)}, u32[]{:S(2)}, u32[]{:S(2)}) collective-permute-start(bf16[4,24,1024]{2,1,0:T(8,128)(2,1)S(1)} %pad_maximum_fusion.own), channel_id=1, source_target_pairs={{0,8},{8,16},{16,24},{24,32},{32,40},{40,48},{48,56},{56,0},{1,9},... | collective-permute-start | bytes 589832 | tf_op jit(solution)/shard_map/ppermute | solution.py:242
  41.1 11.9 %collective-permute-start.7 = (bf16[4,24,1024]{2,1,0:T(8,128)(2,1)S(1)}, bf16[4,24,1024]{2,1,0:T(8,128)(2,1)S(1)}, u32[]{:S(2)}, u32[]{:S(2)}) collective-permute-start(bf16[4,24,1024]{2,1,0:T(8,128)(2,1)S(1)} %collective-permute-done.5.refs_1_), channel_id=1, source_target_pairs={{0,56},{8,0},{16,8},{24,16},{32,24},{40,32},{48,40},{56,48},{1,57}... | collective-permute-start | bytes 589832 | tf_op jit(solution)/shard_map/ppermute | solution.py:242
  42.4 10.6 %collective-permute-start.6 = (bf16[4,24,1024]{2,1,0:T(8,128)(2,1)S(1)}, bf16[4,24,1024]{2,1,0:T(8,128)(2,1)}, u32[]{:S(2)}, u32[]{:S(2)}) collective-permute-start(bf16[4,24,1024]{2,1,0:T(8,128)(2,1)S(1)} %collective-permute-done.4.refs_0_), channel_id=1, source_target_pairs={{0,8},{8,16},{16,24},{24,32},{32,40},{40,48},{48,56},{56,0},{1,9},... | collective-permute-start | bytes 589832 | tf_op jit(solution)/shard_map/ppermute | solution.py:242
  53.7 23.8 %all-to-all-start.2 = ((f32[8,336,128]{2,1,0:T(8,128)}), f32[8,336,128]{2,1,0:T(8,128)S(1)}, u32[]{:S(2)}, u32[]{:S(2)}) async-start(f32[8,336,128]{2,1,0:T(8,128)} %pre.1), calls=%async_computation.2 | async-start | bytes 2752512 | tf_op jit(solution)/shard_map/all_to_all | solution.py:348
  58.0 7.5 %collective-permute-start.9 = (bf16[4,24,1024]{2,1,0:T(8,128)(2,1)}, bf16[4,24,1024]{2,1,0:T(8,128)(2,1)S(1)}, u32[]{:S(2)}, u32[]{:S(2)}) collective-permute-start(bf16[4,24,1024]{2,1,0:T(8,128)(2,1)} %copy-done.19), channel_id=1, source_target_pairs={{0,56},{8,0},{16,8},{24,16},{32,24},{40,32},{48,40},{56,48},{1,57}... | collective-permute-start | bytes 589832 | tf_op jit(solution)/shard_map/ppermute | solution.py:242
  59.4 9.4 %collective-permute-start.8 = (bf16[4,24,1024]{2,1,0:T(8,128)(2,1)}, bf16[4,24,1024]{2,1,0:T(8,128)(2,1)S(1)}, u32[]{:S(2)}, u32[]{:S(2)}) collective-permute-start(bf16[4,24,1024]{2,1,0:T(8,128)(2,1)} %collective-permute-done.6.refs_2_), channel_id=1, source_target_pairs={{0,8},{8,16},{16,24},{24,32},{32,40},{40,48},{48,56},{56,0},{1,9},... | collective-permute-start | bytes 589832 | tf_op jit(solution)/shard_map/ppermute | solution.py:242
  69.5 6.1 %collective-permute-start.10 = (bf16[4,24,512]{2,1,0:T(8,128)(2,1)}, bf16[4,24,512]{2,1,0:T(8,128)(2,1)}, u32[]{:S(2)}, u32[]{:S(2)}) collective-permute-start(bf16[4,24,512]{2,1,0:T(8,128)(2,1)} %slice.26), channel_id=1, source_target_pairs={{0,8},{8,16},{16,24},{24,32},{32,40},{40,48},{48,56},{56,0},{1,9},... | collective-permute-start | bytes 294920 | tf_op jit(solution)/shard_map/ppermute | solution.py:242
  83.1 16.3 %all-to-all-start.3 = ((bf16[8,336,128]{2,1,0:T(8,128)(2,1)}), bf16[8,336,128]{2,1,0:T(8,128)(2,1)}, u32[]{:S(2)}, u32[]{:S(2)}) async-start(bf16[8,336,128]{2,1,0:T(8,128)(2,1)} %get-tuple-element.34), calls=%async_computation.3 | async-start | bytes 1376256 | tf_op jit(solution)/shard_map/all_to_all | solution.py:359
  99.4 23.8 %all-to-all-start.4 = ((f32[8,336,128]{2,1,0:T(8,128)}), f32[8,336,128]{2,1,0:T(8,128)}, u32[]{:S(2)}, u32[]{:S(2)}) async-start(f32[8,336,128]{2,1,0:T(8,128)} %grad_act.1), calls=%async_computation.4 | async-start | bytes 2752512 | tf_op jit(solution)/shard_map/all_to_all | solution.py:360
  108.4 19.7 %collective-permute-start.12 = (bf16[192,1536]{1,0:T(8,128)(2,1)}, bf16[192,1536]{1,0:T(8,128)(2,1)}, u32[]{:S(2)}, u32[]{:S(2)}) collective-permute-start(bf16[192,1536]{1,0:T(8,128)(2,1)} %get-tuple-element.38), channel_id=1, source_target_pairs={{0,64},{64,128},{128,192},{192,0},{1,65},{65,129},{129,193},{193,1... | collective-permute-start | bytes 1769480 | tf_op jit(solution)/shard_map/ppermute | solution.py:242
  108.7 19.4 %collective-permute-start.13 = (bf16[192,1536]{1,0:T(8,128)(2,1)}, bf16[192,1536]{1,0:T(8,128)(2,1)}, u32[]{:S(2)}, u32[]{:S(2)}) collective-permute-start(bf16[192,1536]{1,0:T(8,128)(2,1)} %get-tuple-element.39), channel_id=1, source_target_pairs={{0,192},{64,0},{128,64},{192,128},{1,193},{65,1},{129,65},{193,129... | collective-permute-start | bytes 1769480 | tf_op jit(solution)/shard_map/ppermute | solution.py:242
  128.1 16.3 %all-to-all-start.5 = ((bf16[8,336,128]{2,1,0:T(8,128)(2,1)}), bf16[8,336,128]{2,1,0:T(8,128)(2,1)}, u32[]{:S(2)}, u32[]{:S(2)}) async-start(bf16[8,336,128]{2,1,0:T(8,128)(2,1)} %grad_pre.1), calls=%async_computation.5 | async-start | bytes 1376256 | tf_op jit(solution)/shard_map/all_to_all | solution.py:382
  133.3 7.3 %collective-permute-start.14 = (bf16[192,512]{1,0:T(8,128)(2,1)S(1)}, bf16[192,512]{1,0:T(8,128)(2,1)S(1)}, u32[]{:S(2)}, u32[]{:S(2)}) collective-permute-start(bf16[192,512]{1,0:T(8,128)(2,1)S(1)} %slice.28), channel_id=1, source_target_pairs={{0,64},{64,128},{128,192},{192,0},{1,65},{65,129},{129,193},{193,1... | collective-permute-start | bytes 589832 | tf_op jit(solution)/shard_map/ppermute | solution.py:242
  134.7 7.0 %collective-permute-start.15 = (bf16[192,512]{1,0:T(8,128)(2,1)S(1)}, bf16[192,512]{1,0:T(8,128)(2,1)S(1)}, u32[]{:S(2)}, u32[]{:S(2)}) collective-permute-start(bf16[192,512]{1,0:T(8,128)(2,1)S(1)} %slice.29), channel_id=1, source_target_pairs={{0,192},{64,0},{128,64},{192,128},{1,193},{65,1},{129,65},{193,129... | collective-permute-start | bytes 589832 | tf_op jit(solution)/shard_map/ppermute | solution.py:242
  150.0 27.8 %all-to-all-start.6 = ((bf16[4,192,1024]{2,1,0:T(8,128)(2,1)}), bf16[4,192,1024]{2,1,0:T(8,128)(2,1)}, u32[]{:S(2)}, u32[]{:S(2)}) async-start(bf16[4,192,1024]{2,1,0:T(8,128)(2,1)} %bitcast.29), calls=%async_computation.6 | async-start | bytes 3145728 | tf_op jit(solution)/shard_map/all_to_all | solution.py:407
  160.6 9.3 %collective-permute-start.16 = (bf16[24,1024]{1,0:T(8,128)(2,1)}, bf16[24,1024]{1,0:T(8,128)(2,1)S(1)}, u32[]{:S(2)}, u32[]{:S(2)}) collective-permute-start(bf16[24,1024]{1,0:T(8,128)(2,1)} %get-tuple-element.41), channel_id=1, source_target_pairs={{0,8},{8,16},{16,24},{24,32},{32,40},{40,48},{48,56},{56,0},{1,9},... | collective-permute-start | bytes 147464 | tf_op jit(solution)/shard_map/ppermute | solution.py:242
  160.6 11.9 %collective-permute-start.17 = (bf16[24,1024]{1,0:T(8,128)(2,1)}, bf16[24,1024]{1,0:T(8,128)(2,1)S(1)}, u32[]{:S(2)}, u32[]{:S(2)}) collective-permute-start(bf16[24,1024]{1,0:T(8,128)(2,1)} %get-tuple-element.42), channel_id=1, source_target_pairs={{0,16},{8,24},{16,32},{24,40},{32,48},{40,56},{48,0},{56,8},{1,17}... | collective-permute-start | bytes 147464 | tf_op jit(solution)/shard_map/ppermute | solution.py:242
  162.1 12.0 %collective-permute-start.18 = (bf16[24,1024]{1,0:T(8,128)(2,1)}, bf16[24,1024]{1,0:T(8,128)(2,1)S(1)}, u32[]{:S(2)}, u32[]{:S(2)}) collective-permute-start(bf16[24,1024]{1,0:T(8,128)(2,1)} %get-tuple-element.43), channel_id=1, source_target_pairs={{0,24},{8,32},{16,40},{24,48},{32,56},{40,0},{48,8},{56,16},{1,25}... | collective-permute-start | bytes 147464 | tf_op jit(solution)/shard_map/ppermute | solution.py:242
  164.0 10.1 %collective-permute-start.19 = (bf16[24,1024]{1,0:T(8,128)(2,1)}, bf16[24,1024]{1,0:T(8,128)(2,1)S(1)}, u32[]{:S(2)}, u32[]{:S(2)}) collective-permute-start(bf16[24,1024]{1,0:T(8,128)(2,1)} %get-tuple-element.44), channel_id=1, source_target_pairs={{0,32},{8,40},{16,48},{24,56},{32,0},{40,8},{48,16},{56,24},{1,33}... | collective-permute-start | bytes 147464 | tf_op jit(solution)/shard_map/ppermute | solution.py:242
  167.1 7.0 %collective-permute-start.20 = (bf16[24,1024]{1,0:T(8,128)(2,1)}, bf16[24,1024]{1,0:T(8,128)(2,1)S(1)}, u32[]{:S(2)}, u32[]{:S(2)}) collective-permute-start(bf16[24,1024]{1,0:T(8,128)(2,1)} %get-tuple-element.45), channel_id=1, source_target_pairs={{0,40},{8,48},{16,56},{24,0},{32,8},{40,16},{48,24},{56,32},{1,41}... | collective-permute-start | bytes 147464 | tf_op jit(solution)/shard_map/ppermute | solution.py:242
  169.9 7.0 %collective-permute-start.21 = (bf16[24,1024]{1,0:T(8,128)(2,1)}, bf16[24,1024]{1,0:T(8,128)(2,1)S(1)}, u32[]{:S(2)}, u32[]{:S(2)}) collective-permute-start(bf16[24,1024]{1,0:T(8,128)(2,1)} %get-tuple-element.46), channel_id=1, source_target_pairs={{0,48},{8,56},{16,0},{24,8},{32,16},{40,24},{48,32},{56,40},{1,49}... | collective-permute-start | bytes 147464 | tf_op jit(solution)/shard_map/ppermute | solution.py:242
  181.3 18.3 %all-to-all-start.7 = ((bf16[8,24,1024]{2,1,0:T(8,128)(2,1)}), bf16[8,24,1024]{2,1,0:T(8,128)(2,1)S(1)}, u32[]{:S(2)}, u32[]{:S(2)}) async-start(bf16[8,24,1024]{2,1,0:T(8,128)(2,1)} %bitcast.30), calls=%async_computation.7 | async-start | bytes 786432 | tf_op jit(solution)/shard_map/all_to_all | solution.py:418
  (55 other events, 268.2 us)

commit v5 on v3

--- a/solution.py
+++ b/solution.py
@@ -398,7 +398,7 @@
         name="grad_in",
     )(once_there(grad_pre_parts, low, high), wuc)
     part = lax.all_to_all(part.reshape(ny, nz * tokens, feat), "y", 0, 0)
-    part = once_there(part, *moved_z)
+    part = once_there(part, *moved_z[:5])
     part = part.astype(F32).sum(axis=0).astype(BF)
     part = lax.all_to_all(part.reshape(nz, tokens, feat), "z", 0, 0)
     grad_input = part.astype(F32).sum(axis=0)

time: 202 us -> 207 us (1.025)
  starting transfers between devices: 70.9 us -> 73 us
    unnamed x77 -> x69, local copies, waits for them, and re-layouts: 16.2 us -> 16.2 us
  transfers between devices with their start and end apart: 31 -> 31, of which waited for: 18 -> 21; matrix products, arithmetic and copies ran while one was open for 7% -> 7% of each run, Pallas kernels for 16% -> 16%
where the time goes in v5:
time: 207 us; the launch traced here: 204 us
  starting transfers between devices  73 us (35%)
  waiting for transfers between devices  51.2 us (25%)
  Pallas kernels  40.7 us (20%)
  local copies, waits for them, and re-layouts  29.2 us (14%)
  other arithmetic  9.03 us (4%)
    ppermute x23, starting transfers between devices, shift(): return lax.ppermute(a, axis, [(i, (i + by) % n) for i in range(n)])  31.8 us
    ppermute x23, waiting for transfers between devices, shift(): return lax.ppermute(a, axis, [(i, (i + by) % n) for i in range(n)])  27.3 us
    unnamed x69, local copies, waits for them, and re-layouts  16.2 us
    all_to_all x1, waiting for transfers between devices, on_device(): grad_parts = lax.all_to_all(once_there(grad_share, act_parts), COL, 0, 0)  11.7 us
    all_to_all x1, starting transfers between devices, gather(): return lax.all_to_all(copies_of(a, axis), axis, 0, 0)  8.47 us
    pallas_call x1, Pallas kernels, on_device(): pl.pallas_call(grad_up_kernel, out_shape=jax.ShapeDtypeStruct((feat, hid)...  6.61 us
    pallas_call x2, Pallas kernels, share(): pl.pallas_call(functools.partial(share_kernel, transposed, chunk), out_sh...  6.01 us
    all_to_all x1, starting transfers between devices, on_device(): part = lax.all_to_all(part.reshape(ny, nz * tokens, feat), 'y', 0, 0)  5.9 us
  transfers between devices with their start and end apart: 31, of which 21 were waited for; matrix products, arithmetic and copies ran while one was open for 7% of the time, Pallas kernels for 16%

profile of v5, /device:TPU:8, one launch (start us, length us, event | category | flops | bytes accessed | tf_op | source)
XLA Modules:
  0.0 204.0 jit_solution(8430629088781464446)
XLA Ops:
  2.2 8.5 %all-to-all-start = ((bf16[8,24,1024]{2,1,0:T(8,128)(2,1)}), bf16[8,24,1024]{2,1,0:T(8,128)(2,1)S(1)}, u32[]{:S(2)}, u32[]{:S(2)}) async-start(bf16[8,24,1024]{2,1,0:T(8,128)(2,1)} %broadcast_in_dim.33), calls=%async_computation | async-start | bytes 786432 | tf_op jit(solution)/shard_map/all_to_all | solution.py:226
  21.2 4.1 %all-to-all-done = bf16[8,24,1024]{2,1,0:T(8,128)(2,1)S(1)} async-done(((bf16[8,24,1024]{2,1,0:T(8,128)(2,1)}), bf16[8,24,1024]{2,1,0:T(8,128)(2,1)S(1)}, u32[]{:S(2)}, u32[]{:S(2)}) %all-to-all-start) | async-done | bytes 393248 | tf_op jit(solution)/shard_map/all_to_all | solution.py:226
  26.7 4.9 %all-to-all-start.1 = ((bf16[4,8,24,1024]{3,2,1,0:T(8,128)(2,1)}), bf16[4,8,24,1024]{3,2,1,0:T(8,128)(2,1)S(1)}, u32[]{:S(2)}, u32[]{:S(2)}) async-start(bf16[4,8,24,1024]{3,2,1,0:T(8,128)(2,1)} %broadcast_in_dim.34), calls=%async_computation.1 | async-start | bytes 3145728 | tf_op jit(solution)/shard_map/all_to_all | solution.py:274
  37.4 3.6 %collective-permute-done.5.refs_1_ = bf16[4,24,1024]{2,1,0:T(8,128)(2,1)S(1)} collective-permute-done((bf16[4,24,1024]{2,1,0:T(8,128)(2,1)S(1)}, bf16[4,24,1024]{2,1,0:T(8,128)(2,1)S(1)}, u32[]{:S(2)}, u32[]{:S(2)}) %collective-permute-start.5) | collective-permute-done | bytes 196640 | tf_op jit(solution)/shard_map/ppermute | solution.py:235
  45.9 3.0 %prep_up.1.w = bf16[1024,512]{1,0:T(8,128)(2,1)S(1)} custom-call(s32[7]{0:T(128)S(1)} %dynamic-slice_reduce_fusion.tu, s32[16,14]{1,0:T(8,128)S(1)} %copy.47.mu, bf16[1024,896]{1,0:T(8,128)(2,1)S(1)} %copy-done.4), custom_call_target="tpu_custom_call" | custom-call | tf_op jit(solution)/shard_map/prep_up/pallas_call | solution.py:307
  53.6 4.3 %all-to-all-start.2 = ((f32[8,336,128]{2,1,0:T(8,128)}), f32[8,336,128]{2,1,0:T(8,128)S(1)}, u32[]{:S(2)}, u32[]{:S(2)}) async-start(f32[8,336,128]{2,1,0:T(8,128)} %pre.1), calls=%async_computation.2 | async-start | bytes 2752512 | tf_op jit(solution)/shard_map/all_to_all | solution.py:341
  60.0 5.5 %collective-permute-done.9.refs_5_ = bf16[4,24,1024]{2,1,0:T(8,128)(2,1)S(1)} collective-permute-done((bf16[4,24,1024]{2,1,0:T(8,128)(2,1)}, bf16[4,24,1024]{2,1,0:T(8,128)(2,1)S(1)}, u32[]{:S(2)}, u32[]{:S(2)}) %collective-permute-start.9) | collective-permute-done | bytes 196640 | tf_op jit(solution)/shard_map/ppermute | solution.py:235
  72.1 3.5 %collective-permute-done.10.refs_6_ = bf16[4,24,512]{2,1,0:T(8,128)(2,1)} collective-permute-done((bf16[4,24,512]{2,1,0:T(8,128)(2,1)}, bf16[4,24,512]{2,1,0:T(8,128)(2,1)}, u32[]{:S(2)}, u32[]{:S(2)}) %collective-permute-start.10) | collective-permute-done | bytes 98336 | tf_op jit(solution)/shard_map/ppermute | solution.py:235
  78.8 4.3 %act.1 = (f32[7,96,128]{2,1,0:T(8,128)}, bf16[8,336,128]{2,1,0:T(8,128)(2,1)}) custom-call(s32[8,7]{1,0:T(8,128)S(1)} %copy-done.23, s32[8,7]{1,0:T(8,128)S(1)} %copy-done.21, f32[8,336,128]{2,1,0:T(8,128)S(1)} %all-to-all-done.2.recv), custom_call_target="tpu_custom_call" | custom-call | tf_op jit(solution)/shard_map/act/pallas_call | solution.py:342
  83.1 4.4 %all-to-all-start.3 = ((bf16[8,336,128]{2,1,0:T(8,128)(2,1)}), bf16[8,336,128]{2,1,0:T(8,128)(2,1)}, u32[]{:S(2)}, u32[]{:S(2)}) async-start(bf16[8,336,128]{2,1,0:T(8,128)(2,1)} %get-tuple-element.34), calls=%async_computation.3 | async-start | bytes 1376256 | tf_op jit(solution)/shard_map/all_to_all | solution.py:352
  93.9 3.2 %grad_act.1 = f32[8,336,128]{2,1,0:T(8,128)} custom-call(bf16[768,1024]{1,0:T(8,128)(2,1)S(1)} %bitcast.24, bf16[512,1024]{1,0:T(8,128)(2,1)S(1)} %prep_down.1.w), custom_call_target="tpu_custom_call" | custom-call | tf_op jit(solution)/shard_map/grad_act/pallas_call | solution.py:329
  99.4 4.3 %all-to-all-start.4 = ((f32[8,336,128]{2,1,0:T(8,128)}), f32[8,336,128]{2,1,0:T(8,128)}, u32[]{:S(2)}, u32[]{:S(2)}) async-start(f32[8,336,128]{2,1,0:T(8,128)} %grad_act.1), calls=%async_computation.4 | async-start | bytes 2752512 | tf_op jit(solution)/shard_map/all_to_all | solution.py:353
  104.9 3.4 %out.1 = (bf16[768,512]{1,0:T(8,128)(2,1)}, bf16[192,1024]{1,0:T(8,128)(2,1)}, bf16[192,1536]{1,0:T(8,128)(2,1)}, bf16[192,1536]{1,0:T(8,128)(2,1)}) custom-call(s32[2]{0:T(128)S(1)} %copy-done.28, bf16[8,336,128]{2,1,0:T(8,128)(2,1)} %all-to-all-done.3.h, bf16[512,1024]{1,0:T(8,128)(2,1)S(1)} %copy-done.1), custom_call_target="tpu_custom_call" | custom-call | tf_op jit(solution)/shard_map/out/pallas_call | solution.py:355
  111.5 11.7 %all-to-all-done.4.recv = f32[8,336,128]{2,1,0:T(8,128)} async-done(((f32[8,336,128]{2,1,0:T(8,128)}), f32[8,336,128]{2,1,0:T(8,128)}, u32[]{:S(2)}, u32[]{:S(2)}) %all-to-all-start.4) | async-done | bytes 1376288 | tf_op jit(solution)/shard_map/all_to_all | solution.py:353
  123.2 4.9 %grad_pre.1 = bf16[8,336,128]{2,1,0:T(8,128)(2,1)} custom-call(s32[8,7]{1,0:T(8,128)S(1)} %copy-done.24, s32[8,7]{1,0:T(8,128)S(1)} %copy-done.22, f32[8,336,128]{2,1,0:T(8,128)} %all-to-all-done.4.recv, f32[7,96,128]{2,1,0:T(8,128)S(1)} %fusion.2.slope), custom_call_target="tpu_custom_call" | custom-call | tf_op jit(solution)/shard_map/grad_pre/pallas_call | solution.py:366
  128.1 4.2 %all-to-all-start.5 = ((bf16[8,336,128]{2,1,0:T(8,128)(2,1)}), bf16[8,336,128]{2,1,0:T(8,128)(2,1)}, u32[]{:S(2)}, u32[]{:S(2)}) async-start(bf16[8,336,128]{2,1,0:T(8,128)(2,1)} %grad_pre.1), calls=%async_computation.5 | async-start | bytes 1376256 | tf_op jit(solution)/shard_map/all_to_all | solution.py:375
  136.4 4.1 %collective-permute-done.14 = bf16[192,512]{1,0:T(8,128)(2,1)S(1)} collective-permute-done((bf16[192,512]{1,0:T(8,128)(2,1)S(1)}, bf16[192,512]{1,0:T(8,128)(2,1)S(1)}, u32[]{:S(2)}, u32[]{:S(2)}) %collective-permute-start.14) | collective-permute-done | bytes 196640 | tf_op jit(solution)/shard_map/ppermute | solution.py:235
  145.6 4.4 %grad_in.1 = (bf16[768,512]{1,0:T(8,128)(2,1)}, bf16[768,1024]{1,0:T(8,128)(2,1)}) custom-call(bf16[8,336,128]{2,1,0:T(8,128)(2,1)} %all-to-all-done.5.h, bf16[1024,512]{1,0:T(8,128)(2,1)S(1)} %copy-done.3), custom_call_target="tpu_custom_call" | custom-call | tf_op jit(solution)/shard_map/grad_in/pallas_call | solution.py:391
  150.0 5.9 %all-to-all-start.6 = ((bf16[4,192,1024]{2,1,0:T(8,128)(2,1)}), bf16[4,192,1024]{2,1,0:T(8,128)(2,1)}, u32[]{:S(2)}, u32[]{:S(2)}) async-start(bf16[4,192,1024]{2,1,0:T(8,128)(2,1)} %bitcast.29), calls=%async_computation.6 | async-start | bytes 3145728 | tf_op jit(solution)/shard_map/all_to_all | solution.py:400
  164.0 3.1 %collective-permute-start.19 = (bf16[24,1024]{1,0:T(8,128)(2,1)}, bf16[24,1024]{1,0:T(8,128)(2,1)S(1)}, u32[]{:S(2)}, u32[]{:S(2)}) collective-permute-start(bf16[24,1024]{1,0:T(8,128)(2,1)} %get-tuple-element.44), channel_id=1, source_target_pairs={{0,32},{8,40},{16,48},{24,56},{32,0},{40,8},{48,16},{56,24},{1,33}... | collective-permute-start | bytes 147464 | tf_op jit(solution)/shard_map/ppermute | solution.py:235
  177.9 4.7 %all-to-all-start.7 = ((bf16[8,24,1024]{2,1,0:T(8,128)(2,1)}), bf16[8,24,1024]{2,1,0:T(8,128)(2,1)}, u32[]{:S(2)}, u32[]{:S(2)}) async-start(bf16[8,24,1024]{2,1,0:T(8,128)(2,1)} %bitcast.30), calls=%async_computation.7 | async-start | bytes 786432 | tf_op jit(solution)/shard_map/all_to_all | solution.py:403
  182.6 4.1 %collective-permute-start.21 = (bf16[24,1024]{1,0:T(8,128)(2,1)}, bf16[24,1024]{1,0:T(8,128)(2,1)S(1)}, u32[]{:S(2)}, u32[]{:S(2)}) collective-permute-start(bf16[24,1024]{1,0:T(8,128)(2,1)} %get-tuple-element.46), channel_id=1, source_target_pairs={{0,48},{8,56},{16,0},{24,8},{32,16},{40,24},{48,32},{56,40},{1,49}... | collective-permute-start | bytes 147464 | tf_op jit(solution)/shard_map/ppermute | solution.py:235
  190.0 3.8 %grad_down.1 = f32[896,1024]{1,0:T(8,128)} custom-call(s32[7]{0:T(128)S(1)} %copy-done.26, s32[14,16]{1,0:T(8,128)S(1)} %dynamic_slice.24.md, bf16[768,512]{1,0:T(8,128)(2,1)S(1)} %copy-done.6, bf16[768,1024]{1,0:T(8,128)(2,1)S(1)} %bitcast.25), custom_call_target="tpu_custom_call" | custom-call | tf_op jit(solution)/shard_map/grad_down/pallas_call | solution.py:405
  195.7 6.6 %grad_up.1 = f32[1024,896]{1,0:T(8,128)} custom-call(s32[14]{0:T(128)S(1)} %fusion.6.su, s32[16,14]{1,0:T(8,128)S(1)} %copy.47.mu, bf16[768,512]{1,0:T(8,128)(2,1)S(1)} %copy-done.7, bf16[768,1024]{1,0:T(8,128)(2,1)S(1)} %bitcast.23), custom_call_target="tpu_custom_call" | custom-call | tf_op jit(solution)/shard_map/grad_up/pallas_call | solution.py:414
  (157 shorter events, 88.5 us)
Async XLA Ops:
  2.2 23.2 %all-to-all-start = ((bf16[8,24,1024]{2,1,0:T(8,128)(2,1)}), bf16[8,24,1024]{2,1,0:T(8,128)(2,1)S(1)}, u32[]{:S(2)}, u32[]{:S(2)}) async-start(bf16[8,24,1024]{2,1,0:T(8,128)(2,1)} %broadcast_in_dim.33), calls=%async_computation | async-start | bytes 786432 | tf_op jit(solution)/shard_map/all_to_all | solution.py:226
  26.7 23.4 %all-to-all-start.1 = ((bf16[4,8,24,1024]{3,2,1,0:T(8,128)(2,1)}), bf16[4,8,24,1024]{3,2,1,0:T(8,128)(2,1)S(1)}, u32[]{:S(2)}, u32[]{:S(2)}) async-start(bf16[4,8,24,1024]{3,2,1,0:T(8,128)(2,1)} %broadcast_in_dim.34), calls=%async_computation.1 | async-start | bytes 3145728 | tf_op jit(solution)/shard_map/all_to_all | solution.py:274
  35.4 7.0 %collective-permute-start.4 = (bf16[4,24,1024]{2,1,0:T(8,128)(2,1)S(1)}, bf16[4,24,1024]{2,1,0:T(8,128)(2,1)S(1)}, u32[]{:S(2)}, u32[]{:S(2)}) collective-permute-start(bf16[4,24,1024]{2,1,0:T(8,128)(2,1)S(1)} %pad_maximum_fusion.own), channel_id=1, source_target_pairs={{0,8},{8,16},{16,24},{24,32},{32,40},{40,48},{48,56},{56,0},{1,9},... | collective-permute-start | bytes 589832 | tf_op jit(solution)/shard_map/ppermute | solution.py:235
  41.1 11.9 %collective-permute-start.7 = (bf16[4,24,1024]{2,1,0:T(8,128)(2,1)S(1)}, bf16[4,24,1024]{2,1,0:T(8,128)(2,1)S(1)}, u32[]{:S(2)}, u32[]{:S(2)}) collective-permute-start(bf16[4,24,1024]{2,1,0:T(8,128)(2,1)S(1)} %collective-permute-done.5.refs_1_), channel_id=1, source_target_pairs={{0,56},{8,0},{16,8},{24,16},{32,24},{40,32},{48,40},{56,48},{1,57}... | collective-permute-start | bytes 589832 | tf_op jit(solution)/shard_map/ppermute | solution.py:235
  42.4 10.6 %collective-permute-start.6 = (bf16[4,24,1024]{2,1,0:T(8,128)(2,1)S(1)}, bf16[4,24,1024]{2,1,0:T(8,128)(2,1)}, u32[]{:S(2)}, u32[]{:S(2)}) collective-permute-start(bf16[4,24,1024]{2,1,0:T(8,128)(2,1)S(1)} %collective-permute-done.4.refs_0_), channel_id=1, source_target_pairs={{0,8},{8,16},{16,24},{24,32},{32,40},{40,48},{48,56},{56,0},{1,9},... | collective-permute-start | bytes 589832 | tf_op jit(solution)/shard_map/ppermute | solution.py:235
  53.6 23.8 %all-to-all-start.2 = ((f32[8,336,128]{2,1,0:T(8,128)}), f32[8,336,128]{2,1,0:T(8,128)S(1)}, u32[]{:S(2)}, u32[]{:S(2)}) async-start(f32[8,336,128]{2,1,0:T(8,128)} %pre.1), calls=%async_computation.2 | async-start | bytes 2752512 | tf_op jit(solution)/shard_map/all_to_all | solution.py:341
  57.9 7.5 %collective-permute-start.9 = (bf16[4,24,1024]{2,1,0:T(8,128)(2,1)}, bf16[4,24,1024]{2,1,0:T(8,128)(2,1)S(1)}, u32[]{:S(2)}, u32[]{:S(2)}) collective-permute-start(bf16[4,24,1024]{2,1,0:T(8,128)(2,1)} %copy-done.19), channel_id=1, source_target_pairs={{0,56},{8,0},{16,8},{24,16},{32,24},{40,32},{48,40},{56,48},{1,57}... | collective-permute-start | bytes 589832 | tf_op jit(solution)/shard_map/ppermute | solution.py:235
  59.3 9.4 %collective-permute-start.8 = (bf16[4,24,1024]{2,1,0:T(8,128)(2,1)}, bf16[4,24,1024]{2,1,0:T(8,128)(2,1)S(1)}, u32[]{:S(2)}, u32[]{:S(2)}) collective-permute-start(bf16[4,24,1024]{2,1,0:T(8,128)(2,1)} %collective-permute-done.6.refs_2_), channel_id=1, source_target_pairs={{0,8},{8,16},{16,24},{24,32},{32,40},{40,48},{48,56},{56,0},{1,9},... | collective-permute-start | bytes 589832 | tf_op jit(solution)/shard_map/ppermute | solution.py:235
  83.1 16.3 %all-to-all-start.3 = ((bf16[8,336,128]{2,1,0:T(8,128)(2,1)}), bf16[8,336,128]{2,1,0:T(8,128)(2,1)}, u32[]{:S(2)}, u32[]{:S(2)}) async-start(bf16[8,336,128]{2,1,0:T(8,128)(2,1)} %get-tuple-element.34), calls=%async_computation.3 | async-start | bytes 1376256 | tf_op jit(solution)/shard_map/all_to_all | solution.py:352
  99.4 23.8 %all-to-all-start.4 = ((f32[8,336,128]{2,1,0:T(8,128)}), f32[8,336,128]{2,1,0:T(8,128)}, u32[]{:S(2)}, u32[]{:S(2)}) async-start(f32[8,336,128]{2,1,0:T(8,128)} %grad_act.1), calls=%async_computation.4 | async-start | bytes 2752512 | tf_op jit(solution)/shard_map/all_to_all | solution.py:353
  108.3 19.8 %collective-permute-start.12 = (bf16[192,1536]{1,0:T(8,128)(2,1)}, bf16[192,1536]{1,0:T(8,128)(2,1)}, u32[]{:S(2)}, u32[]{:S(2)}) collective-permute-start(bf16[192,1536]{1,0:T(8,128)(2,1)} %get-tuple-element.38), channel_id=1, source_target_pairs={{0,64},{64,128},{128,192},{192,0},{1,65},{65,129},{129,193},{193,1... | collective-permute-start | bytes 1769480 | tf_op jit(solution)/shard_map/ppermute | solution.py:235
  108.6 19.5 %collective-permute-start.13 = (bf16[192,1536]{1,0:T(8,128)(2,1)}, bf16[192,1536]{1,0:T(8,128)(2,1)}, u32[]{:S(2)}, u32[]{:S(2)}) collective-permute-start(bf16[192,1536]{1,0:T(8,128)(2,1)} %get-tuple-element.39), channel_id=1, source_target_pairs={{0,192},{64,0},{128,64},{192,128},{1,193},{65,1},{129,65},{193,129... | collective-permute-start | bytes 1769480 | tf_op jit(solution)/shard_map/ppermute | solution.py:235
  128.1 16.3 %all-to-all-start.5 = ((bf16[8,336,128]{2,1,0:T(8,128)(2,1)}), bf16[8,336,128]{2,1,0:T(8,128)(2,1)}, u32[]{:S(2)}, u32[]{:S(2)}) async-start(bf16[8,336,128]{2,1,0:T(8,128)(2,1)} %grad_pre.1), calls=%async_computation.5 | async-start | bytes 1376256 | tf_op jit(solution)/shard_map/all_to_all | solution.py:375
  133.2 7.3 %collective-permute-start.14 = (bf16[192,512]{1,0:T(8,128)(2,1)S(1)}, bf16[192,512]{1,0:T(8,128)(2,1)S(1)}, u32[]{:S(2)}, u32[]{:S(2)}) collective-permute-start(bf16[192,512]{1,0:T(8,128)(2,1)S(1)} %slice.28), channel_id=1, source_target_pairs={{0,64},{64,128},{128,192},{192,0},{1,65},{65,129},{129,193},{193,1... | collective-permute-start | bytes 589832 | tf_op jit(solution)/shard_map/ppermute | solution.py:235
  134.6 7.0 %collective-permute-start.15 = (bf16[192,512]{1,0:T(8,128)(2,1)S(1)}, bf16[192,512]{1,0:T(8,128)(2,1)S(1)}, u32[]{:S(2)}, u32[]{:S(2)}) collective-permute-start(bf16[192,512]{1,0:T(8,128)(2,1)S(1)} %slice.29), channel_id=1, source_target_pairs={{0,192},{64,0},{128,64},{192,128},{1,193},{65,1},{129,65},{193,129... | collective-permute-start | bytes 589832 | tf_op jit(solution)/shard_map/ppermute | solution.py:235
  150.0 25.3 %all-to-all-start.6 = ((bf16[4,192,1024]{2,1,0:T(8,128)(2,1)}), bf16[4,192,1024]{2,1,0:T(8,128)(2,1)}, u32[]{:S(2)}, u32[]{:S(2)}) async-start(bf16[4,192,1024]{2,1,0:T(8,128)(2,1)} %bitcast.29), calls=%async_computation.6 | async-start | bytes 3145728 | tf_op jit(solution)/shard_map/all_to_all | solution.py:400
  160.5 9.3 %collective-permute-start.16 = (bf16[24,1024]{1,0:T(8,128)(2,1)}, bf16[24,1024]{1,0:T(8,128)(2,1)S(1)}, u32[]{:S(2)}, u32[]{:S(2)}) collective-permute-start(bf16[24,1024]{1,0:T(8,128)(2,1)} %get-tuple-element.41), channel_id=1, source_target_pairs={{0,8},{8,16},{16,24},{24,32},{32,40},{40,48},{48,56},{56,0},{1,9},... | collective-permute-start | bytes 147464 | tf_op jit(solution)/shard_map/ppermute | solution.py:235
  160.6 9.2 %collective-permute-start.17 = (bf16[24,1024]{1,0:T(8,128)(2,1)}, bf16[24,1024]{1,0:T(8,128)(2,1)S(1)}, u32[]{:S(2)}, u32[]{:S(2)}) collective-permute-start(bf16[24,1024]{1,0:T(8,128)(2,1)} %get-tuple-element.42), channel_id=1, source_target_pairs={{0,16},{8,24},{16,32},{24,40},{32,48},{40,56},{48,0},{56,8},{1,17}... | collective-permute-start | bytes 147464 | tf_op jit(solution)/shard_map/ppermute | solution.py:235
  162.0 8.9 %collective-permute-start.18 = (bf16[24,1024]{1,0:T(8,128)(2,1)}, bf16[24,1024]{1,0:T(8,128)(2,1)S(1)}, u32[]{:S(2)}, u32[]{:S(2)}) collective-permute-start(bf16[24,1024]{1,0:T(8,128)(2,1)} %get-tuple-element.43), channel_id=1, source_target_pairs={{0,24},{8,32},{16,40},{24,48},{32,56},{40,0},{48,8},{56,16},{1,25}... | collective-permute-start | bytes 147464 | tf_op jit(solution)/shard_map/ppermute | solution.py:235
  164.0 8.8 %collective-permute-start.19 = (bf16[24,1024]{1,0:T(8,128)(2,1)}, bf16[24,1024]{1,0:T(8,128)(2,1)S(1)}, u32[]{:S(2)}, u32[]{:S(2)}) collective-permute-start(bf16[24,1024]{1,0:T(8,128)(2,1)} %get-tuple-element.44), channel_id=1, source_target_pairs={{0,32},{8,40},{16,48},{24,56},{32,0},{40,8},{48,16},{56,24},{1,33}... | collective-permute-start | bytes 147464 | tf_op jit(solution)/shard_map/ppermute | solution.py:235
  167.1 6.7 %collective-permute-start.20 = (bf16[24,1024]{1,0:T(8,128)(2,1)}, bf16[24,1024]{1,0:T(8,128)(2,1)S(1)}, u32[]{:S(2)}, u32[]{:S(2)}) collective-permute-start(bf16[24,1024]{1,0:T(8,128)(2,1)} %get-tuple-element.45), channel_id=1, source_target_pairs={{0,40},{8,48},{16,56},{24,0},{32,8},{40,16},{48,24},{56,32},{1,41}... | collective-permute-start | bytes 147464 | tf_op jit(solution)/shard_map/ppermute | solution.py:235
  177.9 24.4 %all-to-all-start.7 = ((bf16[8,24,1024]{2,1,0:T(8,128)(2,1)}), bf16[8,24,1024]{2,1,0:T(8,128)(2,1)}, u32[]{:S(2)}, u32[]{:S(2)}) async-start(bf16[8,24,1024]{2,1,0:T(8,128)(2,1)} %bitcast.30), calls=%async_computation.7 | async-start | bytes 786432 | tf_op jit(solution)/shard_map/all_to_all | solution.py:403
  182.6 11.8 %collective-permute-start.21 = (bf16[24,1024]{1,0:T(8,128)(2,1)}, bf16[24,1024]{1,0:T(8,128)(2,1)S(1)}, u32[]{:S(2)}, u32[]{:S(2)}) collective-permute-start(bf16[24,1024]{1,0:T(8,128)(2,1)} %get-tuple-element.46), channel_id=1, source_target_pairs={{0,48},{8,56},{16,0},{24,8},{32,16},{40,24},{48,32},{56,40},{1,49}... | collective-permute-start | bytes 147464 | tf_op jit(solution)/shard_map/ppermute | solution.py:235
  186.7 8.2 %collective-permute-start.22 = (bf16[24,1024]{1,0:T(8,128)(2,1)}, bf16[24,1024]{1,0:T(8,128)(2,1)S(1)}, u32[]{:S(2)}, u32[]{:S(2)}) collective-permute-start(bf16[24,1024]{1,0:T(8,128)(2,1)} %get-tuple-element.47), channel_id=1, source_target_pairs={{0,56},{8,0},{16,8},{24,16},{32,24},{40,32},{48,40},{56,48},{1,57}... | collective-permute-start | bytes 147464 | tf_op jit(solution)/shard_map/ppermute | solution.py:235
  (41 other events, 222.5 us)
